TPU v7x, 32 devices: a whole 2x2x4 slice. The times are simulated.
32 devices in a mesh: expert: 4 (over y, x), fsdp: 8 (over z, core).
Axes of the slice: x: 2, y: 2, z: 4, core: 2. Of those that a mesh axis runs over, the one named last changes fastest.
Arguments:
- tokens: bfloat16 [512, 3072], P('expert'), may hold values from -6 to 6
- assignment: int32 [512, 2], P('expert'), may hold values from 0 to 3, all different within a row; in each aligned block of 128 rows (0 to 127, 128 to 255, ...) at most 96 rows name the same one
- route_weight: float32 [512, 2], P('expert'), may hold values from 0.25 to 1
- cotangent: bfloat16 [512, 3072], P('expert'), may hold values from -6 to 6
- w_gate: bfloat16 [4, 3072, 8192], P('expert', None, 'fsdp'), may hold values from -0.109375 to 0.109375
- w_up: bfloat16 [4, 3072, 8192], P('expert', None, 'fsdp'), may hold values from -0.109375 to 0.109375
- w_down: bfloat16 [4, 8192, 3072], P('expert', 'fsdp'), may hold values from -0.0625 to 0.0625
Outputs:
- moe_out: bfloat16 [512, 3072], P('expert')
- grad_tokens: bfloat16 [512, 3072], P('expert')
- grad_prob: float32 [512, 2], P('expert')
- grad_gate: bfloat16 [4, 3072, 8192], P('expert', None, 'fsdp')
- grad_up: bfloat16 [4, 3072, 8192], P('expert', None, 'fsdp')
- grad_down: bfloat16 [4, 8192, 3072], P('expert', 'fsdp')
Inputs may be any that keep to these rules, and one draw needn't show every extreme that they name: `assignment`: each token names two different experts. Among the 128 tokens of one block no expert is named more than 96 times, and in some block some expert is named exactly 96 times.
All inputs are finite; a program needn't handle non-finite values.
Results may differ from a plain program's by a relative error of at most 0.02.
Values may be sent and summed in bfloat16 or wider, within the bound.
No kernel may reach another device: no remote copies, remote signals or barrier semaphores. Data moves between devices by JAX's collectives and lax.ppermute only.
A program may use at most 128 MiB of HBM per device.

v0:
```python
import jax
import jax.numpy as jnp
from jax import lax
from jax.sharding import PartitionSpec as P


def slot_table(assignment, groups, capacity):
    flat = assignment.reshape(-1)
    onehot = (flat[:, None] == jnp.arange(groups, dtype=jnp.int32)[None, :]).astype(jnp.int32)
    before = jnp.cumsum(onehot, axis=0) - onehot
    position = jnp.sum(before * onehot, axis=1)
    return (flat * capacity + position).reshape(assignment.shape)


def front_half(gathered, gate_local, up_local):
    pre_gate = jnp.dot(gathered, gate_local, preferred_element_type=jnp.float32)
    pre_up = jnp.dot(gathered, up_local, preferred_element_type=jnp.float32)
    sigma = jax.nn.sigmoid(pre_gate)
    silu_gate = pre_gate * sigma
    hidden = (silu_gate * pre_up).astype(jnp.bfloat16)
    return (pre_gate, pre_up, sigma, silu_gate, hidden)


def spread(buffer, groups, capacity):
    width = buffer.shape[-1]
    blocks = buffer.reshape(groups, capacity, width)
    arrived = lax.all_to_all(blocks, "expert", split_axis=0, concat_axis=0, tiled=True)
    return arrived.reshape(-1, width)


def return_rows(term_fn, groups, capacity, width):
    full_term = term_fn(0, groups * capacity)
    columns = lax.psum_scatter(
        full_term.astype(jnp.bfloat16), "fsdp", scatter_dimension=1, tiled=True
    )
    part = columns.shape[1]
    moved = lax.all_to_all(
        columns.reshape(groups, capacity, part), "expert", split_axis=0, concat_axis=0, tiled=True
    )
    back = lax.all_gather(moved, "fsdp", axis=2, tiled=True)
    return back.reshape(-1, width)


def per_device(tokens, assignment, route_weight, cotangent, w_gate, w_up, w_down):
    tok_dev = tokens.shape[0]
    width = tokens.shape[1]
    groups = lax.axis_size("expert")
    capacity = max(2, 3 * tok_dev // groups)
    slot_count = groups * capacity
    table = slot_table(assignment, groups, capacity)
    slot_ids = jnp.arange(slot_count, dtype=jnp.int32)
    pick_first = slot_ids[:, None] == table[:, 0][None, :]
    pick_second = slot_ids[:, None] == table[:, 1][None, :]
    pick_both = jnp.logical_or(pick_first, pick_second).astype(jnp.bfloat16)
    sent_tokens = jnp.dot(pick_both, tokens, preferred_element_type=jnp.float32).astype(
        jnp.bfloat16
    )
    weighted = (route_weight[:, :, None] * cotangent[:, None, :].astype(jnp.float32)).astype(
        jnp.bfloat16
    )
    sent_cot = (
        jnp.dot(pick_first.astype(jnp.bfloat16), weighted[:, 0], preferred_element_type=jnp.float32)
        + jnp.dot(
            pick_second.astype(jnp.bfloat16), weighted[:, 1], preferred_element_type=jnp.float32
        )
    ).astype(jnp.bfloat16)
    gate_local = w_gate[0]
    up_local = w_up[0]
    down_local = w_down[0]
    gathered = spread(sent_tokens, groups, capacity)
    pre_gate, pre_up, sigma, silu_gate, hidden = front_half(gathered, gate_local, up_local)

    def out_term(start, count):
        return jnp.dot(hidden, down_local, preferred_element_type=jnp.float32)

    out_back = return_rows(out_term, groups, capacity, width).astype(jnp.float32)
    select_first = pick_first.astype(jnp.float32)
    select_second = pick_second.astype(jnp.float32)
    first_out = jnp.dot(select_first.T, out_back, precision=lax.Precision.HIGHEST)
    second_out = jnp.dot(select_second.T, out_back, precision=lax.Precision.HIGHEST)
    moe_out = (route_weight[:, 0:1] * first_out + route_weight[:, 1:2] * second_out).astype(
        jnp.bfloat16
    )
    cot_float = cotangent.astype(jnp.float32)
    grad_prob = jnp.stack(
        [jnp.sum(cot_float * first_out, axis=1), jnp.sum(cot_float * second_out, axis=1)], axis=1
    )
    grad_gathered = spread(sent_cot, groups, capacity)
    grad_hidden = jnp.dot(grad_gathered, down_local.T, preferred_element_type=jnp.float32)
    grad_down = jnp.dot(hidden.T, grad_gathered, preferred_element_type=jnp.float32).astype(
        jnp.bfloat16
    )
    grad_pre_gate = (grad_hidden * pre_up * sigma * (1.0 + pre_gate * (1.0 - sigma))).astype(
        jnp.bfloat16
    )
    grad_pre_up = (grad_hidden * silu_gate).astype(jnp.bfloat16)
    grad_gate = jnp.dot(gathered.T, grad_pre_gate, preferred_element_type=jnp.float32).astype(
        jnp.bfloat16
    )
    grad_up = jnp.dot(gathered.T, grad_pre_up, preferred_element_type=jnp.float32).astype(
        jnp.bfloat16
    )

    def back_term(start, count):
        return jnp.dot(grad_pre_gate, gate_local.T, preferred_element_type=jnp.float32) + jnp.dot(
            grad_pre_up, up_local.T, preferred_element_type=jnp.float32
        )

    grad_back = return_rows(back_term, groups, capacity, width).astype(jnp.float32)
    grad_tokens = (
        jnp.dot(select_first.T, grad_back, precision=lax.Precision.HIGHEST)
        + jnp.dot(select_second.T, grad_back, precision=lax.Precision.HIGHEST)
    ).astype(jnp.bfloat16)
    return (moe_out, grad_tokens, grad_prob, grad_gate[None], grad_up[None], grad_down[None])


def solution(mesh):
    return jax.shard_map(
        per_device,
        mesh=mesh,
        in_specs=(
            P("expert", None),
            P("expert", None),
            P("expert", None),
            P("expert", None),
            P("expert", None, "fsdp"),
            P("expert", None, "fsdp"),
            P("expert", "fsdp", None),
        ),
        out_specs=(
            P("expert", None),
            P("expert", None),
            P("expert", None),
            P("expert", None, "fsdp"),
            P("expert", None, "fsdp"),
            P("expert", "fsdp", None),
        ),
        check_vma=False,
    )
```

profile of v0, /device:TPU:0, one launch (start us, length us, event | category | flops | bytes accessed | tf_op | source)
XLA Modules:
  0.0 253.0 jit_solution(2533631216367700508)
XLA Ops:
  7.2 0.0 copy-start
  7.2 0.9 copy.34
  8.0 0.1 eq.60
  8.2 0.1 eq.56
  8.3 1.2 reduce-window.6
  9.6 0.1 slice.32
  9.6 0.1 copy.36
  9.8 0.1 copy.37
  9.9 0.1 add_bitcast_fusion
  10.0 0.1 reduce_sum.30
  10.1 0.1 copy.38
  10.2 0.7 multiply_add_fusion
  10.9 0.0 copy-done
  10.9 2.2 convolution_convert_fusion
  13.1 5.3 %all-to-all-start = ((bf16[4,96,3072]{2,1,0:T(8,128)(2,1)}), bf16[4,96,3072]{2,1,0:T(8,128)(2,1)S(1)}, u32[]{:S(2)}, u32[]{:S(2)}) async-start(bf16[4,96,3072]{2,1,0:T(8,128)(2,1)} %bitcast.5), calls=%async_computation | async-start | bytes 4718592 | tf_op jit(solution)/shard_map/all_to_all | solution.py:27
  18.4 0.0 copy-done.4
  18.4 0.1 convert_element_type.64
  18.5 0.0 copy-done.5
  18.5 0.3 multiply_convert_fusion
  18.8 0.8 fusion.19
  19.6 2.2 add_convert_fusion.1
  21.8 24.2 %all-to-all-done = bf16[4,96,3072]{2,1,0:T(8,128)(2,1)S(1)} async-done(((bf16[4,96,3072]{2,1,0:T(8,128)(2,1)}), bf16[4,96,3072]{2,1,0:T(8,128)(2,1)S(1)}, u32[]{:S(2)}, u32[]{:S(2)}) %all-to-all-start) | async-done | bytes 2359328 | tf_op jit(solution)/shard_map/all_to_all | solution.py:27
  46.1 4.5 %all-to-all-start.2 = ((bf16[4,96,3072]{2,1,0:T(8,128)(2,1)}), bf16[4,96,3072]{2,1,0:T(8,128)(2,1)}, u32[]{:S(2)}, u32[]{:S(2)}) async-start(bf16[4,96,3072]{2,1,0:T(8,128)(2,1)} %bitcast.15), calls=%async_computation.2 | async-start | bytes 4718592 | tf_op jit(solution)/shard_map/all_to_all | solution.py:27
  50.6 0.0 reduce-scatter.7.cloned.1.call-start
  50.6 6.5 %fusion.6 = f32[384,1024]{1,0:T(8,128)} fusion(bf16[384,3072]{1,0:T(8,128)(2,1)S(1)} %bitcast.97, bf16[1,3072,1024]{2,1,0:T(8,128)(2,1)} %param.12), kind=kOutput, calls=%fused_computation.6 | convolution fusion | flops 2415919104 | bytes 10223616 | tf_op jit(solution)/shard_map/dot_general | solution.py:17
  57.1 20.6 %all-to-all-done.2 = bf16[4,96,3072]{2,1,0:T(8,128)(2,1)} async-done(((bf16[4,96,3072]{2,1,0:T(8,128)(2,1)}), bf16[4,96,3072]{2,1,0:T(8,128)(2,1)}, u32[]{:S(2)}, u32[]{:S(2)}) %all-to-all-start.2) | async-done | bytes 2359328 | tf_op jit(solution)/shard_map/all_to_all | solution.py:27
  77.8 5.6 %fusion = f32[384,1024]{1,0:T(8,128)S(1)} fusion(bf16[384,3072]{1,0:T(8,128)(2,1)} %bitcast.16, bf16[1,1024,3072]{2,1,0:T(8,128)(2,1)} %param.13), kind=kOutput, calls=%fused_computation | convolution fusion | flops 2415919104 | bytes 10223616 | tf_op jit(solution)/shard_map/dot_general | solution.py:89
  83.4 0.0 copy-done.10
  83.4 0.0 slice-start.1
  83.4 7.3 %multiply_convert_fusion.2 = (bf16[384,1024]{1,0:T(8,128)(2,1)}, bf16[384,1024]{1,0:T(8,128)(2,1)}, bf16[384,1024]{1,0:T(8,128)(2,1)S(1)}) fusion(f32[384,1024]{1,0:T(8,128)S(1)} %fusion, f32[384,1024]{1,0:T(8,128)S(1)} %copy-done.10, bf16[384,3072]{1,0:T(8,128)(2,1)S(1)} %bitcast.98, bf16[1,3072,1024]{2,1,0:T(8,128)(2,1)} %param.11), kind=kOutput, calls=%fused_computation.25 | convolution fusion | flops 2421817344 | bytes 14155776 | tf_op jit(solution)/shard_map/dot_general | solution.py:16
  90.8 0.9 copy-done.6
  91.6 3.8 %fusion.14 = bf16[384,3072]{1,0:T(8,128)(2,1)} fusion(bf16[384,1024]{1,0:T(8,128)(2,1)S(1)} %get-tuple-element.11, bf16[1,1024,3072]{2,1,0:T(8,128)(2,1)S(1)} %bitcast.109), kind=kOutput, calls=%fused_computation.18 | convolution fusion | flops 2417098752 | bytes 9437184 | tf_op jit(solution)/shard_map/dot_general | solution.py:74
  95.5 4.3 %copy.39 = bf16[384,3072]{0,1:T(8,128)(2,1)} copy(bf16[384,3072]{1,0:T(8,128)(2,1)} %fusion.14) | data formatting | bytes 4718592
  99.7 0.0 reduce-scatter.7.cloned.1.call-update
  99.8 0.2 reduce-scatter.9.cloned.1.call-start
  100.0 0.0 copy-start.7
  100.0 5.0 %fusion.4 = f32[384,3072]{1,0:T(8,128)S(1)} fusion(bf16[384,1024]{1,0:T(8,128)(2,1)} %get-tuple-element.10, bf16[1,3072,1024]{2,1,0:T(8,128)(2,1)} %param.12), kind=kOutput, calls=%fused_computation.4 | convolution fusion | flops 2415919104 | bytes 11796480 | tf_op jit(solution)/shard_map/dot_general | solution.py:105
  105.1 0.0 copy-done.7
  105.1 8.5 %add_convert_fusion = bf16[384,3072]{1,0:T(8,128)(2,1)} fusion(f32[384,3072]{1,0:T(8,128)S(1)} %fusion.4, bf16[384,1024]{1,0:T(8,128)(2,1)S(1)} %copy-done.7, bf16[1,3072,1024]{2,1,0:T(8,128)(2,1)} %param.11), kind=kOutput, calls=%fused_computation.15 | convolution fusion | flops 2418278400 | bytes 14155776 | tf_op jit(solution)/shard_map/dot_general | solution.py:105
  113.6 4.3 %copy.41 = bf16[384,3072]{0,1:T(8,128)(2,1)} copy(bf16[384,3072]{1,0:T(8,128)(2,1)} %add_convert_fusion) | data formatting | bytes 4718592
  117.8 0.0 reduce-scatter.9.cloned.1.call-update
  117.9 0.0 all-gather.3.cloned.1.call-start
  117.9 18.8 %reduce-scatter.7.cloned.1.call-done = bf16[384,384]{1,0:T(8,128)(2,1)} async-done(((bf16[3072,384]{1,0:T(8,128)(2,1)}), bf16[384,384]{1,0:T(8,128)(2,1)}) %reduce-scatter.7.cloned.1.call-update) | async-done | bytes 294928
  136.7 1.2 copy.40
  137.8 9.8 %all_to_all.20 = bf16[4,96,384]{2,1,0:T(8,128)(2,1)} all-to-all(bf16[4,96,384]{2,1,0:T(8,128)(2,1)S(1)} %bitcast.101), channel_id=1, replica_groups=mesh['expert'=4,'fsdp'=8] {'expert'}, dimensions={0} | all-to-all | bytes 589824 | tf_op jit(solution)/shard_map/all_to_all | solution.py:37
  147.6 0.0 all-gather.3.cloned.1.call-update
  147.7 0.0 all-gather.5.cloned.1.call-start
  147.7 27.3 %reduce-scatter.9.cloned.1.call-done = bf16[384,384]{1,0:T(8,128)(2,1)} async-done(((bf16[3072,384]{1,0:T(8,128)(2,1)}), bf16[384,384]{1,0:T(8,128)(2,1)}) %reduce-scatter.9.cloned.1.call-update) | async-done | bytes 294928
  175.0 1.2 copy.42
  176.2 10.0 %all_to_all.21 = bf16[4,96,384]{2,1,0:T(8,128)(2,1)} all-to-all(bf16[4,96,384]{2,1,0:T(8,128)(2,1)S(1)} %bitcast.102), channel_id=1, replica_groups=mesh['expert'=4,'fsdp'=8] {'expert'}, dimensions={0} | all-to-all | bytes 589824 | tf_op jit(solution)/shard_map/all_to_all | solution.py:37
  186.2 0.0 all-gather.5.cloned.1.call-update
  186.3 0.0 copy-start.8
  186.3 8.2 %convert_bitcast_fusion = bf16[1,1024,3072]{2,1,0:T(8,128)(2,1)} fusion(bf16[384,1024]{1,0:T(8,128)(2,1)} %copy-done.6, bf16[384,3072]{1,0:T(8,128)(2,1)} %bitcast.16), kind=kOutput, calls=%fused_computation.12 | convolution fusion | flops 2419064832 | bytes 9437184 | tf_op jit(solution)/shard_map/dot_general | solution.py:90
  194.4 5.4 %convert_bitcast_fusion.2 = bf16[1,3072,1024]{2,1,0:T(8,128)(2,1)} fusion(bf16[384,3072]{1,0:T(8,128)(2,1)S(1)} %bitcast.99, bf16[384,1024]{1,0:T(8,128)(2,1)S(1)} %copy-done.8), kind=kOutput, calls=%fused_computation.14 | convolution fusion | flops 2419064832 | bytes 9437184 | tf_op jit(solution)/shard_map/dot_general | solution.py:97
  199.8 0.0 copy-done.9
  199.8 5.4 %convert_bitcast_fusion.1 = bf16[1,3072,1024]{2,1,0:T(8,128)(2,1)} fusion(bf16[384,3072]{1,0:T(8,128)(2,1)S(1)} %bitcast.100, bf16[384,1024]{1,0:T(8,128)(2,1)S(1)} %copy-done.9), kind=kOutput, calls=%fused_computation.13 | convolution fusion | flops 2419064832 | bytes 9437184 | tf_op jit(solution)/shard_map/dot_general | solution.py:100
  205.2 2.4 all-gather.3.cloned.1.call-done
  207.5 2.3 fusion.20
  209.8 29.9 %all-gather.5.cloned.1.call-done = bf16[4,96,3072]{2,1,0:T(8,128)(2,1)} async-done(((bf16[4,96,384]{2,1,0:T(8,128)(2,1)}), bf16[4,96,3072]{2,1,0:T(8,128)(2,1)}) %all-gather.5.cloned.1.call-update) | async-done | bytes 2359312 | tf_op jit(solution)/shard_map/all_gather | solution.py:40
  239.8 2.4 fusion.22
  242.2 1.5 fusion.17
  243.7 0.3 copy-done.2
  244.0 1.9 multiply_reduce_fusion.1
  245.9 0.6 pad_maximum_fusion
  (21 shorter events, 0.1 us)
Async XLA Ops:
  7.2 3.7 %copy-start = (bf16[128,3072]{1,0:T(8,128)(2,1)S(1)}, bf16[128,3072]{1,0:T(8,128)(2,1)}, u32[]{:S(2)}) copy-start(bf16[128,3072]{1,0:T(8,128)(2,1)} %param.7) | copy-start | bytes 2359300
  13.1 5.3 %copy-start.4 = (bf16[128,3072]{1,0:T(8,128)(2,1)S(1)}, bf16[128,3072]{1,0:T(8,128)(2,1)}, u32[]{:S(2)}) copy-start(bf16[128,3072]{1,0:T(8,128)(2,1)} %param.10) | copy-start | bytes 2359300
  13.1 5.5 %copy-start.5 = (f32[128,2]{0,1:T(2,128)S(1)}, f32[128,2]{0,1:T(2,128)}, u32[]{:S(2)}) copy-start(f32[128,2]{0,1:T(2,128)} %param.9) | copy-start | bytes 3076
  13.1 33.0 %all-to-all-start = ((bf16[4,96,3072]{2,1,0:T(8,128)(2,1)}), bf16[4,96,3072]{2,1,0:T(8,128)(2,1)S(1)}, u32[]{:S(2)}, u32[]{:S(2)}) async-start(bf16[4,96,3072]{2,1,0:T(8,128)(2,1)} %bitcast.5), calls=%async_computation | async-start | bytes 4718592 | tf_op jit(solution)/shard_map/all_to_all | solution.py:27
  46.1 31.7 %all-to-all-start.2 = ((bf16[4,96,3072]{2,1,0:T(8,128)(2,1)}), bf16[4,96,3072]{2,1,0:T(8,128)(2,1)}, u32[]{:S(2)}, u32[]{:S(2)}) async-start(bf16[4,96,3072]{2,1,0:T(8,128)(2,1)} %bitcast.15), calls=%async_computation.2 | async-start | bytes 4718592 | tf_op jit(solution)/shard_map/all_to_all | solution.py:27
  50.6 86.1 %reduce-scatter.7.cloned.1.call-start = ((), (), s32[]{:S(2)}) async-start(), calls=%async_computation.8 | async-start | bytes 2654208
  77.8 5.6 %copy-start.10 = (f32[384,1024]{1,0:T(8,128)S(1)}, f32[384,1024]{1,0:T(8,128)}, u32[]{:S(2)}) copy-start(f32[384,1024]{1,0:T(8,128)} %fusion.6) | copy-start | bytes 4718596
  77.8 13.9 %slice-start = ((s8[6291456]{0:T(1024)(128)(4,1)}), s8[2097152]{0:T(1024)(128)(4,1)S(1)}, s32[]{:S(2)}) async-start(s8[6291456]{0:T(1024)(128)(4,1)} %bitcast.108), calls=%async_computation.10 | async-start | bytes 4194304
  83.4 8.2 %slice-start.1 = ((s8[6291456]{0:T(1024)(128)(4,1)}), s8[4194304]{0:T(1024)(128)(4,1)S(1)}, s32[]{:S(2)}) async-start(s8[6291456]{0:T(1024)(128)(4,1)} %bitcast.108), calls=%async_computation.11 | async-start | bytes 8388608
  90.8 0.9 copy-start.6
  99.8 75.3 %reduce-scatter.9.cloned.1.call-start = ((), (), s32[]{:S(2)}) async-start(), calls=%async_computation.9 | async-start | bytes 2654208
  100.0 5.1 %copy-start.7 = (bf16[384,1024]{1,0:T(8,128)(2,1)S(1)}, bf16[384,1024]{1,0:T(8,128)(2,1)}, u32[]{:S(2)}) copy-start(bf16[384,1024]{1,0:T(8,128)(2,1)} %get-tuple-element.9) | copy-start | bytes 2359300
  117.9 89.7 %all-gather.3.cloned.1.call-start = ((), (), s32[]{:S(2)}) async-start(), calls=%async_computation.6 | async-start | bytes 2654208 | tf_op jit(solution)/shard_map/all_gather | solution.py:40
  147.7 92.1 %all-gather.5.cloned.1.call-start = ((), (), s32[]{:S(2)}) async-start(), calls=%async_computation.7 | async-start | bytes 2654208 | tf_op jit(solution)/shard_map/all_gather | solution.py:40
  186.3 8.2 %copy-start.8 = (bf16[384,1024]{1,0:T(8,128)(2,1)S(1)}, bf16[384,1024]{1,0:T(8,128)(2,1)}, u32[]{:S(2)}) copy-start(bf16[384,1024]{1,0:T(8,128)(2,1)} %get-tuple-element.9) | copy-start | bytes 2359300
  194.4 5.4 %copy-start.9 = (bf16[384,1024]{1,0:T(8,128)(2,1)S(1)}, bf16[384,1024]{1,0:T(8,128)(2,1)}, u32[]{:S(2)}) copy-start(bf16[384,1024]{1,0:T(8,128)(2,1)} %get-tuple-element.10) | copy-start | bytes 2359300
  239.8 2.4 copy-start.3
  242.2 1.8 copy-start.2
  243.7 2.7 %copy-start.1 = (bf16[128,3072]{1,0:T(8,128)(2,1)S(1)}, bf16[128,3072]{1,0:T(8,128)(2,1)}, u32[]{:S(2)}) copy-start(bf16[128,3072]{1,0:T(8,128)(2,1)} %param.7) | copy-start | bytes 2359300
Sparse Core Ops, SparseCore 0:
  99.9 36.7 reduce-scatter.6
  139.6 35.4 reduce-scatter.8
  176.7 30.8 all-gather.2
  209.0 30.7 all-gather.4
where the time goes:
time: 254 us; the launch traced here: 253 us
  waiting for transfers between devices  123 us (48%)
  matrix products  69 us (27%)
  blocking collectives  19.8 us (8%)
  between operations  14 us (6%)
  local copies, waits for them, and re-layouts  13.7 us (5%)
  starting transfers between devices  10.1 us (4%)
  other arithmetic  3.09 us (1%)
    unnamed x6, waiting for transfers between devices  46.1 us
    all_to_all x2, waiting for transfers between devices, spread(): lax.all_to_all(blocks, 'expert', split_axis=0, concat_axis=0, tiled=True)  44.9 us
    all_gather x2, waiting for transfers between devices, return_rows(): back = lax.all_gather(moved, 'fsdp', axis=2, tiled=True)  32.3 us
    all_to_all x2, blocking collectives, return_rows(): lax.all_to_all(columns.reshape(groups, capacity, part), 'expert', split_a...  19.8 us
    unnamed x31, local copies, waits for them, and re-layouts  13 us
    all_to_all x2, starting transfers between devices, spread(): lax.all_to_all(blocks, 'expert', split_axis=0, concat_axis=0, tiled=True)  9.79 us
    dot_general x1, matrix products, back_term(): jnp.dot(grad_pre_gate, gate_local.T, preferred_element_type=jnp.float32)  8.49 us
    dot_general x1, matrix products, per_device(): jnp.dot(hidden.T, grad_gathered, preferred_element_type=jnp.float32)  8.16 us
  transfers between devices with their start and end apart: 6, of which 6 were waited for; matrix products, arithmetic and copies ran while one was open for 20% of the time, Pallas kernels for 0%

commit v1 on v0

v1 whole, which is shorter than its diff:
```python
import jax
import jax.numpy as jnp
from jax import lax
from jax.sharding import PartitionSpec as P

AXES = ("expert", "fsdp")


def log2(size):
    return size.bit_length() - 1


def swap(value, groups, shards, partner):
    pairs = []
    for e in range(groups):
        for f in range(shards):
            to_e, to_f = partner(e, f)
            pairs.append((e * shards + f, to_e * shards + to_f))
    return lax.ppermute(value, AXES, pairs)


class Links:
    def __init__(self):
        self.groups = lax.axis_size("expert")
        self.shards = lax.axis_size("fsdp")
        self.steps = log2(self.groups)
        self.expert = lax.axis_index("expert")
        fsdp = lax.axis_index("fsdp")
        self.core = fsdp % 2
        self.deep = (fsdp // 2) % 2

    def order(self, core):
        return [(k + core) % self.steps for k in range(self.steps)]

    def offsets(self, core):
        found = [0]
        for bit in self.order(core):
            found = found + [o ^ (1 << bit) for o in found]
        return found

    def to_core(self, value):
        return swap(value, self.groups, self.shards, lambda e, f: (e, f ^ 1))

    def to_expert(self, value, step):
        orders = [self.order(0), self.order(1)]
        return swap(
            value, self.groups, self.shards, lambda e, f: (e ^ (1 << orders[f % 2][step]), f)
        )

    def to_offset(self, value, offset):
        return swap(value, self.groups, self.shards, lambda e, f: (e ^ offset, f))

    def to_shard(self, value, bit):
        return swap(value, self.groups, self.shards, lambda e, f: (e, f ^ (1 << bit)))


def add(left, right):
    return (left.astype(jnp.float32) + right.astype(jnp.float32)).astype(jnp.bfloat16)


def gather_rows(links, rows):
    half = rows.shape[0] // 2
    own = lax.dynamic_slice_in_dim(rows, links.core * half, half, 0)
    rest = lax.dynamic_slice_in_dim(rows, (1 - links.core) * half, half, 0)
    held = own
    for step in range(links.steps):
        held = jnp.concatenate([held, links.to_expert(held, step)], axis=0)
    other = links.to_core(held[half:])
    return jnp.concatenate([held, rest, other], axis=0)


def order_rows(links, per_offset):
    half = per_offset.shape[1] // 2
    low = jnp.concatenate([per_offset[o, :half] for o in links.offsets(0)])
    high = jnp.concatenate([per_offset[o, half:] for o in links.offsets(1)])
    return jnp.where(
        links.core == 0, jnp.concatenate([low, high]), jnp.concatenate([high, low])
    )


def sum_rows(links, terms):
    middle = terms.shape[0] // 2
    held = add(terms[:middle], links.to_core(terms[middle:]))
    for step in reversed(range(links.steps)):
        count = held.shape[0] // 2
        held = add(held[:count], links.to_expert(held[count:], step))
    quarter = held.shape[0] // 2
    mine = lax.dynamic_slice_in_dim(held, links.deep * quarter, quarter, 0)
    theirs = lax.dynamic_slice_in_dim(held, (1 - links.deep) * quarter, quarter, 0)
    mine = add(mine, links.to_shard(theirs, 1))
    for bit in range(2, log2(links.shards)):
        mine = add(mine, links.to_shard(mine, bit))
    theirs = links.to_shard(mine, 1)
    part = jnp.where(
        links.deep == 0,
        jnp.concatenate([mine, theirs], axis=0),
        jnp.concatenate([theirs, mine], axis=0),
    )
    other = links.to_core(part)
    return jnp.where(
        links.core == 0,
        jnp.concatenate([part, other], axis=0),
        jnp.concatenate([other, part], axis=0),
    )


def per_device(tokens, assignment, route_weight, cotangent, w_gate, w_up, w_down):
    links = Links()
    width = tokens.shape[1]
    groups = links.groups
    gate_local, up_local, down_local = w_gate[0], w_up[0], w_down[0]

    received = []
    for offset in range(groups):
        there = links.expert ^ offset
        column = jnp.sum(jnp.where(assignment == there, route_weight, 0.0), axis=1)
        received.append(column if offset == 0 else links.to_offset(column, offset))
    weight = order_rows(links, jnp.stack(received))[:, None]

    rows_x = gather_rows(links, tokens)
    rows_c = gather_rows(links, cotangent)

    pre_gate = jnp.dot(rows_x, gate_local, preferred_element_type=jnp.float32)
    pre_up = jnp.dot(rows_x, up_local, preferred_element_type=jnp.float32)
    sigma = jax.nn.sigmoid(pre_gate)
    silu_gate = pre_gate * sigma
    hidden = silu_gate * pre_up
    scaled = (weight * hidden).astype(jnp.bfloat16)
    out_terms = jnp.dot(scaled, down_local, preferred_element_type=jnp.float32).astype(
        jnp.bfloat16
    )
    moe_out = sum_rows(links, out_terms)

    raw_hidden = jnp.dot(rows_c, down_local.T, preferred_element_type=jnp.float32)
    prob_term = jnp.sum(hidden * raw_hidden, axis=1, keepdims=True)
    lane = lax.broadcasted_iota(jnp.int32, (1, 128), 1)
    prob_terms = jnp.where(lane == links.expert, prob_term, 0.0).astype(jnp.bfloat16)
    grad_hidden = raw_hidden * weight
    grad_pre_gate = (grad_hidden * pre_up * sigma * (1.0 + pre_gate * (1.0 - sigma))).astype(
        jnp.bfloat16
    )
    grad_pre_up = (grad_hidden * silu_gate).astype(jnp.bfloat16)
    back_terms = (
        jnp.dot(grad_pre_gate, gate_local.T, preferred_element_type=jnp.float32)
        + jnp.dot(grad_pre_up, up_local.T, preferred_element_type=jnp.float32)
    ).astype(jnp.bfloat16)
    back = sum_rows(links, jnp.concatenate([back_terms, prob_terms], axis=1))
    grad_tokens = back[:, :width]
    prob_all = back[:, width:].astype(jnp.float32)
    grad_prob = jnp.stack(
        [
            jnp.sum(jnp.where(lane == assignment[:, k : k + 1], prob_all, 0.0), axis=1)
            for k in range(assignment.shape[1])
        ],
        axis=1,
    )

    grad_down = jnp.dot(scaled.T, rows_c, preferred_element_type=jnp.float32).astype(jnp.bfloat16)
    grad_gate = jnp.dot(rows_x.T, grad_pre_gate, preferred_element_type=jnp.float32).astype(
        jnp.bfloat16
    )
    grad_up = jnp.dot(rows_x.T, grad_pre_up, preferred_element_type=jnp.float32).astype(
        jnp.bfloat16
    )
    return (moe_out, grad_tokens, grad_prob, grad_gate[None], grad_up[None], grad_down[None])


def solution(mesh):
    return jax.shard_map(
        per_device,
        mesh=mesh,
        in_specs=(
            P("expert", None),
            P("expert", None),
            P("expert", None),
            P("expert", None),
            P("expert", None, "fsdp"),
            P("expert", None, "fsdp"),
            P("expert", "fsdp", None),
        ),
        out_specs=(
            P("expert", None),
            P("expert", None),
            P("expert", None),
            P("expert", None, "fsdp"),
            P("expert", None, "fsdp"),
            P("expert", "fsdp", None),
        ),
        check_vma=False,
    )
```

time: 254 us -> 150 us (0.59)
  waiting for transfers between devices: 123 us -> 63 us
  matrix products: 69 us -> 48.5 us
  blocking collectives: 19.8 us -> 0 us
  between operations: 14 us -> 1.06 us
  starting transfers between devices: 10.1 us -> 22.4 us
  local copies, waits for them, and re-layouts: 13.7 us -> 9.29 us
    ppermute x0 -> x23, waiting for transfers between devices: none -> 63 us  [swap(): return lax.ppermute(value, AXES, pairs)]
    unnamed x6 -> x0, waiting for transfers between devices: 46.1 us -> none
    all_to_all x2 -> x0, waiting for transfers between devices: 44.9 us -> none  [spread(): lax.all_to_all(blocks, 'expert', split_axis=0, concat_axis=0, tiled=True)]
    all_gather x2 -> x0, waiting for transfers between devices: 32.3 us -> none  [return_rows(): back = lax.all_gather(moved, 'fsdp', axis=2, tiled=True)]
    ppermute x0 -> x23, starting transfers between devices: none -> 22.4 us  [swap(): return lax.ppermute(value, AXES, pairs)]
    dot_general x16 -> x9, matrix products: 69 us -> 48.5 us  [the longest x1 7.51 us: per_device(): pre_gate = jnp.dot(rows_x, gate_local, preferred_element_type=jnp.float32)]
    all_to_all x2 -> x0, blocking collectives: 19.8 us -> none  [return_rows(): lax.all_to_all(columns.reshape(groups, capacity, part), 'expert', split_a...]
    all_to_all x2 -> x0, starting transfers between devices: 9.79 us -> none  [spread(): lax.all_to_all(blocks, 'expert', split_axis=0, concat_axis=0, tiled=True)]
  transfers between devices with their start and end apart: 6 -> 23, of which waited for: 6 -> 12; matrix products, arithmetic and copies ran while one was open for 20% -> 28% of each run, Pallas kernels for 0% -> 0%
where the time goes in v1:
time: 150 us; the launch traced here: 149 us
  waiting for transfers between devices  63 us (42%)
  matrix products  48.5 us (32%)
  starting transfers between devices  22.4 us (15%)
  local copies, waits for them, and re-layouts  9.29 us (6%)
  other arithmetic  5.12 us (3%)
    ppermute x23, waiting for transfers between devices, swap(): return lax.ppermute(value, AXES, pairs)  63 us
    ppermute x23, starting transfers between devices, swap(): return lax.ppermute(value, AXES, pairs)  22.4 us
    dot_general x1, matrix products, per_device(): pre_gate = jnp.dot(rows_x, gate_local, preferred_element_type=jnp.float32)  7.51 us
    dot_general x1, matrix products, per_device(): jnp.dot(grad_pre_gate, gate_local.T, preferred_element_type=jnp.float32)  7.44 us
    unnamed x25, local copies, waits for them, and re-layouts  7.41 us
    dot_general x1, matrix products, per_device(): jnp.dot(scaled.T, rows_c, preferred_element_type=jnp.float32)  5.37 us
    dot_general x1, matrix products, per_device(): jnp.dot(rows_x.T, grad_pre_gate, preferred_element_type=jnp.float32)  5.37 us
    dot_general x1, matrix products, per_device(): jnp.dot(rows_x.T, grad_pre_up, preferred_element_type=jnp.float32)  5.37 us
  transfers between devices with their start and end apart: 23, of which 12 were waited for; matrix products, arithmetic and copies ran while one was open for 28% of the time, Pallas kernels for 0%

profile of v1, /device:TPU:0, one launch (start us, length us, event | category | flops | bytes accessed | tf_op | source)
XLA Modules:
  0.0 149.4 jit_solution(5030699996583423927)
XLA Ops:
  0.7 1.8 %constant_dynamic-update-slice_fusion.7 = (bf16[512,3072]{1,0:T(8,128)(2,1)}, bf16[64,3072]{1,0:T(8,128)(2,1)S(1)}) fusion(bf16[128,3072]{1,0:T(8,128)(2,1)} %param.10, s32[]{:T(128)S(6)} %select_n.110), kind=kLoop, calls=%fused_computation.61 | loop fusion | bytes 1179652
  2.5 2.9 %collective-permute-start.13 = (bf16[64,3072]{1,0:T(8,128)(2,1)S(1)}, bf16[64,3072]{1,0:T(8,128)(2,1)S(1)}, u32[]{:S(2)}, u32[]{:S(2)}) collective-permute-start(bf16[64,3072]{1,0:T(8,128)(2,1)S(1)} %get-tuple-element.13), channel_id=1, source_target_pairs={{0,8},{1,17},{2,10},{3,19},{4,12},{5,21},{6,14},{7,23},{8,0},{9,25... | collective-permute-start | bytes 1179656 | tf_op jit(solution)/shard_map/ppermute | solution.py:19
  5.4 1.8 %constant_dynamic-update-slice_fusion.3 = (bf16[512,3072]{1,0:T(8,128)(2,1)}, bf16[64,3072]{1,0:T(8,128)(2,1)S(1)}) fusion(bf16[128,3072]{1,0:T(8,128)(2,1)} %param.7, s32[]{:T(128)S(6)} %select_n.110), kind=kLoop, calls=%fused_computation.57 | loop fusion | bytes 1179652
  7.2 0.7 fusion.24
  8.0 2.1 %collective-permute-start = (f32[128]{0:T(128)S(1)}, f32[128]{0:T(128)S(1)}, u32[]{:S(2)}, u32[]{:S(2)}) collective-permute-start(f32[128]{0:T(128)S(1)} %get-tuple-element.9), channel_id=1, source_target_pairs={{0,8},{1,9},{2,10},{3,11},{4,12},{5,13},{6,14},{7,15},{8,0},{9,1},... | collective-permute-start | bytes 1544 | tf_op jit(solution)/shard_map/ppermute | solution.py:19
  10.0 1.5 %collective-permute-start.1 = (f32[128]{0:T(128)S(1)}, f32[128]{0:T(128)S(1)}, u32[]{:S(2)}, u32[]{:S(2)}) collective-permute-start(f32[128]{0:T(128)S(1)} %get-tuple-element.11), channel_id=1, source_target_pairs={{0,16},{1,17},{2,18},{3,19},{4,20},{5,21},{6,22},{7,23},{8,24},{9,... | collective-permute-start | bytes 1544 | tf_op jit(solution)/shard_map/ppermute | solution.py:19
  11.6 0.1 slice_bitcast_fusion.5
  11.7 3.8 %collective-permute-done = f32[128]{0:T(128)S(1)} collective-permute-done((f32[128]{0:T(128)S(1)}, f32[128]{0:T(128)S(1)}, u32[]{:S(2)}, u32[]{:S(2)}) %collective-permute-start) | collective-permute-done | bytes 544 | tf_op jit(solution)/shard_map/ppermute | solution.py:19
  15.5 0.1 slice_bitcast_fusion.3
  15.6 1.3 collective-permute-done.2
  16.9 0.1 concatenate.93
  17.0 0.1 concatenate.94
  17.2 0.9 collective-permute-start.4
  18.1 1.3 collective-permute-start.14
  19.4 0.8 constant_dynamic-update-slice_fusion.2
  20.2 9.0 %collective-permute-done.4 = bf16[128,3072]{1,0:T(8,128)(2,1)S(1)} collective-permute-done((bf16[128,3072]{1,0:T(8,128)(2,1)S(1)}, bf16[128,3072]{1,0:T(8,128)(2,1)S(1)}, u32[]{:S(2)}, u32[]{:S(2)}) %collective-permute-start.4) | collective-permute-done | bytes 786464 | tf_op jit(solution)/shard_map/ppermute | solution.py:19
  29.2 0.1 pad_maximum_fusion.1
  29.4 8.2 %collective-permute-done.14 = bf16[128,3072]{1,0:T(8,128)(2,1)S(1)} collective-permute-done((bf16[128,3072]{1,0:T(8,128)(2,1)S(1)}, bf16[128,3072]{1,0:T(8,128)(2,1)S(1)}, u32[]{:S(2)}, u32[]{:S(2)}) %collective-permute-start.14) | collective-permute-done | bytes 786464 | tf_op jit(solution)/shard_map/ppermute | solution.py:19
  37.6 0.1 pad_maximum_fusion.2
  38.1 0.1 constant_dynamic-update-slice_fusion
  38.2 2.4 %copy-done.5 = bf16[1,3072,1024]{2,1,0:T(8,128)(2,1)S(1)} copy-done((bf16[1,3072,1024]{2,1,0:T(8,128)(2,1)S(1)}, bf16[1,3072,1024]{2,1,0:T(8,128)(2,1)}, u32[]{:S(2)}) %copy-start.5) | copy-done | bytes 6291480
  40.6 4.8 %fusion.6 = f32[512,1024]{1,0:T(8,128)} fusion(bf16[512,3072]{1,0:T(8,128)(2,1)S(1)} %constant_dynamic-update-slice_fusion, bf16[1,3072,1024]{2,1,0:T(8,128)(2,1)S(1)} %copy-done.5), kind=kOutput, calls=%fused_computation.6 | convolution fusion | flops 3221225472 | bytes 11534336 | tf_op jit(solution)/shard_map/dot_general | solution.py:124
  45.4 0.1 constant_dynamic-update-slice_fusion.4
  45.5 3.5 %fusion = f32[512,1024]{1,0:T(8,128)S(1)} fusion(bf16[512,3072]{1,0:T(8,128)(2,1)S(1)} %constant_dynamic-update-slice_fusion.4, bf16[1,1024,3072]{2,1,0:T(8,128)(2,1)S(1)} %bitcast.72), kind=kOutput, calls=%fused_computation | convolution fusion | flops 3221225472 | bytes 11534336 | tf_op jit(solution)/shard_map/dot_general | solution.py:134
  49.0 7.5 %multiply_convert_fusion.1 = (bf16[512,1024]{1,0:T(8,128)(2,1)S(1)}, bf16[512]{0:T(512)(128)(2,1)S(1)}, bf16[512,1024]{1,0:T(8,128)(2,1)S(1)}, bf16[512,1024]{1,0:T(8,128)(2,1)S(1)}) fusion(f32[512,1024]{1,0:T(8,128)S(1)} %copy-done.6, f32[512,1024]{1,0:T(8,128)S(1)} %fusion, f32[512]{0:T(512)S(1)} %broadcast_select_fusion, ...), kind=kOutput, calls=%fused_computation.23 | convolution fusion | flops 3231186432 | bytes 16780288 | tf_op jit(solution)/shard_map/dot_general | solution.py:123
  56.5 3.8 %fusion.14 = bf16[512,3072]{1,0:T(8,128)(2,1)S(1)} fusion(bf16[512,1024]{1,0:T(8,128)(2,1)S(1)} %get-tuple-element.19, bf16[1,1024,3072]{2,1,0:T(8,128)(2,1)S(1)} %bitcast.72), kind=kOutput, calls=%fused_computation.16 | convolution fusion | flops 3222798336 | bytes 10485760 | tf_op jit(solution)/shard_map/dot_general | solution.py:129
  60.3 0.1 slice.101
  60.5 0.6 collective-permute-start.6
  61.0 5.3 %fusion.4 = f32[512,3072]{1,0:T(8,128)} fusion(bf16[512,1024]{1,0:T(8,128)(2,1)S(1)} %get-tuple-element.18, bf16[1,3072,1024]{2,1,0:T(8,128)(2,1)S(1)} %copy-done.5), kind=kOutput, calls=%fused_computation.4 | convolution fusion | flops 3221225472 | bytes 13631488 | tf_op jit(solution)/shard_map/dot_general | solution.py:145
  66.4 7.4 %add_convert_fusion = bf16[512,3072]{1,0:T(8,128)(2,1)S(1)} fusion(f32[512,3072]{1,0:T(8,128)} %fusion.4, bf16[512,1024]{1,0:T(8,128)(2,1)S(1)} %get-tuple-element.16, bf16[1,3072,1024]{2,1,0:T(8,128)(2,1)} %param.11), kind=kOutput, calls=%fused_computation.15 | convolution fusion | flops 3224371200 | bytes 16777216 | tf_op jit(solution)/shard_map/dot_general | solution.py:144
  73.8 0.1 select_convert_fusion
  74.0 0.1 pad_maximum_fusion
  74.1 0.1 collective-permute-start.16
  74.2 0.3 copy-done.4
  74.5 5.4 %convert_bitcast_fusion.2 = bf16[1,3072,1024]{2,1,0:T(8,128)(2,1)} fusion(bf16[512,3072]{1,0:T(8,128)(2,1)S(1)} %constant_dynamic-update-slice_fusion, bf16[512,1024]{1,0:T(8,128)(2,1)S(1)} %get-tuple-element.16), kind=kOutput, calls=%fused_computation.14 | convolution fusion | flops 3224371200 | bytes 10485760 | tf_op jit(solution)/shard_map/dot_general | solution.py:159
  79.9 0.6 add_convert_fusion.2
  80.5 0.9 collective-permute-start.7
  81.4 0.5 add_convert_fusion.1
  81.9 1.3 collective-permute-start.17
  83.2 5.4 %convert_bitcast_fusion.1 = bf16[1,3072,1024]{2,1,0:T(8,128)(2,1)} fusion(bf16[512,3072]{1,0:T(8,128)(2,1)S(1)} %constant_dynamic-update-slice_fusion, bf16[512,1024]{1,0:T(8,128)(2,1)S(1)} %get-tuple-element.18), kind=kOutput, calls=%fused_computation.13 | convolution fusion | flops 3224371200 | bytes 10485760 | tf_op jit(solution)/shard_map/dot_general | solution.py:162
  88.6 4.0 %collective-permute-done.7 = bf16[128,3072]{1,0:T(8,128)(2,1)S(1)} collective-permute-done((bf16[128,3072]{1,0:T(8,128)(2,1)S(1)}, bf16[128,3072]{1,0:T(8,128)(2,1)S(1)}, u32[]{:S(2)}, u32[]{:S(2)}) %collective-permute-start.7) | collective-permute-done | bytes 786464 | tf_op jit(solution)/shard_map/ppermute | solution.py:19
  92.6 0.2 add_convert_fusion.4
  92.8 1.6 %collective-permute-start.8 = (bf16[64,3072]{1,0:T(8,128)(2,1)S(1)}, bf16[64,3072]{1,0:T(8,128)(2,1)S(1)}, u32[]{:S(2)}, u32[]{:S(2)}) collective-permute-start(bf16[64,3072]{1,0:T(8,128)(2,1)S(1)} %slice.105), channel_id=1, source_target_pairs={{0,8},{1,17},{2,10},{3,19},{4,12},{5,21},{6,14},{7,23},{8,0},{9,25... | collective-permute-start | bytes 1179656 | tf_op jit(solution)/shard_map/ppermute | solution.py:19
  94.4 11.2 %collective-permute-done.17 = bf16[128,3200]{1,0:T(8,128)(2,1)S(1)} collective-permute-done((bf16[128,3200]{1,0:T(8,128)(2,1)S(1)}, bf16[128,3200]{1,0:T(8,128)(2,1)S(1)}, u32[]{:S(2)}, u32[]{:S(2)}) %collective-permute-start.17) | collective-permute-done | bytes 819232 | tf_op jit(solution)/shard_map/ppermute | solution.py:19
  105.6 0.2 add_convert_fusion.3
  105.8 1.6 %collective-permute-start.18 = (bf16[64,3200]{1,0:T(8,128)(2,1)S(1)}, bf16[64,3200]{1,0:T(8,128)(2,1)S(1)}, u32[]{:S(2)}, u32[]{:S(2)}) collective-permute-start(bf16[64,3200]{1,0:T(8,128)(2,1)S(1)} %slice.111), channel_id=1, source_target_pairs={{0,8},{1,17},{2,10},{3,19},{4,12},{5,21},{6,14},{7,23},{8,0},{9,25... | collective-permute-start | bytes 1228808 | tf_op jit(solution)/shard_map/ppermute | solution.py:19
  107.4 0.1 add_convert_fusion.6
  107.5 1.6 %collective-permute-start.9 = (bf16[32,3072]{1,0:T(8,128)(2,1)S(1)}, bf16[32,3072]{1,0:T(8,128)(2,1)S(1)}, u32[]{:S(2)}, u32[]{:S(2)}) collective-permute-start(bf16[32,3072]{1,0:T(8,128)(2,1)S(1)} %constant_dynamic-slice_fusion.2), channel_id=1, source_target_pairs={{0,2},{1,3},{2,0},{3,1},{4,6},{5,7},{6,4},{7,5},{8,10},{9,11},{10,... | collective-permute-start | bytes 589832 | tf_op jit(solution)/shard_map/ppermute | solution.py:19
  109.1 4.7 %collective-permute-done.18 = bf16[64,3200]{1,0:T(8,128)(2,1)S(1)} collective-permute-done((bf16[64,3200]{1,0:T(8,128)(2,1)S(1)}, bf16[64,3200]{1,0:T(8,128)(2,1)S(1)}, u32[]{:S(2)}, u32[]{:S(2)}) %collective-permute-start.18) | collective-permute-done | bytes 409632 | tf_op jit(solution)/shard_map/ppermute | solution.py:19
  113.8 0.1 add_convert_fusion.5
  113.9 1.6 %collective-permute-start.19 = (bf16[32,3200]{1,0:T(8,128)(2,1)S(1)}, bf16[32,3200]{1,0:T(8,128)(2,1)S(1)}, u32[]{:S(2)}, u32[]{:S(2)}) collective-permute-start(bf16[32,3200]{1,0:T(8,128)(2,1)S(1)} %constant_dynamic-slice_fusion), channel_id=1, source_target_pairs={{0,2},{1,3},{2,0},{3,1},{4,6},{5,7},{6,4},{7,5},{8,10},{9,11},{10,... | collective-permute-start | bytes 614408 | tf_op jit(solution)/shard_map/ppermute | solution.py:19
  115.6 2.7 %collective-permute-start.10 = (bf16[32,3072]{1,0:T(8,128)(2,1)S(1)}, bf16[32,3072]{1,0:T(8,128)(2,1)S(1)}, u32[]{:S(2)}, u32[]{:S(2)}) collective-permute-start(bf16[32,3072]{1,0:T(8,128)(2,1)S(1)} %add_convert_fusion.10), channel_id=1, source_target_pairs={{0,4},{1,5},{2,6},{3,7},{4,0},{5,1},{6,2},{7,3},{8,12},{9,13},{10,... | collective-permute-start | bytes 589832 | tf_op jit(solution)/shard_map/ppermute | solution.py:19
  118.3 4.5 %collective-permute-done.19 = bf16[32,3200]{1,0:T(8,128)(2,1)S(1)} collective-permute-done((bf16[32,3200]{1,0:T(8,128)(2,1)S(1)}, bf16[32,3200]{1,0:T(8,128)(2,1)S(1)}, u32[]{:S(2)}, u32[]{:S(2)}) %collective-permute-start.19) | collective-permute-done | bytes 204832 | tf_op jit(solution)/shard_map/ppermute | solution.py:19
  122.9 1.4 collective-permute-start.20
  124.3 5.8 %collective-permute-done.10 = bf16[32,3072]{1,0:T(8,128)(2,1)S(1)} collective-permute-done((bf16[32,3072]{1,0:T(8,128)(2,1)S(1)}, bf16[32,3072]{1,0:T(8,128)(2,1)S(1)}, u32[]{:S(2)}, u32[]{:S(2)}) %collective-permute-start.10) | collective-permute-done | bytes 196640 | tf_op jit(solution)/shard_map/ppermute | solution.py:19
  130.2 4.3 %collective-permute-done.20 = bf16[32,3200]{1,0:T(8,128)(2,1)S(1)} collective-permute-done((bf16[32,3200]{1,0:T(8,128)(2,1)S(1)}, bf16[32,3200]{1,0:T(8,128)(2,1)S(1)}, u32[]{:S(2)}, u32[]{:S(2)}) %collective-permute-start.20) | collective-permute-done | bytes 204832 | tf_op jit(solution)/shard_map/ppermute | solution.py:19
  134.7 2.2 %collective-permute-done.11 = bf16[32,3072]{1,0:T(8,128)(2,1)S(1)} collective-permute-done((bf16[32,3072]{1,0:T(8,128)(2,1)S(1)}, bf16[32,3072]{1,0:T(8,128)(2,1)S(1)}, u32[]{:S(2)}, u32[]{:S(2)}) %collective-permute-start.11) | collective-permute-done | bytes 196640 | tf_op jit(solution)/shard_map/ppermute | solution.py:19
  137.0 4.0 %collective-permute-done.21 = bf16[32,3200]{1,0:T(8,128)(2,1)S(1)} collective-permute-done((bf16[32,3200]{1,0:T(8,128)(2,1)S(1)}, bf16[32,3200]{1,0:T(8,128)(2,1)S(1)}, u32[]{:S(2)}, u32[]{:S(2)}) %collective-permute-start.21) | collective-permute-done | bytes 204832 | tf_op jit(solution)/shard_map/ppermute | solution.py:19
  141.1 5.4 %convert_bitcast_fusion = bf16[1,1024,3072]{2,1,0:T(8,128)(2,1)} fusion(bf16[512,1024]{1,0:T(8,128)(2,1)S(1)} %get-tuple-element.19, bf16[512,3072]{1,0:T(8,128)(2,1)S(1)} %constant_dynamic-update-slice_fusion.4), kind=kOutput, calls=%fused_computation.12 | convolution fusion | flops 3224371200 | bytes 10485760 | tf_op jit(solution)/shard_map/dot_general | solution.py:158
  146.5 1.0 maximum_select_fusion.1
  147.5 0.1 maximum_select_fusion
  147.7 1.0 slice.112
  148.6 0.2 fusion.19
  148.8 0.6 pad_maximum_fusion.5
  (59 shorter events, 1.5 us)
Async XLA Ops:
  2.5 15.6 %collective-permute-start.13 = (bf16[64,3072]{1,0:T(8,128)(2,1)S(1)}, bf16[64,3072]{1,0:T(8,128)(2,1)S(1)}, u32[]{:S(2)}, u32[]{:S(2)}) collective-permute-start(bf16[64,3072]{1,0:T(8,128)(2,1)S(1)} %get-tuple-element.13), channel_id=1, source_target_pairs={{0,8},{1,17},{2,10},{3,19},{4,12},{5,21},{6,14},{7,23},{8,0},{9,25... | collective-permute-start | bytes 1179656 | tf_op jit(solution)/shard_map/ppermute | solution.py:19
  7.2 9.9 %collective-permute-start.3 = (bf16[64,3072]{1,0:T(8,128)(2,1)S(1)}, bf16[64,3072]{1,0:T(8,128)(2,1)S(1)}, u32[]{:S(2)}, u32[]{:S(2)}) collective-permute-start(bf16[64,3072]{1,0:T(8,128)(2,1)S(1)} %get-tuple-element.15), channel_id=1, source_target_pairs={{0,8},{1,17},{2,10},{3,19},{4,12},{5,21},{6,14},{7,23},{8,0},{9,25... | collective-permute-start | bytes 1179656 | tf_op jit(solution)/shard_map/ppermute | solution.py:19
  8.0 7.5 %collective-permute-start = (f32[128]{0:T(128)S(1)}, f32[128]{0:T(128)S(1)}, u32[]{:S(2)}, u32[]{:S(2)}) collective-permute-start(f32[128]{0:T(128)S(1)} %get-tuple-element.9), channel_id=1, source_target_pairs={{0,8},{1,9},{2,10},{3,11},{4,12},{5,13},{6,14},{7,15},{8,0},{9,1},... | collective-permute-start | bytes 1544 | tf_op jit(solution)/shard_map/ppermute | solution.py:19
  10.0 5.5 %collective-permute-start.1 = (f32[128]{0:T(128)S(1)}, f32[128]{0:T(128)S(1)}, u32[]{:S(2)}, u32[]{:S(2)}) collective-permute-start(f32[128]{0:T(128)S(1)} %get-tuple-element.11), channel_id=1, source_target_pairs={{0,16},{1,17},{2,18},{3,19},{4,20},{5,21},{6,22},{7,23},{8,24},{9,... | collective-permute-start | bytes 1544 | tf_op jit(solution)/shard_map/ppermute | solution.py:19
  11.6 5.3 %collective-permute-start.2 = (f32[128]{0:T(128)S(1)}, f32[128]{0:T(128)S(1)}, u32[]{:S(2)}, u32[]{:S(2)}) collective-permute-start(f32[128]{0:T(128)S(1)} %get-tuple-element.8), channel_id=1, source_target_pairs={{0,24},{1,25},{2,26},{3,27},{4,28},{5,29},{6,30},{7,31},{8,16},{9,... | collective-permute-start | bytes 1544 | tf_op jit(solution)/shard_map/ppermute | solution.py:19
  17.1 2.3 %copy-start.2 = (bf16[512,3072]{1,0:T(8,128)(2,1)S(1)}, bf16[512,3072]{1,0:T(8,128)(2,1)}, u32[]{:S(2)}) copy-start(bf16[512,3072]{1,0:T(8,128)(2,1)} %get-tuple-element.12) | copy-start | bytes 9437188
  17.2 12.1 %collective-permute-start.4 = (bf16[128,3072]{1,0:T(8,128)(2,1)S(1)}, bf16[128,3072]{1,0:T(8,128)(2,1)S(1)}, u32[]{:S(2)}, u32[]{:S(2)}) collective-permute-start(bf16[128,3072]{1,0:T(8,128)(2,1)S(1)} %pad_maximum_fusion.3), channel_id=1, source_target_pairs={{0,16},{1,9},{2,18},{3,11},{4,20},{5,13},{6,22},{7,15},{8,24},{9,1... | collective-permute-start | bytes 2359304 | tf_op jit(solution)/shard_map/ppermute | solution.py:19
  18.1 19.6 %collective-permute-start.14 = (bf16[128,3072]{1,0:T(8,128)(2,1)S(1)}, bf16[128,3072]{1,0:T(8,128)(2,1)S(1)}, u32[]{:S(2)}, u32[]{:S(2)}) collective-permute-start(bf16[128,3072]{1,0:T(8,128)(2,1)S(1)} %pad_maximum_fusion.4), channel_id=1, source_target_pairs={{0,16},{1,9},{2,18},{3,11},{4,20},{5,13},{6,22},{7,15},{8,24},{9,1... | collective-permute-start | bytes 2359304 | tf_op jit(solution)/shard_map/ppermute | solution.py:19
  20.2 17.7 %copy-start.3 = (bf16[512,3072]{1,0:T(8,128)(2,1)S(1)}, bf16[512,3072]{1,0:T(8,128)(2,1)}, u32[]{:S(2)}) copy-start(bf16[512,3072]{1,0:T(8,128)(2,1)} %constant_dynamic-update-slice_fusion.2) | copy-start | bytes 9437188
  29.3 8.7 %copy-start = (bf16[128,3072]{1,0:T(8,128)(2,1)S(1)}, bf16[128,3072]{1,0:T(8,128)(2,1)}, u32[]{:S(2)}) copy-start(bf16[128,3072]{1,0:T(8,128)(2,1)} %param.10) | copy-start | bytes 2359300
  29.3 8.6 %copy-start.1 = (bf16[128,3072]{1,0:T(8,128)(2,1)S(1)}, bf16[128,3072]{1,0:T(8,128)(2,1)}, u32[]{:S(2)}) copy-start(bf16[128,3072]{1,0:T(8,128)(2,1)} %param.7) | copy-start | bytes 2359300
  29.3 8.7 %collective-permute-start.5 = (bf16[192,3072]{1,0:T(8,128)(2,1)S(1)}, bf16[192,3072]{1,0:T(8,128)(2,1)S(1)}, u32[]{:S(2)}, u32[]{:S(2)}) collective-permute-start(bf16[192,3072]{1,0:T(8,128)(2,1)S(1)} %pad_maximum_fusion.1), channel_id=1, source_target_pairs={{0,1},{1,0},{2,3},{3,2},{4,5},{5,4},{6,7},{7,6},{8,9},{9,8},{10,11... | collective-permute-start | bytes 3538952 | tf_op jit(solution)/shard_map/ppermute | solution.py:19
  37.7 7.7 %collective-permute-start.15 = (bf16[192,3072]{1,0:T(8,128)(2,1)S(1)}, bf16[192,3072]{1,0:T(8,128)(2,1)S(1)}, u32[]{:S(2)}, u32[]{:S(2)}) collective-permute-start(bf16[192,3072]{1,0:T(8,128)(2,1)S(1)} %pad_maximum_fusion.2), channel_id=1, source_target_pairs={{0,1},{1,0},{2,3},{3,2},{4,5},{5,4},{6,7},{7,6},{8,9},{9,8},{10,11... | collective-permute-start | bytes 3538952 | tf_op jit(solution)/shard_map/ppermute | solution.py:19
  37.8 2.8 %copy-start.5 = (bf16[1,3072,1024]{2,1,0:T(8,128)(2,1)S(1)}, bf16[1,3072,1024]{2,1,0:T(8,128)(2,1)}, u32[]{:S(2)}) copy-start(bf16[1,3072,1024]{2,1,0:T(8,128)(2,1)} %param.12) | copy-start | bytes 18874372
  38.1 7.4 %slice-start = ((s8[6291456]{0:T(1024)(128)(4,1)}), s8[4194304]{0:T(1024)(128)(4,1)S(1)}, s32[]{:S(2)}) async-start(s8[6291456]{0:T(1024)(128)(4,1)} %bitcast.71), calls=%async_computation | async-start | bytes 8388608
  40.6 4.9 %slice-start.1 = ((s8[6291456]{0:T(1024)(128)(4,1)}), s8[2097152]{0:T(1024)(128)(4,1)S(1)}, s32[]{:S(2)}) async-start(s8[6291456]{0:T(1024)(128)(4,1)} %bitcast.71), calls=%async_computation.1 | async-start | bytes 4194304
  45.5 3.5 %copy-start.6 = (f32[512,1024]{1,0:T(8,128)S(1)}, f32[512,1024]{1,0:T(8,128)}, u32[]{:S(2)}) copy-start(f32[512,1024]{1,0:T(8,128)} %fusion.6) | copy-start | bytes 6291460
  60.5 19.4 %collective-permute-start.6 = (bf16[256,3072]{1,0:T(8,128)(2,1)S(1)}, bf16[256,3072]{1,0:T(8,128)(2,1)S(1)}, u32[]{:S(2)}, u32[]{:S(2)}) collective-permute-start(bf16[256,3072]{1,0:T(8,128)(2,1)S(1)} %slice.101), channel_id=1, source_target_pairs={{0,1},{1,0},{2,3},{3,2},{4,5},{5,4},{6,7},{7,6},{8,9},{9,8},{10,11... | collective-permute-start | bytes 4718600 | tf_op jit(solution)/shard_map/ppermute | solution.py:19
  73.8 0.7 copy-start.4
  74.1 7.3 %collective-permute-start.16 = (bf16[256,3200]{1,0:T(8,128)(2,1)S(1)}, bf16[256,3200]{1,0:T(8,128)(2,1)S(1)}, u32[]{:S(2)}, u32[]{:S(2)}) collective-permute-start(bf16[256,3200]{1,0:T(8,128)(2,1)S(1)} %pad_maximum_fusion), channel_id=1, source_target_pairs={{0,1},{1,0},{2,3},{3,2},{4,5},{5,4},{6,7},{7,6},{8,9},{9,8},{10,11... | collective-permute-start | bytes 4915208 | tf_op jit(solution)/shard_map/ppermute | solution.py:19
  80.5 12.1 %collective-permute-start.7 = (bf16[128,3072]{1,0:T(8,128)(2,1)S(1)}, bf16[128,3072]{1,0:T(8,128)(2,1)S(1)}, u32[]{:S(2)}, u32[]{:S(2)}) collective-permute-start(bf16[128,3072]{1,0:T(8,128)(2,1)S(1)} %slice.103), channel_id=1, source_target_pairs={{0,16},{1,9},{2,18},{3,11},{4,20},{5,13},{6,22},{7,15},{8,24},{9,1... | collective-permute-start | bytes 2359304 | tf_op jit(solution)/shard_map/ppermute | solution.py:19
  81.9 23.6 %collective-permute-start.17 = (bf16[128,3200]{1,0:T(8,128)(2,1)S(1)}, bf16[128,3200]{1,0:T(8,128)(2,1)S(1)}, u32[]{:S(2)}, u32[]{:S(2)}) collective-permute-start(bf16[128,3200]{1,0:T(8,128)(2,1)S(1)} %slice.109), channel_id=1, source_target_pairs={{0,16},{1,9},{2,18},{3,11},{4,20},{5,13},{6,22},{7,15},{8,24},{9,1... | collective-permute-start | bytes 2457608 | tf_op jit(solution)/shard_map/ppermute | solution.py:19
  92.8 14.6 %collective-permute-start.8 = (bf16[64,3072]{1,0:T(8,128)(2,1)S(1)}, bf16[64,3072]{1,0:T(8,128)(2,1)S(1)}, u32[]{:S(2)}, u32[]{:S(2)}) collective-permute-start(bf16[64,3072]{1,0:T(8,128)(2,1)S(1)} %slice.105), channel_id=1, source_target_pairs={{0,8},{1,17},{2,10},{3,19},{4,12},{5,21},{6,14},{7,23},{8,0},{9,25... | collective-permute-start | bytes 1179656 | tf_op jit(solution)/shard_map/ppermute | solution.py:19
  105.8 8.0 %collective-permute-start.18 = (bf16[64,3200]{1,0:T(8,128)(2,1)S(1)}, bf16[64,3200]{1,0:T(8,128)(2,1)S(1)}, u32[]{:S(2)}, u32[]{:S(2)}) collective-permute-start(bf16[64,3200]{1,0:T(8,128)(2,1)S(1)} %slice.111), channel_id=1, source_target_pairs={{0,8},{1,17},{2,10},{3,19},{4,12},{5,21},{6,14},{7,23},{8,0},{9,25... | collective-permute-start | bytes 1228808 | tf_op jit(solution)/shard_map/ppermute | solution.py:19
  107.5 8.1 %collective-permute-start.9 = (bf16[32,3072]{1,0:T(8,128)(2,1)S(1)}, bf16[32,3072]{1,0:T(8,128)(2,1)S(1)}, u32[]{:S(2)}, u32[]{:S(2)}) collective-permute-start(bf16[32,3072]{1,0:T(8,128)(2,1)S(1)} %constant_dynamic-slice_fusion.2), channel_id=1, source_target_pairs={{0,2},{1,3},{2,0},{3,1},{4,6},{5,7},{6,4},{7,5},{8,10},{9,11},{10,... | collective-permute-start | bytes 589832 | tf_op jit(solution)/shard_map/ppermute | solution.py:19
  113.9 8.9 %collective-permute-start.19 = (bf16[32,3200]{1,0:T(8,128)(2,1)S(1)}, bf16[32,3200]{1,0:T(8,128)(2,1)S(1)}, u32[]{:S(2)}, u32[]{:S(2)}) collective-permute-start(bf16[32,3200]{1,0:T(8,128)(2,1)S(1)} %constant_dynamic-slice_fusion), channel_id=1, source_target_pairs={{0,2},{1,3},{2,0},{3,1},{4,6},{5,7},{6,4},{7,5},{8,10},{9,11},{10,... | collective-permute-start | bytes 614408 | tf_op jit(solution)/shard_map/ppermute | solution.py:19
  115.6 14.4 %collective-permute-start.10 = (bf16[32,3072]{1,0:T(8,128)(2,1)S(1)}, bf16[32,3072]{1,0:T(8,128)(2,1)S(1)}, u32[]{:S(2)}, u32[]{:S(2)}) collective-permute-start(bf16[32,3072]{1,0:T(8,128)(2,1)S(1)} %add_convert_fusion.10), channel_id=1, source_target_pairs={{0,4},{1,5},{2,6},{3,7},{4,0},{5,1},{6,2},{7,3},{8,12},{9,13},{10,... | collective-permute-start | bytes 589832 | tf_op jit(solution)/shard_map/ppermute | solution.py:19
  122.9 11.7 %collective-permute-start.20 = (bf16[32,3200]{1,0:T(8,128)(2,1)S(1)}, bf16[32,3200]{1,0:T(8,128)(2,1)S(1)}, u32[]{:S(2)}, u32[]{:S(2)}) collective-permute-start(bf16[32,3200]{1,0:T(8,128)(2,1)S(1)} %add_convert_fusion.8), channel_id=1, source_target_pairs={{0,4},{1,5},{2,6},{3,7},{4,0},{5,1},{6,2},{7,3},{8,12},{9,13},{10,... | collective-permute-start | bytes 614408 | tf_op jit(solution)/shard_map/ppermute | solution.py:19
  130.1 6.7 %collective-permute-start.11 = (bf16[32,3072]{1,0:T(8,128)(2,1)S(1)}, bf16[32,3072]{1,0:T(8,128)(2,1)S(1)}, u32[]{:S(2)}, u32[]{:S(2)}) collective-permute-start(bf16[32,3072]{1,0:T(8,128)(2,1)S(1)} %add_convert_fusion.9), channel_id=1, source_target_pairs={{0,2},{1,3},{2,0},{3,1},{4,6},{5,7},{6,4},{7,5},{8,10},{9,11},{10,... | collective-permute-start | bytes 589832 | tf_op jit(solution)/shard_map/ppermute | solution.py:19
  134.6 6.4 %collective-permute-start.21 = (bf16[32,3200]{1,0:T(8,128)(2,1)S(1)}, bf16[32,3200]{1,0:T(8,128)(2,1)S(1)}, u32[]{:S(2)}, u32[]{:S(2)}) collective-permute-start(bf16[32,3200]{1,0:T(8,128)(2,1)S(1)} %add_convert_fusion.7), channel_id=1, source_target_pairs={{0,2},{1,3},{2,0},{3,1},{4,6},{5,7},{6,4},{7,5},{8,10},{9,11},{10,... | collective-permute-start | bytes 614408 | tf_op jit(solution)/shard_map/ppermute | solution.py:19
  136.9 9.6 %collective-permute-start.12 = (bf16[64,3072]{1,0:T(8,128)(2,1)S(1)}, bf16[64,3072]{1,0:T(8,128)(2,1)S(1)}, u32[]{:S(2)}, u32[]{:S(2)}) collective-permute-start(bf16[64,3072]{1,0:T(8,128)(2,1)S(1)} %maximum_select_fusion.3), channel_id=1, source_target_pairs={{0,1},{1,0},{2,3},{3,2},{4,5},{5,4},{6,7},{7,6},{8,9},{9,8},{10,11... | collective-permute-start | bytes 1179656 | tf_op jit(solution)/shard_map/ppermute | solution.py:19
  141.0 6.5 %collective-permute-start.22 = (bf16[64,3200]{1,0:T(8,128)(2,1)S(1)}, bf16[64,3200]{1,0:T(8,128)(2,1)S(1)}, u32[]{:S(2)}, u32[]{:S(2)}) collective-permute-start(bf16[64,3200]{1,0:T(8,128)(2,1)S(1)} %maximum_select_fusion.2), channel_id=1, source_target_pairs={{0,1},{1,0},{2,3},{3,2},{4,5},{5,4},{6,7},{7,6},{8,9},{9,8},{10,11... | collective-permute-start | bytes 1228808 | tf_op jit(solution)/shard_map/ppermute | solution.py:19

commit v2 on v1

v2 whole, which is shorter than its diff:
```python
import jax
import jax.numpy as jnp
from jax import lax
from jax.experimental import pallas as pl
from jax.experimental.pallas import tpu as pltpu
from jax.sharding import PartitionSpec as P

AXES = ("expert", "fsdp")
LANES = 128
BF = jnp.bfloat16
F32 = jnp.float32


def log2(size):
    return size.bit_length() - 1


def tile_of(size, most):
    tile = most
    while size % tile:
        tile -= LANES
    return tile


def swap(value, groups, shards, partner):
    pairs = []
    for e in range(groups):
        for f in range(shards):
            to_e, to_f = partner(e, f)
            pairs.append((e * shards + f, to_e * shards + to_f))
    return lax.ppermute(value, AXES, pairs)


class Links:
    def __init__(self):
        self.groups = lax.axis_size("expert")
        self.shards = lax.axis_size("fsdp")
        self.steps = log2(self.groups)
        self.expert = lax.axis_index("expert")
        fsdp = lax.axis_index("fsdp")
        self.core = fsdp % 2
        self.deep = (fsdp // 2) % 2

    def order(self, core):
        return [(k + core) % self.steps for k in range(self.steps)]

    def offsets(self, core):
        found = [0]
        for bit in self.order(core):
            found = found + [o ^ (1 << bit) for o in found]
        return found

    def to_core(self, value):
        return swap(value, self.groups, self.shards, lambda e, f: (e, f ^ 1))

    def to_expert(self, value, step):
        orders = [self.order(0), self.order(1)]
        return swap(
            value, self.groups, self.shards, lambda e, f: (e ^ (1 << orders[f % 2][step]), f)
        )

    def to_offset(self, value, offset):
        return swap(value, self.groups, self.shards, lambda e, f: (e ^ offset, f))

    def to_shard(self, value, bit):
        return swap(value, self.groups, self.shards, lambda e, f: (e, f ^ (1 << bit)))


def add(left, right):
    return (left.astype(F32) + right.astype(F32)).astype(BF)


def hold(value, *others):
    return lax.optimization_barrier((value, *others))[0]


def halves(links, rows):
    quarter = rows.shape[0] // 4
    found = []
    for core in (links.core, 1 - links.core):
        parts = [
            lax.dynamic_slice_in_dim(rows, (2 * core + deep) * quarter, quarter, 0)
            for deep in (links.deep, 1 - links.deep)
        ]
        found.append(jnp.concatenate(parts, axis=0))
    return found


def order_rows(links, per_offset):
    half, quarter = per_offset.shape[1] // 2, per_offset.shape[1] // 4
    parts = per_offset.reshape(links.groups, 2, 2, quarter)
    parts = jnp.where(links.deep == 0, parts, parts[:, :, ::-1]).reshape(links.groups, 2, half)
    middle = links.groups // 2
    chunks = []
    for part in (slice(0, middle), slice(middle, None)):
        low = jnp.concatenate([parts[o, 0] for o in links.offsets(0)[part]])
        high = jnp.concatenate([parts[o, 1] for o in links.offsets(1)[part]])
        chunks.append(
            jnp.where(
                links.core == 0, jnp.concatenate([low, high]), jnp.concatenate([high, low])
            )[:, None]
        )
    return chunks


def gather_tokens(links, own, rest):
    held = own
    for step in range(links.steps - 1):
        held = jnp.concatenate([held, links.to_expert(held, step)], axis=0)
    last = links.to_expert(held, links.steps - 1)
    other = links.to_core(held[own.shape[0] :])
    first = jnp.concatenate([held, rest, other], axis=0)
    return first, jnp.concatenate([last, links.to_core(last)], axis=0)


def gather_cotangent(links, own, rest):
    half = own.shape[0]
    quarter = half // 2
    held = own[:quarter]
    for step in range(links.steps):
        held = jnp.concatenate([held, links.to_expert(held, step)], axis=0)
    beside = links.to_shard(held[quarter:], 1)
    blocks = links.groups - 1
    both = jnp.stack(
        [held[quarter:].reshape(blocks, quarter, -1), beside.reshape(blocks, quarter, -1)], axis=1
    ).reshape(blocks * half, -1)
    other = links.to_core(both)
    middle = (links.groups // 2 - 1) * half
    first = jnp.concatenate([own, both[:middle], rest, other[:middle]], axis=0)
    return first, jnp.concatenate([both[middle:], other[middle:]], axis=0)


class Sum:
    def __init__(self, links):
        self.links = links

    def second(self, terms):
        self.late, self.sent = terms[0], self.links.to_core(terms[1])

    def first(self, terms):
        self.early, self.early_sent = terms[0], self.links.to_core(terms[1])

    def join_second(self, *after):
        self.late = add(self.late, hold(self.sent, *after))
        self.came = self.links.to_expert(self.late, self.links.steps - 1)
        return self.late

    def join_first(self, *after):
        came = hold(self.came, *after)
        total = self.early.astype(F32) + self.early_sent.astype(F32) + came.astype(F32)
        held = total.astype(BF)
        for step in reversed(range(1, self.links.steps - 1)):
            count = held.shape[0] // 2
            held = add(held[:count], self.links.to_expert(held[count:], step))
        count = held.shape[0] // 2
        self.held = held[:count]
        self.came = self.links.to_expert(held[count:], 0)
        return held

    def join_expert(self, *after):
        held = add(self.held, hold(self.came, *after))
        quarter = held.shape[0] // 2
        self.mine = held[:quarter]
        self.came = self.links.to_shard(held[quarter:], 1)
        return held

    def join_near(self, *after):
        self.mine = add(self.mine, hold(self.came, *after))
        self.came = self.links.to_shard(self.mine, 2)
        return self.mine

    def join_far(self, *after):
        self.mine = add(self.mine, hold(self.came, *after))
        for bit in range(3, log2(self.links.shards)):
            self.mine = add(self.mine, self.links.to_shard(self.mine, bit))
        self.came = self.links.to_shard(self.mine, 1)
        return self.mine

    def join_half(self, *after):
        beside = hold(self.came, *after)
        self.part = jnp.where(
            self.links.deep == 0,
            jnp.concatenate([self.mine, beside], axis=0),
            jnp.concatenate([beside, self.mine], axis=0),
        )
        self.came = self.links.to_core(self.part)
        return self.part

    def rows(self, columns, *after):
        part, other = self.part[:, columns], hold(self.came, *after)[:, columns]
        return jnp.where(
            self.links.core == 0,
            jnp.concatenate([part, other], axis=0),
            jnp.concatenate([other, part], axis=0),
        )


def whole(array):
    return pl.BlockSpec(array.shape, lambda j: (0,) * array.ndim)


def call(kernel, tiles, operands, specs, outs, out_specs, scratch, after, flops, vmem):
    size = sum(a.size * a.dtype.itemsize for a in operands)
    size += sum(a.size * a.dtype.itemsize for a in outs)
    count = len(operands)

    def body(*refs):
        kernel(*refs[:count], *refs[count + len(after) :])

    return pl.pallas_call(
        body,
        grid=(tiles,),
        in_specs=list(specs) + [pl.BlockSpec(memory_space=pl.ANY)] * len(after),
        out_specs=out_specs,
        out_shape=outs,
        scratch_shapes=scratch,
        compiler_params=pltpu.CompilerParams(vmem_limit_bytes=vmem << 20),
        cost_estimate=pl.CostEstimate(flops=flops, bytes_accessed=size, transcendentals=0),
    )(*operands, *after)


def dot(left, right, left_dim, right_dim):
    return lax.dot_general(
        left, right, (((left_dim,), (right_dim,)), ((), ())), preferred_element_type=F32
    )


def front(rows, gate, up, weight):
    pre_gate = dot(rows, gate, 1, 0)
    pre_up = dot(rows, up, 1, 0)
    sigma = jax.nn.sigmoid(pre_gate)
    silu = pre_gate * sigma
    scaled = (weight * (silu * pre_up)).astype(BF)
    slope = (weight * (pre_up * sigma * (1.0 + pre_gate * (1.0 - sigma)))).astype(BF)
    return lax.optimization_barrier(
        (scaled, slope, (weight * silu).astype(BF), pre_up.astype(BF))
    )


def hidden_grads(rows, down, slope, silu):
    raw = dot(rows, down, 1, 1)
    return lax.optimization_barrier(
        ((raw * slope.astype(F32)).astype(BF), (raw * silu.astype(F32)).astype(BF))
    )


def out_terms(scaled, down):
    middle = scaled.shape[0] // 2
    term = dot(scaled, down, 1, 0).astype(BF)
    return term[:middle], term[middle:]


def back_terms(grad_gate, grad_up, pre_up, gate, up, after=()):
    rows, units, width = grad_gate.shape[0], gate.shape[1], gate.shape[0]
    tile = tile_of(width, 512)
    tiles = width // tile
    middle = rows // 2
    nt = (((1,), (1,)), ((), ()))

    def kernel(gate_grad, up_grad, pre_ref, gate_ref, up_ref, keep_ref, send_ref):
        j = pl.program_id(0)
        term = lax.dot_general(gate_grad[...], gate_ref[...], nt, preferred_element_type=F32)
        term += lax.dot_general(up_grad[...], up_ref[...], nt, preferred_element_type=F32)
        term = term.astype(BF)
        columns = pl.ds(pl.multiple_of(j * tile, LANES), tile)
        keep_ref[:, columns] = term[:middle]
        send_ref[:, columns] = term[middle:]

        @pl.when(j == tiles - 1)
        def _():
            lane = lax.broadcasted_iota(jnp.int32, (rows, LANES), 1)
            prob = jnp.sum(
                up_grad[...].astype(F32) * pre_ref[...].astype(F32), axis=1, keepdims=True
            )
            own = jnp.where(lane == lax.axis_index("expert"), prob, 0.0).astype(BF)
            keep_ref[:, width:] = own[:middle]
            send_ref[:, width:] = own[middle:]

    block = pl.BlockSpec((middle, width + LANES), lambda j: (0, 0))
    row = pl.BlockSpec((tile, units), lambda j: (j, 0))
    return call(
        kernel,
        tiles,
        [grad_gate, grad_up, pre_up, gate, up],
        [whole(grad_gate), whole(grad_up), whole(pre_up), row, row],
        [jax.ShapeDtypeStruct((middle, width + LANES), BF)] * 2,
        [block, block],
        [],
        after,
        4 * rows * width * units,
        32,
    )


def per_device(tokens, assignment, route_weight, cotangent, w_gate, w_up, w_down):
    links = Links()
    width = tokens.shape[1]
    gate, up, down = w_gate[0], w_up[0], w_down[0]

    c_own, c_rest = lax.optimization_barrier(tuple(halves(links, cotangent)))
    x_own, x_rest = lax.optimization_barrier(tuple(halves(links, hold(tokens, c_own))))
    received = []
    for offset in range(links.groups):
        there = links.expert ^ offset
        column = jnp.sum(
            jnp.where(hold(assignment, x_own) == there, route_weight, 0.0), axis=1
        )
        received.append(column if offset == 0 else links.to_offset(column, offset))
    weight1, weight2 = order_rows(links, jnp.stack(received))
    x1, x2 = gather_tokens(links, x_own, x_rest)
    c1, c2 = gather_cotangent(links, c_own, c_rest)

    outs, backs = Sum(links), Sum(links)
    scaled1, slope1, silu1, up1 = front(x1, gate, up, weight1)
    scaled2, slope2, silu2, up2 = front(hold(x2, scaled1), gate, up, weight2)
    outs.second(lax.optimization_barrier(out_terms(scaled2, down)))
    gate_grad2, up_grad2 = hidden_grads(hold(c2, outs.late), down, slope2, silu2)
    o_late = outs.join_second(gate_grad2)
    back2 = back_terms(gate_grad2, up_grad2, up2, gate, up, after=[o_late])
    backs.second(back2)
    out1 = lax.optimization_barrier(out_terms(hold(scaled1, *back2), down))
    outs.first(out1)
    b_late = backs.join_second(*out1)
    gate_grad1, up_grad1 = hidden_grads(hold(c1, b_late), down, slope1, silu1)
    o_held = outs.join_first(gate_grad1)
    back1 = back_terms(gate_grad1, up_grad1, up1, gate, up, after=[o_held])
    backs.first(back1)
    o_sum = outs.join_expert(*back1)

    x_all = jnp.concatenate([x1, x2], axis=0)
    c_all = jnp.concatenate([c1, c2], axis=0)
    scaled = jnp.concatenate([scaled1, scaled2], axis=0)
    gate_grad = jnp.concatenate([gate_grad1, gate_grad2], axis=0)
    up_grad = jnp.concatenate([up_grad1, up_grad2], axis=0)
    grad_down = dot(hold(scaled, o_sum), c_all, 0, 0).astype(BF)
    b_held = backs.join_first(grad_down)
    o_near = outs.join_near(b_held)
    grad_gate = dot(hold(x_all, o_near), gate_grad, 0, 0).astype(BF)
    b_sum = backs.join_expert(grad_gate)
    o_far = outs.join_far(b_sum)
    b_near = backs.join_near(o_far)
    grad_up = dot(hold(x_all, b_near), up_grad, 0, 0).astype(BF)
    o_part = outs.join_half(grad_up)
    b_far = backs.join_far(o_part)
    moe_out = outs.rows(slice(0, width), b_far)
    backs.join_half(moe_out)

    grad_tokens = backs.rows(slice(0, width))
    prob_all = backs.rows(slice(width, None)).astype(F32)
    lane = lax.broadcasted_iota(jnp.int32, (1, LANES), 1)
    grad_prob = jnp.stack(
        [
            jnp.sum(jnp.where(lane == assignment[:, k : k + 1], prob_all, 0.0), axis=1)
            for k in range(assignment.shape[1])
        ],
        axis=1,
    )
    grad_prob = grad_prob / route_weight
    return (moe_out, grad_tokens, grad_prob, grad_gate[None], grad_up[None], grad_down[None])


def solution(mesh):
    return jax.shard_map(
        per_device,
        mesh=mesh,
        in_specs=(
            P("expert", None),
            P("expert", None),
            P("expert", None),
            P("expert", None),
            P("expert", None, "fsdp"),
            P("expert", None, "fsdp"),
            P("expert", "fsdp", None),
        ),
        out_specs=(
            P("expert", None),
            P("expert", None),
            P("expert", None),
            P("expert", None, "fsdp"),
            P("expert", None, "fsdp"),
            P("expert", "fsdp", None),
        ),
        check_vma=False,
    )
```

time: 150 us -> 126 us (0.84)
  waiting for transfers between devices: 63 us -> 33.2 us
  Pallas kernels: 0 us -> 9.4 us
  matrix products: 48.5 us -> 42.8 us
  starting transfers between devices: 22.4 us -> 24.5 us
    ppermute x23 -> x27, waiting for transfers between devices: 63 us -> 33.2 us  [swap(): return lax.ppermute(value, AXES, pairs)]
    pallas_call x0 -> x2, Pallas kernels: none -> 9.4 us  [call(): pl.pallas_call(body, grid=(tiles,), in_specs=list(specs) + [pl.BlockSpec(...]
    dot_general x9 -> x11, matrix products: 48.5 us -> 42.8 us  [dot(): lax.dot_general(left, right, (((left_dim,), (right_dim,)), ((), ())), pre...]
    ppermute x23 -> x27, starting transfers between devices: 22.4 us -> 24.5 us  [swap(): return lax.ppermute(value, AXES, pairs)]
    unnamed x25 -> x36, local copies, waits for them, and re-layouts: 7.41 us -> 5.8 us
  transfers between devices with their start and end apart: 23 -> 27, of which waited for: 12 -> 11; matrix products, arithmetic and copies ran while one was open for 28% -> 42% of each run, Pallas kernels for 0% -> 7%
where the time goes in v2:
time: 126 us
  matrix products  42.8 us (34%)
  waiting for transfers between devices  33.2 us (26%)
  starting transfers between devices  24.5 us (19%)
  Pallas kernels  9.4 us (7%)
  local copies, waits for them, and re-layouts  9.16 us (7%)
  other arithmetic  5.38 us (4%)
  between operations  1.31 us (1%)
    dot_general x11, matrix products, dot(): lax.dot_general(left, right, (((left_dim,), (right_dim,)), ((), ())), pre...  42.8 us
    ppermute x27, waiting for transfers between devices, swap(): return lax.ppermute(value, AXES, pairs)  33.2 us
    ppermute x27, starting transfers between devices, swap(): return lax.ppermute(value, AXES, pairs)  24.5 us
    pallas_call x2, Pallas kernels, call(): pl.pallas_call(body, grid=(tiles,), in_specs=list(specs) + [pl.BlockSpec(...  9.4 us
    unnamed x36, local copies, waits for them, and re-layouts  5.8 us
  transfers between devices with their start and end apart: 27, of which 11 were waited for; matrix products, arithmetic and copies ran while one was open for 42% of the time, Pallas kernels for 7%

profile of v2, /device:TPU:0, one launch (start us, length us, event | category | flops | bytes accessed | tf_op | source)
XLA Modules:
  0.0 125.7 jit_solution(18099577863737901377)
XLA Ops:
  0.7 1.3 %constant_dynamic-slice_fusion.5 = (bf16[32,3072]{1,0:T(8,128)(2,1)S(1)}, bf16[32,3072]{1,0:T(8,128)(2,1)S(1)}, bf16[32,3072]{1,0:T(8,128)(2,1)S(1)}, bf16[32,3072]{1,0:T(8,128)(2,1)S(1)}) fusion(bf16[128,3072]{1,0:T(8,128)(2,1)} %param.10, s32[]{:T(128)S(6)} %select_n.124, s32[]{:T(128)S(6)} %select_n.123, s32[]{:T(128)S(6)} %select_n.122, s32[]{:T(128)S(6)} %select_n.125), kind=kLoop, calls=%fused_computation.99 | loop fusion | bytes 1572880 | tf_op jit(solution)/shard_map/dynamic_slice | solution.py:82
  2.1 3.0 %collective-permute-start.5 = (bf16[32,3072]{1,0:T(8,128)(2,1)S(1)}, bf16[32,3072]{1,0:T(8,128)(2,1)S(1)}, u32[]{:S(2)}, u32[]{:S(2)}) collective-permute-start(bf16[32,3072]{1,0:T(8,128)(2,1)S(1)} %slice.106), channel_id=1, source_target_pairs={{0,8},{1,17},{2,10},{3,19},{4,12},{5,21},{6,14},{7,23},{8,0},{9,25... | collective-permute-start | bytes 589832 | tf_op jit(solution)/shard_map/ppermute | solution.py:31
  5.4 2.0 %collective-permute-start = (f32[128]{0:T(128)S(1)}, f32[128]{0:T(128)S(1)}, u32[]{:S(2)}, u32[]{:S(2)}) collective-permute-start(f32[128]{0:T(128)S(1)} %get-tuple-element.102), channel_id=1, source_target_pairs={{0,8},{1,9},{2,10},{3,11},{4,12},{5,13},{6,14},{7,15},{8,0},{9,1},... | collective-permute-start | bytes 1544 | tf_op jit(solution)/shard_map/ppermute | solution.py:31
  7.5 1.5 %collective-permute-start.1 = (f32[128]{0:T(128)S(1)}, f32[128]{0:T(128)S(1)}, u32[]{:S(2)}, u32[]{:S(2)}) collective-permute-start(f32[128]{0:T(128)S(1)} %get-tuple-element.101), channel_id=1, source_target_pairs={{0,16},{1,17},{2,18},{3,19},{4,20},{5,21},{6,22},{7,23},{8,24},{9,... | collective-permute-start | bytes 1544 | tf_op jit(solution)/shard_map/ppermute | solution.py:31
  9.0 0.8 constant_dynamic-update-slice_fusion.15
  9.8 1.0 constant_dynamic-update-slice_fusion.21
  10.8 2.4 %collective-permute-done = f32[128]{0:T(128)S(1)} collective-permute-done((f32[128]{0:T(128)S(1)}, f32[128]{0:T(128)S(1)}, u32[]{:S(2)}, u32[]{:S(2)}) %collective-permute-start) | collective-permute-done | bytes 544 | tf_op jit(solution)/shard_map/ppermute | solution.py:31
  13.4 1.1 collective-permute-done.2
  14.9 0.9 collective-permute-start.6
  15.9 1.2 collective-permute-start.9
  17.2 1.0 constant_dynamic-update-slice_fusion.20
  18.1 1.0 constant_dynamic-update-slice_fusion.19
  19.1 3.7 %collective-permute-done.6 = bf16[64,3072]{1,0:T(8,128)(2,1)S(1)} collective-permute-done((bf16[64,3072]{1,0:T(8,128)(2,1)S(1)}, bf16[64,3072]{1,0:T(8,128)(2,1)S(1)}, u32[]{:S(2)}, u32[]{:S(2)}) %collective-permute-start.6) | collective-permute-done | bytes 393248 | tf_op jit(solution)/shard_map/ppermute | solution.py:31
  22.8 1.6 %collective-permute-start.7 = (bf16[96,3072]{1,0:T(8,128)(2,1)S(1)}, bf16[96,3072]{1,0:T(8,128)(2,1)S(1)}, u32[]{:S(2)}, u32[]{:S(2)}) collective-permute-start(bf16[96,3072]{1,0:T(8,128)(2,1)S(1)} %constant_dynamic-update-slice_fusion.8), channel_id=1, source_target_pairs={{0,2},{1,3},{2,0},{3,1},{4,6},{5,7},{6,4},{7,5},{8,10},{9,11},{10,... | collective-permute-start | bytes 1769480 | tf_op jit(solution)/shard_map/ppermute | solution.py:31
  24.4 1.0 constant_dynamic-update-slice_fusion.18
  25.4 3.8 %fusion.34 = f32[256,1024]{1,0:T(8,128)S(1)} fusion(bf16[256,3072]{1,0:T(8,128)(2,1)} %get-tuple-element.133, bf16[1,3072,1024]{2,1,0:T(8,128)(2,1)S(1)} %copy-done), kind=kOutput, calls=%fused_computation.127 | convolution fusion | flops 1610612736 | bytes 8912896 | tf_op jit(solution)/shard_map/dot_general | solution.py:223
  29.3 2.4 %multiply_convert_fusion.8 = (bf16[256,1024]{1,0:T(8,128)(2,1)S(1)}, bf16[256,1024]{1,0:T(8,128)(2,1)S(1)}, bf16[256,1024]{1,0:T(8,128)(2,1)S(1)}, bf16[256,1024]{1,0:T(8,128)(2,1)S(1)}) fusion(f32[256,1024]{1,0:T(8,128)S(1)} %fusion.34, f32[256]{0:T(256)S(1)} %maximum_select_fusion.5, bf16[256,3072]{1,0:T(8,128)(2,1)S(1)} %copy-done.2, ...), kind=kOutput, calls=%fused_computation.42 | convolution fusion | flops 1615069184 | bytes 11011072 | tf_op jit(solution)/shard_map/dot_general | solution.py:223
  31.7 3.5 %collective-permute-done.7 = bf16[96,3072]{1,0:T(8,128)(2,1)S(1)} collective-permute-done((bf16[96,3072]{1,0:T(8,128)(2,1)S(1)}, bf16[96,3072]{1,0:T(8,128)(2,1)S(1)}, u32[]{:S(2)}, u32[]{:S(2)}) %collective-permute-start.7) | collective-permute-done | bytes 589856 | tf_op jit(solution)/shard_map/ppermute | solution.py:31
  35.2 0.1 pad_maximum_fusion.3
  35.5 0.6 collective-permute-start.10
  36.2 0.9 constant_dynamic-update-slice_fusion.17
  37.1 2.2 %collective-permute-done.10 = bf16[128,3072]{1,0:T(8,128)(2,1)S(1)} collective-permute-done((bf16[128,3072]{1,0:T(8,128)(2,1)S(1)}, bf16[128,3072]{1,0:T(8,128)(2,1)S(1)}, u32[]{:S(2)}, u32[]{:S(2)}) %collective-permute-start.10) | collective-permute-done | bytes 786464 | tf_op jit(solution)/shard_map/ppermute | solution.py:31
  39.5 1.8 %fusion.32 = f32[256,1024]{1,0:T(8,128)S(1)} fusion(bf16[256,3072]{1,0:T(8,128)(2,1)S(1)} %pad_maximum_fusion.1, bf16[1,3072,1024]{2,1,0:T(8,128)(2,1)S(1)} %copy-done), kind=kOutput, calls=%fused_computation.125 | convolution fusion | flops 1610612736 | bytes 8912896 | tf_op jit(solution)/shard_map/dot_general | solution.py:223
  41.3 2.3 %multiply_convert_fusion.5 = (bf16[256,1024]{1,0:T(8,128)(2,1)S(1)}, bf16[256,1024]{1,0:T(8,128)(2,1)S(1)}, bf16[256,1024]{1,0:T(8,128)(2,1)S(1)}, bf16[256,1024]{1,0:T(8,128)(2,1)S(1)}) fusion(f32[256,1024]{1,0:T(8,128)S(1)} %fusion.32, f32[256]{0:T(256)S(1)} %maximum_select_fusion.6, bf16[256,3072]{1,0:T(8,128)(2,1)S(1)} %pad_maximum_fusion.1, ...), kind=kOutput, calls=%fused_computation.37 | convolution fusion | flops 1615069184 | bytes 11011072 | tf_op jit(solution)/shard_map/dot_general | solution.py:223
  43.7 1.8 %fusion.8 = bf16[256,3072]{1,0:T(8,128)(2,1)S(1)} fusion(bf16[256,1024]{1,0:T(8,128)(2,1)S(1)} %get-tuple-element.59, bf16[1,1024,3072]{2,1,0:T(8,128)(2,1)S(1)} %bitcast.97), kind=kOutput, calls=%fused_computation.11 | convolution fusion | flops 1611399168 | bytes 8388608 | tf_op jit(solution)/shard_map/dot_general | solution.py:223
  45.6 0.1 fusion.41
  45.7 0.2 collective-permute-start.11
  45.9 0.9 constant_dynamic-update-slice_fusion.16
  47.0 0.2 constant_dynamic-update-slice_fusion.10
  47.1 0.1 pad_maximum_fusion
  47.3 4.9 %multiply_convert_fusion.2 = (bf16[256,1024]{1,0:T(8,128)(2,1)S(1)}, bf16[256,1024]{1,0:T(8,128)(2,1)S(1)}) fusion(bf16[256,1024]{1,0:T(8,128)(2,1)S(1)} %get-tuple-element.63, bf16[256,1024]{1,0:T(8,128)(2,1)S(1)} %get-tuple-element.62, bf16[256,3072]{1,0:T(8,128)(2,1)S(1)} %pad_maximum_fusion, bf16[1,1024,3072]{2,1,0:T(8,128)(2,1)} %param.13), kind=kOutput, calls=%fused_computation.34 | convolution fusion | flops 1612185600 | bytes 9961472 | tf_op jit(solution)/shard_map/dot_general | solution.py:223
  52.1 0.1 pad_maximum_fusion.2
  52.2 0.2 add_convert_fusion.3.refs_5_
  52.4 1.7 %collective-permute-start.13 = (bf16[128,3072]{1,0:T(8,128)(2,1)S(1)}, bf16[128,3072]{1,0:T(8,128)(2,1)S(1)}, u32[]{:S(2)}, u32[]{:S(2)}) collective-permute-start(bf16[128,3072]{1,0:T(8,128)(2,1)S(1)} %add_convert_fusion.3.refs_5_), channel_id=1, source_target_pairs={{0,16},{1,9},{2,18},{3,11},{4,20},{5,13},{6,22},{7,15},{8,24},{9,1... | collective-permute-start | bytes 2359304 | tf_op jit(solution)/shard_map/ppermute | solution.py:31
  54.2 4.7 %shard_map.118 = (bf16[128,3200]{1,0:T(8,128)(2,1)S(1)}, bf16[128,3200]{1,0:T(8,128)(2,1)S(1)}) custom-call(bf16[256,1024]{1,0:T(8,128)(2,1)S(1)} %get-tuple-element.64.refs_0_, bf16[256,1024]{1,0:T(8,128)(2,1)S(1)} %get-tuple-element.65.refs_1_, bf16[256,1024]{1,0:T(8,128)(2,1)S(1)} %get-tuple-element.66.refs_2_, bf16[3072,1024]{1,0:T(8,128)(2,1)S(1)} %bitcast.81, ...), custom_call_target="tpu_custom_call" | custom-call | flops 3221225472 | bytes 15794176 | tf_op jit(solution)/shard_map/pallas_call | solution.py:210
  58.9 0.1 collective-permute-start.14
  59.0 4.6 %fusion.11 = bf16[256,3072]{1,0:T(8,128)(2,1)S(1)} fusion(bf16[256,1024]{1,0:T(8,128)(2,1)S(1)} %get-tuple-element.71, bf16[1,1024,3072]{2,1,0:T(8,128)(2,1)} %param.13), kind=kOutput, calls=%fused_computation.12 | convolution fusion | flops 1611399168 | bytes 8388608 | tf_op jit(solution)/shard_map/dot_general | solution.py:223
  63.6 0.1 fusion.40
  63.7 0.5 collective-permute-start.12
  64.2 0.2 add_convert_fusion.1
  64.4 4.7 %multiply_convert_fusion = (bf16[256,1024]{1,0:T(8,128)(2,1)S(1)}, bf16[256,1024]{1,0:T(8,128)(2,1)S(1)}) fusion(bf16[256,1024]{1,0:T(8,128)(2,1)S(1)} %get-tuple-element.78, bf16[256,1024]{1,0:T(8,128)(2,1)S(1)} %get-tuple-element.77, bf16[256,3072]{1,0:T(8,128)(2,1)S(1)} %pad_maximum_fusion.2, bf16[1,1024,3072]{2,1,0:T(8,128)(2,1)} %param.13), kind=kOutput, calls=%fused_computation.32 | convolution fusion | flops 1612185600 | bytes 9961472 | tf_op jit(solution)/shard_map/dot_general | solution.py:223
  69.1 0.4 add_convert_fusion.2.refs_5_
  69.5 1.6 %collective-permute-start.15 = (bf16[64,3072]{1,0:T(8,128)(2,1)S(1)}, bf16[64,3072]{1,0:T(8,128)(2,1)S(1)}, u32[]{:S(2)}, u32[]{:S(2)}) collective-permute-start(bf16[64,3072]{1,0:T(8,128)(2,1)S(1)} %slice.154), channel_id=1, source_target_pairs={{0,8},{1,17},{2,10},{3,19},{4,12},{5,21},{6,14},{7,23},{8,0},{9,25... | collective-permute-start | bytes 1179656 | tf_op jit(solution)/shard_map/ppermute | solution.py:31
  71.2 0.6 collective-permute-start.18
  71.7 4.7 %shard_map.119 = (bf16[128,3200]{1,0:T(8,128)(2,1)S(1)}, bf16[128,3200]{1,0:T(8,128)(2,1)S(1)}) custom-call(bf16[256,1024]{1,0:T(8,128)(2,1)S(1)} %get-tuple-element.79.refs_0_, bf16[256,1024]{1,0:T(8,128)(2,1)S(1)} %get-tuple-element.81.refs_1_, bf16[256,1024]{1,0:T(8,128)(2,1)S(1)} %get-tuple-element.82.refs_2_, bf16[3072,1024]{1,0:T(8,128)(2,1)S(1)} %bitcast.82, ...), custom_call_target="tpu_custom_call" | custom-call | flops 3221225472 | bytes 15794176 | tf_op jit(solution)/shard_map/pallas_call | solution.py:210
  76.5 4.7 %collective-permute-done.15 = bf16[64,3072]{1,0:T(8,128)(2,1)S(1)} collective-permute-done((bf16[64,3072]{1,0:T(8,128)(2,1)S(1)}, bf16[64,3072]{1,0:T(8,128)(2,1)S(1)}, u32[]{:S(2)}, u32[]{:S(2)}) %collective-permute-start.15) | collective-permute-done | bytes 393248 | tf_op jit(solution)/shard_map/ppermute | solution.py:31
  81.3 1.6 %collective-permute-start.16 = (bf16[32,3072]{1,0:T(8,128)(2,1)S(1)}, bf16[32,3072]{1,0:T(8,128)(2,1)S(1)}, u32[]{:S(2)}, u32[]{:S(2)}) collective-permute-start(bf16[32,3072]{1,0:T(8,128)(2,1)S(1)} %slice.156), channel_id=1, source_target_pairs={{0,2},{1,3},{2,0},{3,1},{4,6},{5,7},{6,4},{7,5},{8,10},{9,11},{10,... | collective-permute-start | bytes 589832 | tf_op jit(solution)/shard_map/ppermute | solution.py:31
  83.0 5.4 %convolution_convert_fusion.2 = bf16[1024,3072]{1,0:T(8,128)(2,1)} fusion(bf16[512,1024]{1,0:T(8,128)(2,1)S(1)} %pad_maximum_fusion.4, bf16[512,3072]{1,0:T(8,128)(2,1)S(1)} %get-tuple-element.112), kind=kOutput, calls=%fused_computation.10 | convolution fusion | flops 3224371200 | bytes 10485760 | tf_op jit(solution)/shard_map/dot_general | solution.py:223
  88.3 0.3 add_convert_fusion
  88.8 2.6 %collective-permute-start.19 = (bf16[32,3072]{1,0:T(8,128)(2,1)S(1)}, bf16[32,3072]{1,0:T(8,128)(2,1)S(1)}, u32[]{:S(2)}, u32[]{:S(2)}) collective-permute-start(bf16[32,3072]{1,0:T(8,128)(2,1)S(1)} %add_convert_fusion.9), channel_id=1, source_target_pairs={{0,4},{1,5},{2,6},{3,7},{4,0},{5,1},{6,2},{7,3},{8,12},{9,13},{10,... | collective-permute-start | bytes 589832 | tf_op jit(solution)/shard_map/ppermute | solution.py:31
  91.4 1.8 %collective-permute-start.20 = (bf16[64,3200]{1,0:T(8,128)(2,1)S(1)}, bf16[64,3200]{1,0:T(8,128)(2,1)S(1)}, u32[]{:S(2)}, u32[]{:S(2)}) collective-permute-start(bf16[64,3200]{1,0:T(8,128)(2,1)S(1)} %slice.158), channel_id=1, source_target_pairs={{0,8},{1,17},{2,10},{3,19},{4,12},{5,21},{6,14},{7,23},{8,0},{9,25... | collective-permute-start | bytes 1228808 | tf_op jit(solution)/shard_map/ppermute | solution.py:31
  93.2 5.4 %convolution_convert_fusion.1 = bf16[3072,1024]{1,0:T(8,128)(2,1)} fusion(bf16[512,3072]{1,0:T(8,128)(2,1)S(1)} %copy-done.4, bf16[256,1024]{1,0:T(8,128)(2,1)S(1)} %get-tuple-element.64.refs_0_, bf16[256,1024]{1,0:T(8,128)(2,1)S(1)} %get-tuple-element.79.refs_0_), kind=kOutput, calls=%fused_computation.9 | convolution fusion | flops 3226468352 | bytes 10485760 | tf_op jit(solution)/shard_map/dot_general | solution.py:223
  98.7 0.7 collective-permute-done.20
  99.5 0.5 collective-permute-start.22
  100.1 1.6 %collective-permute-start.21 = (bf16[32,3072]{1,0:T(8,128)(2,1)S(1)}, bf16[32,3072]{1,0:T(8,128)(2,1)S(1)}, u32[]{:S(2)}, u32[]{:S(2)}) collective-permute-start(bf16[32,3072]{1,0:T(8,128)(2,1)S(1)} %add_convert_fusion.8), channel_id=1, source_target_pairs={{0,2},{1,3},{2,0},{3,1},{4,6},{5,7},{6,4},{7,5},{8,10},{9,11},{10,... | collective-permute-start | bytes 589832 | tf_op jit(solution)/shard_map/ppermute | solution.py:31
  101.7 6.0 %collective-permute-done.22 = bf16[32,3200]{1,0:T(8,128)(2,1)S(1)} collective-permute-done((bf16[32,3200]{1,0:T(8,128)(2,1)S(1)}, bf16[32,3200]{1,0:T(8,128)(2,1)S(1)}, u32[]{:S(2)}, u32[]{:S(2)}) %collective-permute-start.22) | collective-permute-done | bytes 204832 | tf_op jit(solution)/shard_map/ppermute | solution.py:31
  107.8 5.7 %convolution_convert_fusion = bf16[3072,1024]{1,0:T(8,128)(2,1)} fusion(bf16[512,3072]{1,0:T(8,128)(2,1)S(1)} %copy-done.4, bf16[256,1024]{1,0:T(8,128)(2,1)S(1)} %get-tuple-element.65.refs_1_, bf16[256,1024]{1,0:T(8,128)(2,1)S(1)} %get-tuple-element.81.refs_1_), kind=kOutput, calls=%fused_computation.8 | convolution fusion | flops 3226468352 | bytes 10485760 | tf_op jit(solution)/shard_map/dot_general | solution.py:223
  113.6 2.5 %collective-permute-done.24 = bf16[32,3200]{1,0:T(8,128)(2,1)S(1)} collective-permute-done((bf16[32,3200]{1,0:T(8,128)(2,1)S(1)}, bf16[32,3200]{1,0:T(8,128)(2,1)S(1)}, u32[]{:S(2)}, u32[]{:S(2)}) %collective-permute-start.24) | collective-permute-done | bytes 204832 | tf_op jit(solution)/shard_map/ppermute | solution.py:31
  116.3 1.0 maximum_select_fusion
  117.3 4.7 %collective-permute-done.25 = bf16[32,3200]{1,0:T(8,128)(2,1)S(1)} collective-permute-done((bf16[32,3200]{1,0:T(8,128)(2,1)S(1)}, bf16[32,3200]{1,0:T(8,128)(2,1)S(1)}, u32[]{:S(2)}, u32[]{:S(2)}) %collective-permute-start.25) | collective-permute-done | bytes 204832 | tf_op jit(solution)/shard_map/ppermute | solution.py:31
  122.2 1.7 %collective-permute-done.26 = bf16[64,3200]{1,0:T(8,128)(2,1)S(1)} collective-permute-done((bf16[64,3200]{1,0:T(8,128)(2,1)S(1)}, bf16[64,3200]{1,0:T(8,128)(2,1)S(1)}, u32[]{:S(2)}, u32[]{:S(2)}) %collective-permute-start.26) | collective-permute-done | bytes 409632 | tf_op jit(solution)/shard_map/ppermute | solution.py:31
  123.9 0.2 fusion.24
  124.1 0.6 maximum_divide_fusion
  124.7 1.0 maximum_select_fusion.1
  (98 shorter events, 2.8 us)
Async XLA Ops:
  0.6 4.5 %copy-start.1 = (bf16[128,3072]{1,0:T(8,128)(2,1)S(1)}, bf16[128,3072]{1,0:T(8,128)(2,1)}, u32[]{:S(2)}) copy-start(bf16[128,3072]{1,0:T(8,128)(2,1)} %param.7) | copy-start | bytes 2359300
  2.1 3.3 %copy-start.5 = (f32[128,2]{0,1:T(2,128)S(1)}, f32[128,2]{0,1:T(2,128)}, u32[]{:S(2)}) copy-start(f32[128,2]{0,1:T(2,128)} %param.9) | copy-start | bytes 3076
  2.1 3.3 %copy-start.6 = (s32[128,2]{0,1:T(2,128)S(1)}, s32[128,2]{0,1:T(2,128)}, u32[]{:S(2)}) copy-start(s32[128,2]{0,1:T(2,128)} %param.8) | copy-start | bytes 3076
  2.1 12.7 %collective-permute-start.5 = (bf16[32,3072]{1,0:T(8,128)(2,1)S(1)}, bf16[32,3072]{1,0:T(8,128)(2,1)S(1)}, u32[]{:S(2)}, u32[]{:S(2)}) collective-permute-start(bf16[32,3072]{1,0:T(8,128)(2,1)S(1)} %slice.106), channel_id=1, source_target_pairs={{0,8},{1,17},{2,10},{3,19},{4,12},{5,21},{6,14},{7,23},{8,0},{9,25... | collective-permute-start | bytes 589832 | tf_op jit(solution)/shard_map/ppermute | solution.py:31
  5.3 10.6 %collective-permute-start.3 = (bf16[64,3072]{1,0:T(8,128)(2,1)S(1)}, bf16[64,3072]{1,0:T(8,128)(2,1)S(1)}, u32[]{:S(2)}, u32[]{:S(2)}) collective-permute-start(bf16[64,3072]{1,0:T(8,128)(2,1)S(1)} %pad_maximum_fusion.8), channel_id=1, source_target_pairs={{0,8},{1,17},{2,10},{3,19},{4,12},{5,21},{6,14},{7,23},{8,0},{9,25... | collective-permute-start | bytes 1179656 | tf_op jit(solution)/shard_map/ppermute | solution.py:31
  5.4 7.8 %collective-permute-start = (f32[128]{0:T(128)S(1)}, f32[128]{0:T(128)S(1)}, u32[]{:S(2)}, u32[]{:S(2)}) collective-permute-start(f32[128]{0:T(128)S(1)} %get-tuple-element.102), channel_id=1, source_target_pairs={{0,8},{1,9},{2,10},{3,11},{4,12},{5,13},{6,14},{7,15},{8,0},{9,1},... | collective-permute-start | bytes 1544 | tf_op jit(solution)/shard_map/ppermute | solution.py:31
  7.5 5.8 %collective-permute-start.1 = (f32[128]{0:T(128)S(1)}, f32[128]{0:T(128)S(1)}, u32[]{:S(2)}, u32[]{:S(2)}) collective-permute-start(f32[128]{0:T(128)S(1)} %get-tuple-element.101), channel_id=1, source_target_pairs={{0,16},{1,17},{2,18},{3,19},{4,20},{5,21},{6,22},{7,23},{8,24},{9,... | collective-permute-start | bytes 1544 | tf_op jit(solution)/shard_map/ppermute | solution.py:31
  9.0 5.5 %collective-permute-start.2 = (f32[128]{0:T(128)S(1)}, f32[128]{0:T(128)S(1)}, u32[]{:S(2)}, u32[]{:S(2)}) collective-permute-start(f32[128]{0:T(128)S(1)} %get-tuple-element.100), channel_id=1, source_target_pairs={{0,24},{1,25},{2,26},{3,27},{4,28},{5,29},{6,30},{7,31},{8,16},{9,... | collective-permute-start | bytes 1544 | tf_op jit(solution)/shard_map/ppermute | solution.py:31
  14.9 7.8 %collective-permute-start.6 = (bf16[64,3072]{1,0:T(8,128)(2,1)S(1)}, bf16[64,3072]{1,0:T(8,128)(2,1)S(1)}, u32[]{:S(2)}, u32[]{:S(2)}) collective-permute-start(bf16[64,3072]{1,0:T(8,128)(2,1)S(1)} %pad_maximum_fusion.10), channel_id=1, source_target_pairs={{0,16},{1,9},{2,18},{3,11},{4,20},{5,13},{6,22},{7,15},{8,24},{9,1... | collective-permute-start | bytes 1179656 | tf_op jit(solution)/shard_map/ppermute | solution.py:31
  15.8 9.6 %copy-start = (bf16[1,3072,1024]{2,1,0:T(8,128)(2,1)S(1)}, bf16[1,3072,1024]{2,1,0:T(8,128)(2,1)}, u32[]{:S(2)}) copy-start(bf16[1,3072,1024]{2,1,0:T(8,128)(2,1)} %param.12) | copy-start | bytes 18874372
  15.9 19.6 %collective-permute-start.9 = (bf16[128,3072]{1,0:T(8,128)(2,1)S(1)}, bf16[128,3072]{1,0:T(8,128)(2,1)S(1)}, u32[]{:S(2)}, u32[]{:S(2)}) collective-permute-start(bf16[128,3072]{1,0:T(8,128)(2,1)S(1)} %pad_maximum_fusion.5), channel_id=1, source_target_pairs={{0,16},{1,9},{2,18},{3,11},{4,20},{5,13},{6,22},{7,15},{8,24},{9,1... | collective-permute-start | bytes 2359304 | tf_op jit(solution)/shard_map/ppermute | solution.py:31
  17.2 7.3 %collective-permute-start.4 = (bf16[64,3072]{1,0:T(8,128)(2,1)S(1)}, bf16[64,3072]{1,0:T(8,128)(2,1)S(1)}, u32[]{:S(2)}, u32[]{:S(2)}) collective-permute-start(bf16[64,3072]{1,0:T(8,128)(2,1)S(1)} %collective-permute-done.3), channel_id=1, source_target_pairs={{0,1},{1,0},{2,3},{3,2},{4,5},{5,4},{6,7},{7,6},{8,9},{9,8},{10,11... | collective-permute-start | bytes 1179656 | tf_op jit(solution)/shard_map/ppermute | solution.py:31
  22.8 12.4 %collective-permute-start.7 = (bf16[96,3072]{1,0:T(8,128)(2,1)S(1)}, bf16[96,3072]{1,0:T(8,128)(2,1)S(1)}, u32[]{:S(2)}, u32[]{:S(2)}) collective-permute-start(bf16[96,3072]{1,0:T(8,128)(2,1)S(1)} %constant_dynamic-update-slice_fusion.8), channel_id=1, source_target_pairs={{0,2},{1,3},{2,0},{3,1},{4,6},{5,7},{6,4},{7,5},{8,10},{9,11},{10,... | collective-permute-start | bytes 1769480 | tf_op jit(solution)/shard_map/ppermute | solution.py:31
  24.4 4.8 %slice-start = ((s8[6291456]{0:T(1024)(128)(4,1)}), s8[4194304]{0:T(1024)(128)(4,1)S(1)}, s32[]{:S(2)}) async-start(s8[6291456]{0:T(1024)(128)(4,1)} %bitcast.79), calls=%async_computation | async-start | bytes 8388608
  25.4 3.9 %slice-start.1 = ((s8[6291456]{0:T(1024)(128)(4,1)}), s8[2097152]{0:T(1024)(128)(4,1)S(1)}, s32[]{:S(2)}) async-start(s8[6291456]{0:T(1024)(128)(4,1)} %bitcast.79), calls=%async_computation.1 | async-start | bytes 4194304
  25.4 3.9 %copy-start.2 = (bf16[256,3072]{1,0:T(8,128)(2,1)S(1)}, bf16[256,3072]{1,0:T(8,128)(2,1)}, u32[]{:S(2)}) copy-start(bf16[256,3072]{1,0:T(8,128)(2,1)} %get-tuple-element.133) | copy-start | bytes 4718596
  31.7 3.8 %copy-start.3 = (bf16[512,3072]{1,0:T(8,128)(2,1)S(1)}, bf16[512,3072]{1,0:T(8,128)(2,1)}, u32[]{:S(2)}) copy-start(bf16[512,3072]{1,0:T(8,128)(2,1)} %constant_dynamic-update-slice_fusion.15) | copy-start | bytes 9437188
  35.3 11.5 %collective-permute-start.8 = (bf16[192,3072]{1,0:T(8,128)(2,1)S(1)}, bf16[192,3072]{1,0:T(8,128)(2,1)S(1)}, u32[]{:S(2)}, u32[]{:S(2)}) collective-permute-start(bf16[192,3072]{1,0:T(8,128)(2,1)S(1)} %bitcast.93), channel_id=1, source_target_pairs={{0,1},{1,0},{2,3},{3,2},{4,5},{5,4},{6,7},{7,6},{8,9},{9,8},{10,11... | collective-permute-start | bytes 3538952 | tf_op jit(solution)/shard_map/ppermute | solution.py:31
  35.5 3.9 %collective-permute-start.10 = (bf16[128,3072]{1,0:T(8,128)(2,1)S(1)}, bf16[128,3072]{1,0:T(8,128)(2,1)S(1)}, u32[]{:S(2)}, u32[]{:S(2)}) collective-permute-start(bf16[128,3072]{1,0:T(8,128)(2,1)S(1)} %collective-permute-done.9), channel_id=1, source_target_pairs={{0,1},{1,0},{2,3},{3,2},{4,5},{5,4},{6,7},{7,6},{8,9},{9,8},{10,11... | collective-permute-start | bytes 2359304 | tf_op jit(solution)/shard_map/ppermute | solution.py:31
  39.5 4.2 %slice-start.2 = ((s8[6291456]{0:T(1024)(128)(4,1)}), s8[4194304]{0:T(1024)(128)(4,1)S(1)}, s32[]{:S(2)}) async-start(s8[6291456]{0:T(1024)(128)(4,1)} %bitcast.96), calls=%async_computation.2 | async-start | bytes 8388608
  41.3 2.4 %slice-start.3 = ((s8[6291456]{0:T(1024)(128)(4,1)}), s8[2097152]{0:T(1024)(128)(4,1)S(1)}, s32[]{:S(2)}) async-start(s8[6291456]{0:T(1024)(128)(4,1)} %bitcast.96), calls=%async_computation.3 | async-start | bytes 4194304
  45.7 6.6 %collective-permute-start.11 = (bf16[128,3072]{1,0:T(8,128)(2,1)S(1)}, bf16[128,3072]{1,0:T(8,128)(2,1)S(1)}, u32[]{:S(2)}, u32[]{:S(2)}) collective-permute-start(bf16[128,3072]{1,0:T(8,128)(2,1)S(1)} %get-tuple-element.67), channel_id=1, source_target_pairs={{0,1},{1,0},{2,3},{3,2},{4,5},{5,4},{6,7},{7,6},{8,9},{9,8},{10,11... | collective-permute-start | bytes 2359304 | tf_op jit(solution)/shard_map/ppermute | solution.py:31
  52.4 16.7 %collective-permute-start.13 = (bf16[128,3072]{1,0:T(8,128)(2,1)S(1)}, bf16[128,3072]{1,0:T(8,128)(2,1)S(1)}, u32[]{:S(2)}, u32[]{:S(2)}) collective-permute-start(bf16[128,3072]{1,0:T(8,128)(2,1)S(1)} %add_convert_fusion.3.refs_5_), channel_id=1, source_target_pairs={{0,16},{1,9},{2,18},{3,11},{4,20},{5,13},{6,22},{7,15},{8,24},{9,1... | collective-permute-start | bytes 2359304 | tf_op jit(solution)/shard_map/ppermute | solution.py:31
  58.9 5.3 %collective-permute-start.14 = (bf16[128,3200]{1,0:T(8,128)(2,1)S(1)}, bf16[128,3200]{1,0:T(8,128)(2,1)S(1)}, u32[]{:S(2)}, u32[]{:S(2)}) collective-permute-start(bf16[128,3200]{1,0:T(8,128)(2,1)S(1)} %get-tuple-element.70), channel_id=1, source_target_pairs={{0,1},{1,0},{2,3},{3,2},{4,5},{5,4},{6,7},{7,6},{8,9},{9,8},{10,11... | collective-permute-start | bytes 2457608 | tf_op jit(solution)/shard_map/ppermute | solution.py:31
  63.7 5.4 %collective-permute-start.12 = (bf16[128,3072]{1,0:T(8,128)(2,1)S(1)}, bf16[128,3072]{1,0:T(8,128)(2,1)S(1)}, u32[]{:S(2)}, u32[]{:S(2)}) collective-permute-start(bf16[128,3072]{1,0:T(8,128)(2,1)S(1)} %get-tuple-element.73), channel_id=1, source_target_pairs={{0,1},{1,0},{2,3},{3,2},{4,5},{5,4},{6,7},{7,6},{8,9},{9,8},{10,11... | collective-permute-start | bytes 2359304 | tf_op jit(solution)/shard_map/ppermute | solution.py:31
  69.5 11.7 %collective-permute-start.15 = (bf16[64,3072]{1,0:T(8,128)(2,1)S(1)}, bf16[64,3072]{1,0:T(8,128)(2,1)S(1)}, u32[]{:S(2)}, u32[]{:S(2)}) collective-permute-start(bf16[64,3072]{1,0:T(8,128)(2,1)S(1)} %slice.154), channel_id=1, source_target_pairs={{0,8},{1,17},{2,10},{3,19},{4,12},{5,21},{6,14},{7,23},{8,0},{9,25... | collective-permute-start | bytes 1179656 | tf_op jit(solution)/shard_map/ppermute | solution.py:31
  71.2 17.2 %collective-permute-start.18 = (bf16[128,3200]{1,0:T(8,128)(2,1)S(1)}, bf16[128,3200]{1,0:T(8,128)(2,1)S(1)}, u32[]{:S(2)}, u32[]{:S(2)}) collective-permute-start(bf16[128,3200]{1,0:T(8,128)(2,1)S(1)} %add_convert_fusion.1), channel_id=1, source_target_pairs={{0,16},{1,9},{2,18},{3,11},{4,20},{5,13},{6,22},{7,15},{8,24},{9,1... | collective-permute-start | bytes 2457608 | tf_op jit(solution)/shard_map/ppermute | solution.py:31
  76.5 11.9 %collective-permute-start.17 = (bf16[128,3200]{1,0:T(8,128)(2,1)S(1)}, bf16[128,3200]{1,0:T(8,128)(2,1)S(1)}, u32[]{:S(2)}, u32[]{:S(2)}) collective-permute-start(bf16[128,3200]{1,0:T(8,128)(2,1)S(1)} %get-tuple-element.84), channel_id=1, source_target_pairs={{0,1},{1,0},{2,3},{3,2},{4,5},{5,4},{6,7},{7,6},{8,9},{9,8},{10,11... | collective-permute-start | bytes 2457608 | tf_op jit(solution)/shard_map/ppermute | solution.py:31
  81.3 7.4 %collective-permute-start.16 = (bf16[32,3072]{1,0:T(8,128)(2,1)S(1)}, bf16[32,3072]{1,0:T(8,128)(2,1)S(1)}, u32[]{:S(2)}, u32[]{:S(2)}) collective-permute-start(bf16[32,3072]{1,0:T(8,128)(2,1)S(1)} %slice.156), channel_id=1, source_target_pairs={{0,2},{1,3},{2,0},{3,1},{4,6},{5,7},{6,4},{7,5},{8,10},{9,11},{10,... | collective-permute-start | bytes 589832 | tf_op jit(solution)/shard_map/ppermute | solution.py:31
  88.3 4.9 %copy-start.4 = (bf16[512,3072]{1,0:T(8,128)(2,1)S(1)}, bf16[512,3072]{1,0:T(8,128)(2,1)}, u32[]{:S(2)}) copy-start(bf16[512,3072]{1,0:T(8,128)(2,1)} %constant_dynamic-update-slice_fusion.16) | copy-start | bytes 9437188
  88.8 11.3 %collective-permute-start.19 = (bf16[32,3072]{1,0:T(8,128)(2,1)S(1)}, bf16[32,3072]{1,0:T(8,128)(2,1)S(1)}, u32[]{:S(2)}, u32[]{:S(2)}) collective-permute-start(bf16[32,3072]{1,0:T(8,128)(2,1)S(1)} %add_convert_fusion.9), channel_id=1, source_target_pairs={{0,4},{1,5},{2,6},{3,7},{4,0},{5,1},{6,2},{7,3},{8,12},{9,13},{10,... | collective-permute-start | bytes 589832 | tf_op jit(solution)/shard_map/ppermute | solution.py:31
  91.4 8.0 %collective-permute-start.20 = (bf16[64,3200]{1,0:T(8,128)(2,1)S(1)}, bf16[64,3200]{1,0:T(8,128)(2,1)S(1)}, u32[]{:S(2)}, u32[]{:S(2)}) collective-permute-start(bf16[64,3200]{1,0:T(8,128)(2,1)S(1)} %slice.158), channel_id=1, source_target_pairs={{0,8},{1,17},{2,10},{3,19},{4,12},{5,21},{6,14},{7,23},{8,0},{9,25... | collective-permute-start | bytes 1228808 | tf_op jit(solution)/shard_map/ppermute | solution.py:31
  99.5 8.2 %collective-permute-start.22 = (bf16[32,3200]{1,0:T(8,128)(2,1)S(1)}, bf16[32,3200]{1,0:T(8,128)(2,1)S(1)}, u32[]{:S(2)}, u32[]{:S(2)}) collective-permute-start(bf16[32,3200]{1,0:T(8,128)(2,1)S(1)} %slice.160), channel_id=1, source_target_pairs={{0,2},{1,3},{2,0},{3,1},{4,6},{5,7},{6,4},{7,5},{8,10},{9,11},{10,... | collective-permute-start | bytes 614408 | tf_op jit(solution)/shard_map/ppermute | solution.py:31
  100.1 13.4 %collective-permute-start.21 = (bf16[32,3072]{1,0:T(8,128)(2,1)S(1)}, bf16[32,3072]{1,0:T(8,128)(2,1)S(1)}, u32[]{:S(2)}, u32[]{:S(2)}) collective-permute-start(bf16[32,3072]{1,0:T(8,128)(2,1)S(1)} %add_convert_fusion.8), channel_id=1, source_target_pairs={{0,2},{1,3},{2,0},{3,1},{4,6},{5,7},{6,4},{7,5},{8,10},{9,11},{10,... | collective-permute-start | bytes 589832 | tf_op jit(solution)/shard_map/ppermute | solution.py:31
  107.7 8.4 %collective-permute-start.24 = (bf16[32,3200]{1,0:T(8,128)(2,1)S(1)}, bf16[32,3200]{1,0:T(8,128)(2,1)S(1)}, u32[]{:S(2)}, u32[]{:S(2)}) collective-permute-start(bf16[32,3200]{1,0:T(8,128)(2,1)S(1)} %add_convert_fusion.7), channel_id=1, source_target_pairs={{0,4},{1,5},{2,6},{3,7},{4,0},{5,1},{6,2},{7,3},{8,12},{9,13},{10,... | collective-permute-start | bytes 614408 | tf_op jit(solution)/shard_map/ppermute | solution.py:31
  113.5 2.7 %collective-permute-start.23 = (bf16[64,3072]{1,0:T(8,128)(2,1)S(1)}, bf16[64,3072]{1,0:T(8,128)(2,1)S(1)}, u32[]{:S(2)}, u32[]{:S(2)}) collective-permute-start(bf16[64,3072]{1,0:T(8,128)(2,1)S(1)} %maximum_select_fusion.3), channel_id=1, source_target_pairs={{0,1},{1,0},{2,3},{3,2},{4,5},{5,4},{6,7},{7,6},{8,9},{9,8},{10,11... | collective-permute-start | bytes 1179656 | tf_op jit(solution)/shard_map/ppermute | solution.py:31
  116.2 5.8 %collective-permute-start.25 = (bf16[32,3200]{1,0:T(8,128)(2,1)S(1)}, bf16[32,3200]{1,0:T(8,128)(2,1)S(1)}, u32[]{:S(2)}, u32[]{:S(2)}) collective-permute-start(bf16[32,3200]{1,0:T(8,128)(2,1)S(1)} %add_convert_fusion.6), channel_id=1, source_target_pairs={{0,2},{1,3},{2,0},{3,1},{4,6},{5,7},{6,4},{7,5},{8,10},{9,11},{10,... | collective-permute-start | bytes 614408 | tf_op jit(solution)/shard_map/ppermute | solution.py:31
  122.1 1.8 %collective-permute-start.26 = (bf16[64,3200]{1,0:T(8,128)(2,1)S(1)}, bf16[64,3200]{1,0:T(8,128)(2,1)S(1)}, u32[]{:S(2)}, u32[]{:S(2)}) collective-permute-start(bf16[64,3200]{1,0:T(8,128)(2,1)S(1)} %maximum_select_fusion.2), channel_id=1, source_target_pairs={{0,1},{1,0},{2,3},{3,2},{4,5},{5,4},{6,7},{7,6},{8,9},{9,8},{10,11... | collective-permute-start | bytes 1228808 | tf_op jit(solution)/shard_map/ppermute | solution.py:31

commit v3 on v2

v3 whole, which is shorter than its diff:
```python
import jax
import jax.numpy as jnp
from jax import lax
from jax.experimental import pallas as pl
from jax.experimental.pallas import tpu as pltpu
from jax.sharding import PartitionSpec as P

AXES = ("expert", "fsdp")
LANES = 128
BACK_VMEM = 32
EARLY_FLOPS = 60_000_000_000
BF = jnp.bfloat16
F32 = jnp.float32


def log2(size):
    return size.bit_length() - 1


def tile_of(size, most):
    tile = most
    while size % tile:
        tile -= LANES
    return tile


def swap(value, groups, shards, partner):
    pairs = []
    for e in range(groups):
        for f in range(shards):
            to_e, to_f = partner(e, f)
            pairs.append((e * shards + f, to_e * shards + to_f))
    return lax.ppermute(value, AXES, pairs)


class Links:
    def __init__(self):
        self.groups = lax.axis_size("expert")
        self.shards = lax.axis_size("fsdp")
        self.steps = log2(self.groups)
        self.expert = lax.axis_index("expert")
        fsdp = lax.axis_index("fsdp")
        self.core = fsdp % 2
        self.deep = (fsdp // 2) % 2

    def order(self, core):
        return [(k + core) % self.steps for k in range(self.steps)]

    def offsets(self, core):
        found = [0]
        for bit in self.order(core):
            found = found + [o ^ (1 << bit) for o in found]
        return found

    def to_core(self, value):
        return swap(value, self.groups, self.shards, lambda e, f: (e, f ^ 1))

    def to_expert(self, value, step):
        orders = [self.order(0), self.order(1)]
        return swap(
            value, self.groups, self.shards, lambda e, f: (e ^ (1 << orders[f % 2][step]), f)
        )

    def to_offset(self, value, offset):
        return swap(value, self.groups, self.shards, lambda e, f: (e ^ offset, f))

    def to_shard(self, value, bit):
        return swap(value, self.groups, self.shards, lambda e, f: (e, f ^ (1 << bit)))


def add(left, right):
    return (left.astype(F32) + right.astype(F32)).astype(BF)


def hold(value, *others):
    return lax.optimization_barrier((value, *others))[0]


def halves(links, rows, routes=(), weight=0):
    count, width = rows.shape
    quarter, groups = count // 4, links.groups
    extra = LANES if routes else 0
    top = routes[0].shape[1] if routes else 0

    def kernel(*refs):
        inputs, (own_ref, rest_ref) = refs[: 1 + len(routes)], refs[1 + len(routes) :][:2]
        names_ref, weights_ref, sems = refs[-3:]
        fsdp = lax.axis_index("fsdp")
        core, deep = fsdp % 2, (fsdp // 2) % 2
        copies = []
        for source, target in zip(inputs[1:], (names_ref, weights_ref)):
            copies.append((source, target))
        for target, side in ((own_ref, core), (rest_ref, 1 - core)):
            for place, part in enumerate((deep, 1 - deep)):
                start = pl.multiple_of((2 * side + part) * quarter, quarter)
                here = pl.ds(place * quarter, quarter)
                copies.append(
                    (inputs[0].at[pl.ds(start, quarter), :], target.at[here, pl.ds(0, width)])
                )
        copies = [
            pltpu.make_async_copy(source, target, sems.at[k])
            for k, (source, target) in enumerate(copies)
        ]
        for copy in copies:
            copy.start()
        for copy in copies:
            copy.wait()
        if routes:
            source = lax.broadcasted_iota(jnp.int32, (count, count), 1)
            index = lax.broadcasted_iota(jnp.int32, (count, count), 0)
            lane = lax.broadcasted_iota(jnp.int32, (1, LANES), 1)
            for target, side in ((own_ref, core), (rest_ref, 1 - core)):
                place = (index // quarter) % 2
                part = jnp.where(place == 0, deep, 1 - deep)
                wanted = (2 * side + part) * quarter + index % quarter
                left = jnp.zeros((count, LANES), F32)
                for k in range(top):
                    chosen = source == wanted
                    names = jnp.where(chosen, names_ref[k : k + 1, :].astype(F32), 0.0)
                    weights = jnp.where(chosen, weights_ref[k : k + 1, :], 0.0)
                    name = jnp.sum(names, axis=1, keepdims=True)
                    weight = jnp.sum(weights, axis=1, keepdims=True)
                    left += jnp.where(name == (lane % groups).astype(F32), weight, 0.0)
                columns = jnp.zeros_like(left)
                for limb in range(3):
                    high = left.astype(BF).astype(F32)
                    columns = jnp.where(lane // groups == limb, high, columns)
                    left = left - high
                target[:, width:] = columns[: 2 * quarter].astype(BF)

    operands = [rows, *(route.T for route in routes)]
    return pl.pallas_call(
        kernel,
        in_specs=[pl.BlockSpec(memory_space=pltpu.HBM)] * len(operands),
        out_specs=[pl.BlockSpec(memory_space=pltpu.VMEM)] * 2,
        out_shape=[jax.ShapeDtypeStruct((2 * quarter, width + extra), BF)] * 2,
        scratch_shapes=[
            pltpu.VMEM((max(top, 1), count), jnp.int32),
            pltpu.VMEM((max(top, 1), count), F32),
            pltpu.SemaphoreType.DMA((6,)),
        ],
        compiler_params=pltpu.CompilerParams(vmem_limit_bytes=(16 if weight else 63) << 20),
        cost_estimate=pl.CostEstimate(flops=weight, bytes_accessed=0, transcendentals=0),
    )(*operands)


class Rows:
    def __init__(self, links, rows, routes=(), weight=0):
        self.links = links
        self.own, self.rest = halves(links, rows, routes, weight)
        self.came = None
        if links.steps > 1:
            self.came = links.to_expert(self.own, 0)

    def send(self, *after):
        links, held, pieces = self.links, self.own, []
        for step in range(links.steps - 1):
            came = hold(self.came, *after) if step == 0 else links.to_expert(held, step)
            held = jnp.concatenate([held, came], axis=0)
            pieces.append(came)
        self.held = held
        self.last = links.to_expert(self.held, links.steps - 1)
        self.other = links.to_core(jnp.concatenate(pieces, axis=0))

    def first(self, *after):
        return jnp.concatenate([self.held, self.rest, hold(self.other, *after)], axis=0)

    def second(self, *after):
        last = hold(self.last, *after)
        return jnp.concatenate([last, self.links.to_core(last)], axis=0)


def joined(pieces, *after):
    return jnp.concatenate(lax.optimization_barrier((*pieces, *after))[: len(pieces)], axis=0)


class Sum:
    def __init__(self, links):
        self.links = links

    def second(self, terms):
        self.late, self.sent = terms[0], self.links.to_core(terms[1])

    def first(self, terms):
        self.early, self.early_sent = terms[0], self.links.to_core(terms[1])

    def join_second(self, *after):
        self.late = add(self.late, hold(self.sent, *after))
        self.came = self.links.to_expert(self.late, self.links.steps - 1)
        return self.late

    def join_first(self, *after):
        came = hold(self.came, *after)
        total = self.early.astype(F32) + self.early_sent.astype(F32) + came.astype(F32)
        held = total.astype(BF)
        for step in reversed(range(1, self.links.steps - 1)):
            count = held.shape[0] // 2
            held = add(held[:count], self.links.to_expert(held[count:], step))
        count = held.shape[0] // 2
        self.held = held[:count]
        self.came = self.links.to_expert(held[count:], 0)
        return held

    def join_expert(self, *after):
        held = add(self.held, hold(self.came, *after))
        quarter = held.shape[0] // 2
        self.mine = held[:quarter]
        self.came = self.links.to_shard(held[quarter:], 1)
        return held

    def join_near(self, *after):
        self.mine = add(self.mine, hold(self.came, *after))
        self.came = self.links.to_shard(self.mine, 2)
        return self.mine

    def join_far(self, *after):
        self.mine = add(self.mine, hold(self.came, *after))
        for bit in range(3, log2(self.links.shards)):
            self.mine = add(self.mine, self.links.to_shard(self.mine, bit))
        self.came = self.links.to_shard(self.mine, 1)
        return self.mine

    def join_half(self, *after):
        beside = hold(self.came, *after)
        self.part = jnp.where(
            self.links.deep == 0,
            jnp.concatenate([self.mine, beside], axis=0),
            jnp.concatenate([beside, self.mine], axis=0),
        )
        self.came = self.links.to_core(self.part)
        return self.part

    def rows(self, columns, *after):
        part, other = self.part[:, columns], hold(self.came, *after)[:, columns]
        return jnp.where(
            self.links.core == 0,
            jnp.concatenate([part, other], axis=0),
            jnp.concatenate([other, part], axis=0),
        )


def dot(left, right, left_dim, right_dim):
    return lax.dot_general(
        left, right, (((left_dim,), (right_dim,)), ((), ())), preferred_element_type=F32
    )


def front(rows, gate, up, *after):
    pre_gate = dot(rows, gate, 1, 0)
    pre_up = dot(hold(rows, pre_gate, *after), up, 1, 0)
    sigma = jax.nn.sigmoid(pre_gate)
    silu = pre_gate * sigma
    hidden = (silu * pre_up).astype(BF)
    slope = (pre_up * sigma * (1.0 + pre_gate * (1.0 - sigma))).astype(BF)
    return lax.optimization_barrier((hidden, slope, silu.astype(BF), pre_up.astype(BF)))


def hidden_grads(rows, down, slope, silu, weight):
    raw = dot(rows, down, 1, 1) * weight
    return lax.optimization_barrier(
        ((raw * slope.astype(F32)).astype(BF), (raw * silu.astype(F32)).astype(BF))
    )


def out_terms(hidden, down, weight):
    middle = hidden.shape[0] // 2
    term = (dot(hidden, down, 1, 0) * weight).astype(BF)
    return term[:middle], term[middle:]


def back_terms(grads_gate, grads_up, pre_ups, gate, up):
    rows, units, width = grads_gate[0].shape[0], gate.shape[1], gate.shape[0]
    chunks = len(grads_gate)
    tile = tile_of(width, 512)
    tiles = width // tile
    middle = rows // 2
    nt = (((1,), (1,)), ((), ()))

    def kernel(*refs):
        grad_refs = refs[: 3 * chunks]
        gate_ref, up_ref = refs[3 * chunks : 3 * chunks + 2]
        outs = refs[3 * chunks + 2 : 3 * chunks + 2 + 2 * chunks]
        gate_all, up_all = refs[-2:]
        j = pl.program_id(0)

        @pl.when(j == 0)
        def _():
            for k in range(chunks):
                gate_all[k * rows : (k + 1) * rows, :] = grad_refs[k][...]
                up_all[k * rows : (k + 1) * rows, :] = grad_refs[chunks + k][...]

        term = lax.dot_general(gate_all[...], gate_ref[...], nt, preferred_element_type=F32)
        term += lax.dot_general(up_all[...], up_ref[...], nt, preferred_element_type=F32)
        term = term.astype(BF)
        columns = pl.ds(pl.multiple_of(j * tile, LANES), tile)
        for k in range(2 * chunks):
            outs[k][:, columns] = term[k * middle : (k + 1) * middle]

        @pl.when(j == tiles - 1)
        def _():
            lane = lax.broadcasted_iota(jnp.int32, (rows, LANES), 1)
            for k in range(chunks):
                prob = jnp.sum(
                    grad_refs[chunks + k][...].astype(F32)
                    * grad_refs[2 * chunks + k][...].astype(F32),
                    axis=1,
                    keepdims=True,
                )
                own = jnp.where(lane == lax.axis_index("expert"), prob, 0.0).astype(BF)
                outs[2 * k][:, width:] = own[:middle]
                outs[2 * k + 1][:, width:] = own[middle:]

    operands = [*grads_gate, *grads_up, *pre_ups, gate, up]
    size = sum(a.size * a.dtype.itemsize for a in operands)
    size += 2 * chunks * middle * (width + LANES) * 2
    block = pl.BlockSpec((middle, width + LANES), lambda j: (0, 0))
    full = pl.BlockSpec((rows, units), lambda j: (0, 0))
    row = pl.BlockSpec((tile, units), lambda j: (j, 0))
    outs = pl.pallas_call(
        kernel,
        grid=(tiles,),
        in_specs=[full] * (3 * chunks) + [row] * 2,
        out_specs=[block] * (2 * chunks),
        out_shape=[jax.ShapeDtypeStruct((middle, width + LANES), BF)] * (2 * chunks),
        scratch_shapes=[pltpu.VMEM((chunks * rows, units), BF)] * 2,
        compiler_params=pltpu.CompilerParams(vmem_limit_bytes=BACK_VMEM << 20),
        cost_estimate=pl.CostEstimate(
            flops=0, bytes_accessed=0, transcendentals=0
        ),
    )(*operands)
    return [(outs[2 * k], outs[2 * k + 1]) for k in range(chunks)]


def per_device(tokens, assignment, route_weight, cotangent, w_gate, w_up, w_down):
    links = Links()
    width = tokens.shape[1]
    gate, up, down = w_gate[0], w_up[0], w_down[0]
    lane = lax.broadcasted_iota(jnp.int32, (1, LANES), 1)

    x = Rows(links, tokens, (assignment, route_weight))
    c = Rows(links, hold(cotangent, x.own), weight=EARLY_FLOPS)

    def weights(chunk):
        own = jnp.logical_and(lane % links.groups == links.expert, lane < 3 * links.groups)
        limbs = jnp.where(own, chunk[:, width:].astype(F32), 0.0)
        return jnp.sum(limbs, axis=1, keepdims=True)

    outs, backs = Sum(links), Sum(links)
    x.send()
    x1 = x.first()
    hidden1, slope1, silu1, up1 = front(x1[:, :width], gate, up, c.came)
    weight1 = weights(x1)
    c.send(x1)
    c1 = c.first()
    gate_grad1, up_grad1 = hidden_grads(c1, down, slope1, silu1, weight1)
    x2 = x.second()
    x2 = hold(x2, gate_grad1)
    hidden2, slope2, silu2, up2 = front(x2[:, :width], gate, up)
    weight2 = weights(x2)
    out2 = lax.optimization_barrier(out_terms(hidden2, down, weight2))
    outs.second(out2)
    out1 = lax.optimization_barrier(out_terms(hold(hidden1, *out2), down, weight1))
    outs.first(out1)
    o_late = outs.join_second(*out1)
    c2 = c.second(hidden2)
    gate_grad2, up_grad2 = hidden_grads(hold(c2, o_late), down, slope2, silu2, weight2)
    (back2,) = back_terms([gate_grad2], [up_grad2], [up2], gate, up)
    backs.second(back2)
    o_held = outs.join_first(*back2)
    (back1,) = back_terms([hold(gate_grad1, o_held)], [up_grad1], [up1], gate, up)
    backs.first(back1)
    b_late = backs.join_second(*back1)

    weight = jnp.concatenate([weight1, weight2], axis=0)
    scaled = (joined([hidden1, hidden2], b_late).astype(F32) * weight).astype(BF)
    grad_down = dot(scaled, joined([c1, c2], b_late), 0, 0).astype(BF)
    o_sum = outs.join_expert(grad_down)
    b_held = backs.join_first(o_sum)
    x_all = joined([x1, x2], b_held)[:, :width]
    grad_gate = dot(x_all, joined([gate_grad1, gate_grad2]), 0, 0).astype(BF)
    b_sum = backs.join_expert(grad_gate)
    o_near = outs.join_near(b_sum)
    b_near = backs.join_near(o_near)
    grad_up = dot(hold(x_all, b_near), joined([up_grad1, up_grad2]), 0, 0).astype(BF)
    o_far = outs.join_far(grad_up)
    b_far = backs.join_far(o_far)
    o_part = outs.join_half(b_far)
    backs.join_half(o_part)
    moe_out = outs.rows(slice(0, width), backs.part)

    grad_tokens = backs.rows(slice(0, width))
    prob_all = backs.rows(slice(width, None)).astype(F32)
    grad_prob = jnp.stack(
        [
            jnp.sum(jnp.where(lane == assignment[:, k : k + 1], prob_all, 0.0), axis=1)
            for k in range(assignment.shape[1])
        ],
        axis=1,
    )
    grad_prob = grad_prob / route_weight
    return (moe_out, grad_tokens, grad_prob, grad_gate[None], grad_up[None], grad_down[None])


def solution(mesh):
    return jax.shard_map(
        per_device,
        mesh=mesh,
        in_specs=(
            P("expert", None),
            P("expert", None),
            P("expert", None),
            P("expert", None),
            P("expert", None, "fsdp"),
            P("expert", None, "fsdp"),
            P("expert", "fsdp", None),
        ),
        out_specs=(
            P("expert", None),
            P("expert", None),
            P("expert", None),
            P("expert", None, "fsdp"),
            P("expert", None, "fsdp"),
            P("expert", "fsdp", None),
        ),
        check_vma=False,
    )
```

time: 126 us -> 114 us (0.905)
  waiting for transfers between devices: 33.2 us -> 27.5 us
  matrix products: 42.8 us -> 37.5 us
  local copies, waits for them, and re-layouts: 9.16 us -> 4.7 us
  Pallas kernels: 9.4 us -> 12.9 us
    ppermute x27 -> x24, waiting for transfers between devices: 33.2 us -> 27.5 us  [swap(): return lax.ppermute(value, AXES, pairs)]
    dot_general x11, matrix products: 42.8 us -> 37.5 us  [dot(): lax.dot_general(left, right, (((left_dim,), (right_dim,)), ((), ())), pre...]
    pallas_call x2 -> x4, Pallas kernels: 9.4 us -> 12.9 us  [the longest x2 9.55 us: back_terms(): pl.pallas_call(kernel, grid=(tiles,), in_specs=[full] * (3 * chunks) + [r...]
    unnamed x36 -> x21, local copies, waits for them, and re-layouts: 5.8 us -> 3.91 us
    dynamic_slice x2 -> x0, local copies, waits for them, and re-layouts: 1.38 us -> none  [halves(): lax.dynamic_slice_in_dim(rows, (2 * core + deep) * quarter, quarter, 0)]
    ppermute x27 -> x24, starting transfers between devices: 24.5 us -> 24.2 us  [swap(): return lax.ppermute(value, AXES, pairs)]
  transfers between devices with their start and end apart: 27 -> 24, of which waited for: 11 -> 11; matrix products, arithmetic and copies ran while one was open for 42% -> 37% of each run, Pallas kernels for 7% -> 9%
where the time goes in v3:
time: 114 us; the launch traced here: 113 us
  matrix products  37.5 us (33%)
  waiting for transfers between devices  27.5 us (24%)
  starting transfers between devices  24.2 us (21%)
  Pallas kernels  12.9 us (11%)
  other arithmetic  5.47 us (5%)
  local copies, waits for them, and re-layouts  4.7 us (4%)
    dot_general x11, matrix products, dot(): lax.dot_general(left, right, (((left_dim,), (right_dim,)), ((), ())), pre...  37.5 us
    ppermute x24, waiting for transfers between devices, swap(): return lax.ppermute(value, AXES, pairs)  27.5 us
    ppermute x24, starting transfers between devices, swap(): return lax.ppermute(value, AXES, pairs)  24.2 us
    pallas_call x2, Pallas kernels, back_terms(): pl.pallas_call(kernel, grid=(tiles,), in_specs=[full] * (3 * chunks) + [r...  9.55 us
    unnamed x21, local copies, waits for them, and re-layouts  3.91 us
    pallas_call x2, Pallas kernels, halves(): pl.pallas_call(kernel, in_specs=[pl.BlockSpec(memory_space=pltpu.HBM)] *...  3.39 us
  transfers between devices with their start and end apart: 24, of which 11 were waited for; matrix products, arithmetic and copies ran while one was open for 37% of the time, Pallas kernels for 9%

profile of v3, /device:TPU:0, one launch (start us, length us, event | category | flops | bytes accessed | tf_op | source)
XLA Modules:
  0.0 113.4 jit_solution(15731734477962153521)
XLA Ops:
  0.6 2.3 %shard_map.118 = (bf16[64,3200]{1,0:T(8,128)(2,1)}, bf16[64,3200]{1,0:T(8,128)(2,1)}) custom-call(bf16[128,3072]{1,0:T(8,128)(2,1)} %refs_0_.1, s32[2,128]{1,0:T(2,128)} %bitcast.67, f32[2,128]{1,0:T(2,128)} %bitcast.66), custom_call_target="tpu_custom_call" | custom-call | tf_op jit(solution)/shard_map/pallas_call | solution.py:132
  3.0 3.0 %collective-permute-start = (bf16[64,3200]{1,0:T(8,128)(2,1)}, bf16[64,3200]{1,0:T(8,128)(2,1)S(1)}, u32[]{:S(2)}, u32[]{:S(2)}) collective-permute-start(bf16[64,3200]{1,0:T(8,128)(2,1)} %get-tuple-element.63), channel_id=1, source_target_pairs={{0,8},{1,17},{2,10},{3,19},{4,12},{5,21},{6,14},{7,23},{8,0},{9,25... | collective-permute-start | bytes 1228808 | tf_op jit(solution)/shard_map/ppermute | solution.py:33
  6.0 1.1 copy-done.1
  7.1 1.1 shard_map.119
  8.3 3.8 %collective-permute-done = bf16[64,3200]{1,0:T(8,128)(2,1)S(1)} collective-permute-done((bf16[64,3200]{1,0:T(8,128)(2,1)}, bf16[64,3200]{1,0:T(8,128)(2,1)S(1)}, u32[]{:S(2)}, u32[]{:S(2)}) %collective-permute-start) | collective-permute-done | bytes 409632 | tf_op jit(solution)/shard_map/ppermute | solution.py:33
  12.2 2.1 %collective-permute-start.3 = (bf16[128,3200]{1,0:T(8,128)(2,1)S(1)}, bf16[128,3200]{1,0:T(8,128)(2,1)S(1)}, u32[]{:S(2)}, u32[]{:S(2)}) collective-permute-start(bf16[128,3200]{1,0:T(8,128)(2,1)S(1)} %pad_maximum_fusion.4), channel_id=1, source_target_pairs={{0,16},{1,9},{2,18},{3,11},{4,20},{5,13},{6,22},{7,15},{8,24},{9,1... | collective-permute-start | bytes 2457608 | tf_op jit(solution)/shard_map/ppermute | solution.py:33
  14.3 0.1 pad_maximum_fusion.1
  14.4 0.2 slice.92
  14.6 2.5 %copy-done = bf16[1,3072,1024]{2,1,0:T(8,128)(2,1)S(1)} copy-done((bf16[1,3072,1024]{2,1,0:T(8,128)(2,1)S(1)}, bf16[1,3072,1024]{2,1,0:T(8,128)(2,1)}, u32[]{:S(2)}) %copy-start) | copy-done | bytes 6291480
  17.1 1.8 %fusion.54 = f32[256,1024]{1,0:T(8,128)S(1)} fusion(bf16[1,3072,1024]{2,1,0:T(8,128)(2,1)S(1)} %copy-done, bf16[256,3200]{1,0:T(8,128)(2,1)S(1)} %pad_maximum_fusion.1), kind=kOutput, calls=%fused_computation.91 | convolution fusion | flops 1610612736 | bytes 8912896 | tf_op jit(solution)/shard_map/dot_general | solution.py:243
  18.9 0.2 slice-done.1
  19.1 2.1 %multiply_convert_fusion.8 = (bf16[256,1024]{1,0:T(8,128)(2,1)S(1)}, bf16[256,1024]{1,0:T(8,128)(2,1)S(1)}, bf16[256,1024]{1,0:T(8,128)(2,1)S(1)}, bf16[256,1024]{1,0:T(8,128)(2,1)S(1)}) fusion(f32[256,1024]{1,0:T(8,128)S(1)} %fusion.54, bf16[256,3072]{1,0:T(8,128)(2,1)S(1)} %slice.92, bf16[1,3072,1024]{2,1,0:T(8,128)(2,1)S(1)} %bitcast.63), kind=kOutput, calls=%fused_computation.47 | convolution fusion | flops 1614282752 | bytes 11010048 | tf_op jit(solution)/shard_map/dot_general | solution.py:243
  21.2 0.3 collective-permute-start.5
  21.5 1.6 %collective-permute-start.9 = (bf16[128,3072]{1,0:T(8,128)(2,1)S(1)}, bf16[128,3072]{1,0:T(8,128)(2,1)S(1)}, u32[]{:S(2)}, u32[]{:S(2)}) collective-permute-start(bf16[128,3072]{1,0:T(8,128)(2,1)S(1)} %pad_maximum_fusion.5), channel_id=1, source_target_pairs={{0,16},{1,9},{2,18},{3,11},{4,20},{5,13},{6,22},{7,15},{8,24},{9,1... | collective-permute-start | bytes 2359304 | tf_op jit(solution)/shard_map/ppermute | solution.py:33
  23.1 0.1 select_reduce_fusion.1
  23.3 1.4 %collective-permute-done.3 = bf16[128,3200]{1,0:T(8,128)(2,1)S(1)} collective-permute-done((bf16[128,3200]{1,0:T(8,128)(2,1)S(1)}, bf16[128,3200]{1,0:T(8,128)(2,1)S(1)}, u32[]{:S(2)}, u32[]{:S(2)}) %collective-permute-start.3) | collective-permute-done | bytes 819232 | tf_op jit(solution)/shard_map/ppermute | solution.py:33
  24.6 0.3 collective-permute-start.4
  24.9 4.7 %multiply_convert_fusion.6 = (bf16[256,1024]{1,0:T(8,128)(2,1)S(1)}, bf16[256,1024]{1,0:T(8,128)(2,1)S(1)}) fusion(bf16[256,1024]{1,0:T(8,128)(2,1)S(1)} %get-tuple-element.72, bf16[256,1024]{1,0:T(8,128)(2,1)S(1)} %get-tuple-element.71, f32[256]{0:T(256)S(1)} %select_reduce_fusion.1, bf16[1,1024,3072]{2,1,0:T(8,128)(2,1)} %param.13, ...), kind=kOutput, calls=%fused_computation.45 | convolution fusion | flops 1618739200 | bytes 9962496 | tf_op jit(solution)/shard_map/dot_general | solution.py:243
  29.6 0.1 pad_maximum_fusion.3
  29.8 0.1 pad_maximum_fusion.2
  29.9 0.2 slice.71
  30.1 1.8 %fusion.52 = f32[256,1024]{1,0:T(8,128)S(1)} fusion(bf16[1,3072,1024]{2,1,0:T(8,128)(2,1)S(1)} %copy-done, bf16[256,3200]{1,0:T(8,128)(2,1)S(1)} %pad_maximum_fusion.2), kind=kOutput, calls=%fused_computation.89 | convolution fusion | flops 1610612736 | bytes 8912896 | tf_op jit(solution)/shard_map/dot_general | solution.py:243
  31.9 2.1 %multiply_convert_fusion.4 = (bf16[256,1024]{1,0:T(8,128)(2,1)S(1)}, bf16[256,1024]{1,0:T(8,128)(2,1)S(1)}, bf16[256,1024]{1,0:T(8,128)(2,1)S(1)}, bf16[256,1024]{1,0:T(8,128)(2,1)S(1)}) fusion(f32[256,1024]{1,0:T(8,128)S(1)} %fusion.52, bf16[256,3072]{1,0:T(8,128)(2,1)S(1)} %slice.71, bf16[1,3072,1024]{2,1,0:T(8,128)(2,1)S(1)} %bitcast.63), kind=kOutput, calls=%fused_computation.41 | convolution fusion | flops 1614282752 | bytes 11010048 | tf_op jit(solution)/shard_map/dot_general | solution.py:243
  34.0 0.1 select_reduce_fusion
  34.1 0.3 collective-permute-start.10
  34.4 1.9 %fusion.17 = bf16[256,3072]{1,0:T(8,128)(2,1)S(1)} fusion(bf16[256,1024]{1,0:T(8,128)(2,1)S(1)} %get-tuple-element.100, bf16[1,1024,3072]{2,1,0:T(8,128)(2,1)S(1)} %bitcast.74, f32[256]{0:T(256)S(1)} %select_reduce_fusion), kind=kOutput, calls=%fused_computation.14 | convolution fusion | flops 1612185600 | bytes 8389632 | tf_op jit(solution)/shard_map/dot_general | solution.py:243
  36.4 0.4 collective-permute-start.7
  36.7 2.0 %fusion.14 = bf16[256,3072]{1,0:T(8,128)(2,1)S(1)} fusion(bf16[256,1024]{1,0:T(8,128)(2,1)S(1)} %get-tuple-element.99, bf16[1,1024,3072]{2,1,0:T(8,128)(2,1)S(1)} %bitcast.74, f32[256]{0:T(256)S(1)} %select_reduce_fusion.1), kind=kOutput, calls=%fused_computation.13 | convolution fusion | flops 1612185600 | bytes 8389632 | tf_op jit(solution)/shard_map/dot_general | solution.py:243
  38.8 0.1 fusion.58
  39.0 0.3 collective-permute-start.6
  39.2 0.2 add_convert_fusion.3
  39.4 2.2 %collective-permute-start.8 = (bf16[128,3072]{1,0:T(8,128)(2,1)S(1)}, bf16[128,3072]{1,0:T(8,128)(2,1)S(1)}, u32[]{:S(2)}, u32[]{:S(2)}) collective-permute-start(bf16[128,3072]{1,0:T(8,128)(2,1)S(1)} %add_convert_fusion.3), channel_id=1, source_target_pairs={{0,16},{1,9},{2,18},{3,11},{4,20},{5,13},{6,22},{7,15},{8,24},{9,1... | collective-permute-start | bytes 2359304 | tf_op jit(solution)/shard_map/ppermute | solution.py:33
  41.7 4.7 %multiply_convert_fusion.2 = (bf16[256,1024]{1,0:T(8,128)(2,1)S(1)}, bf16[256,1024]{1,0:T(8,128)(2,1)S(1)}) fusion(bf16[256,1024]{1,0:T(8,128)(2,1)S(1)} %get-tuple-element.86, bf16[256,1024]{1,0:T(8,128)(2,1)S(1)} %get-tuple-element.85, f32[256]{0:T(256)S(1)} %select_reduce_fusion, bf16[256,3072]{1,0:T(8,128)(2,1)S(1)} %constant_dynamic-update-slice_fusion, ...), kind=kOutput, calls=%fused_computation.39 | convolution fusion | flops 1612447744 | bytes 9962496 | tf_op jit(solution)/shard_map/dot_general | solution.py:243
  46.4 4.8 %shard_map.120 = (bf16[128,3200]{1,0:T(8,128)(2,1)S(1)}, bf16[128,3200]{1,0:T(8,128)(2,1)S(1)}) custom-call(bf16[256,1024]{1,0:T(8,128)(2,1)S(1)} %get-tuple-element.108.refs_0_, bf16[256,1024]{1,0:T(8,128)(2,1)S(1)} %get-tuple-element.114.refs_1_, bf16[256,1024]{1,0:T(8,128)(2,1)S(1)} %get-tuple-element.89.refs_2_, bf16[3072,1024]{1,0:T(8,128)(2,1)S(1)} %bitcast.60, ...), custom_call_target="tpu_custom_call" | custom-call | tf_op jit(solution)/shard_map/pallas_call | solution.py:319
  51.2 0.2 collective-permute-start.12
  51.5 0.2 collective-permute-done.8
  51.6 0.4 add_convert_fusion.2
  52.0 2.1 %collective-permute-start.11 = (bf16[64,3072]{1,0:T(8,128)(2,1)S(1)}, bf16[64,3072]{1,0:T(8,128)(2,1)S(1)}, u32[]{:S(2)}, u32[]{:S(2)}) collective-permute-start(bf16[64,3072]{1,0:T(8,128)(2,1)S(1)} %slice.99), channel_id=1, source_target_pairs={{0,8},{1,17},{2,10},{3,19},{4,12},{5,21},{6,14},{7,23},{8,0},{9,25... | collective-permute-start | bytes 1179656 | tf_op jit(solution)/shard_map/ppermute | solution.py:33
  54.1 4.8 %shard_map.121 = (bf16[128,3200]{1,0:T(8,128)(2,1)S(1)}, bf16[128,3200]{1,0:T(8,128)(2,1)S(1)}) custom-call(bf16[256,1024]{1,0:T(8,128)(2,1)S(1)} %get-tuple-element.107.refs_0_, bf16[256,1024]{1,0:T(8,128)(2,1)S(1)} %get-tuple-element.113.refs_1_, bf16[256,1024]{1,0:T(8,128)(2,1)S(1)} %get-tuple-element.95.refs_2_, bf16[3072,1024]{1,0:T(8,128)(2,1)S(1)} %bitcast.61, ...), custom_call_target="tpu_custom_call" | custom-call | tf_op jit(solution)/shard_map/pallas_call | solution.py:319
  59.0 0.2 add_convert_fusion.1
  59.1 1.6 %collective-permute-start.15 = (bf16[128,3200]{1,0:T(8,128)(2,1)S(1)}, bf16[128,3200]{1,0:T(8,128)(2,1)S(1)}, u32[]{:S(2)}, u32[]{:S(2)}) collective-permute-start(bf16[128,3200]{1,0:T(8,128)(2,1)S(1)} %add_convert_fusion.1), channel_id=1, source_target_pairs={{0,16},{1,9},{2,18},{3,11},{4,20},{5,13},{6,22},{7,15},{8,24},{9,1... | collective-permute-start | bytes 2457608 | tf_op jit(solution)/shard_map/ppermute | solution.py:33
  60.7 5.6 %convolution_convert_fusion.2 = bf16[1024,3072]{1,0:T(8,128)(2,1)} fusion(bf16[256,3072]{1,0:T(8,128)(2,1)S(1)} %constant_dynamic-update-slice_fusion, bf16[256,3072]{1,0:T(8,128)(2,1)S(1)} %pad_maximum_fusion.3, bf16[256,1024]{1,0:T(8,128)(2,1)S(1)} %get-tuple-element.100, bf16[256,1024]{1,0:T(8,128)(2,1)S(1)} %get-tuple-element.99, f32[512]{0:T(512)S(1)} %bitcast.72), kind=kOutput, calls=%fused_computation.10 | convolution fusion | flops 3233808384 | bytes 10487808 | tf_op jit(solution)/shard_map/dot_general | solution.py:243
  66.4 1.6 %collective-permute-start.13 = (bf16[32,3072]{1,0:T(8,128)(2,1)S(1)}, bf16[32,3072]{1,0:T(8,128)(2,1)S(1)}, u32[]{:S(2)}, u32[]{:S(2)}) collective-permute-start(bf16[32,3072]{1,0:T(8,128)(2,1)S(1)} %slice.101), channel_id=1, source_target_pairs={{0,2},{1,3},{2,0},{3,1},{4,6},{5,7},{6,4},{7,5},{8,10},{9,11},{10,... | collective-permute-start | bytes 589832 | tf_op jit(solution)/shard_map/ppermute | solution.py:33
  68.1 3.5 %collective-permute-done.15 = bf16[128,3200]{1,0:T(8,128)(2,1)S(1)} collective-permute-done((bf16[128,3200]{1,0:T(8,128)(2,1)S(1)}, bf16[128,3200]{1,0:T(8,128)(2,1)S(1)}, u32[]{:S(2)}, u32[]{:S(2)}) %collective-permute-start.15) | collective-permute-done | bytes 819232 | tf_op jit(solution)/shard_map/ppermute | solution.py:33
  71.6 0.3 add_convert_fusion
  71.9 0.9 collective-permute-start.16
  72.8 0.4 pad_maximum_fusion
  73.2 5.5 %convolution_convert_fusion.1 = bf16[3072,1024]{1,0:T(8,128)(2,1)} fusion(bf16[512,3072]{1,0:T(8,128)(2,1)S(1)} %pad_maximum_fusion, bf16[256,1024]{1,0:T(8,128)(2,1)S(1)} %get-tuple-element.108.refs_0_, bf16[256,1024]{1,0:T(8,128)(2,1)S(1)} %get-tuple-element.107.refs_0_), kind=kOutput, calls=%fused_computation.9 | convolution fusion | flops 3226468352 | bytes 10485760 | tf_op jit(solution)/shard_map/dot_general | solution.py:243
  78.7 1.2 %collective-permute-done.16 = bf16[64,3200]{1,0:T(8,128)(2,1)S(1)} collective-permute-done((bf16[64,3200]{1,0:T(8,128)(2,1)S(1)}, bf16[64,3200]{1,0:T(8,128)(2,1)S(1)}, u32[]{:S(2)}, u32[]{:S(2)}) %collective-permute-start.16) | collective-permute-done | bytes 409632 | tf_op jit(solution)/shard_map/ppermute | solution.py:33
  80.0 1.6 %collective-permute-start.18 = (bf16[32,3200]{1,0:T(8,128)(2,1)S(1)}, bf16[32,3200]{1,0:T(8,128)(2,1)S(1)}, u32[]{:S(2)}, u32[]{:S(2)}) collective-permute-start(bf16[32,3200]{1,0:T(8,128)(2,1)S(1)} %slice.105), channel_id=1, source_target_pairs={{0,2},{1,3},{2,0},{3,1},{4,6},{5,7},{6,4},{7,5},{8,10},{9,11},{10,... | collective-permute-start | bytes 614408 | tf_op jit(solution)/shard_map/ppermute | solution.py:33
  81.7 2.7 %collective-permute-start.17 = (bf16[32,3072]{1,0:T(8,128)(2,1)S(1)}, bf16[32,3072]{1,0:T(8,128)(2,1)S(1)}, u32[]{:S(2)}, u32[]{:S(2)}) collective-permute-start(bf16[32,3072]{1,0:T(8,128)(2,1)S(1)} %add_convert_fusion.9), channel_id=1, source_target_pairs={{0,4},{1,5},{2,6},{3,7},{4,0},{5,1},{6,2},{7,3},{8,12},{9,13},{10,... | collective-permute-start | bytes 589832 | tf_op jit(solution)/shard_map/ppermute | solution.py:33
  84.4 5.3 %collective-permute-done.18 = bf16[32,3200]{1,0:T(8,128)(2,1)S(1)} collective-permute-done((bf16[32,3200]{1,0:T(8,128)(2,1)S(1)}, bf16[32,3200]{1,0:T(8,128)(2,1)S(1)}, u32[]{:S(2)}, u32[]{:S(2)}) %collective-permute-start.18) | collective-permute-done | bytes 204832 | tf_op jit(solution)/shard_map/ppermute | solution.py:33
  89.8 0.9 collective-permute-start.20
  90.7 5.5 %convolution_convert_fusion = bf16[3072,1024]{1,0:T(8,128)(2,1)} fusion(bf16[512,3072]{1,0:T(8,128)(2,1)S(1)} %pad_maximum_fusion, bf16[256,1024]{1,0:T(8,128)(2,1)S(1)} %get-tuple-element.114.refs_1_, bf16[256,1024]{1,0:T(8,128)(2,1)S(1)} %get-tuple-element.113.refs_1_), kind=kOutput, calls=%fused_computation.8 | convolution fusion | flops 3226468352 | bytes 10485760 | tf_op jit(solution)/shard_map/dot_general | solution.py:243
  96.2 0.9 collective-permute-done.17
  97.1 1.7 %collective-permute-start.19 = (bf16[32,3072]{1,0:T(8,128)(2,1)S(1)}, bf16[32,3072]{1,0:T(8,128)(2,1)S(1)}, u32[]{:S(2)}, u32[]{:S(2)}) collective-permute-start(bf16[32,3072]{1,0:T(8,128)(2,1)S(1)} %add_convert_fusion.8), channel_id=1, source_target_pairs={{0,2},{1,3},{2,0},{3,1},{4,6},{5,7},{6,4},{7,5},{8,10},{9,11},{10,... | collective-permute-start | bytes 589832 | tf_op jit(solution)/shard_map/ppermute | solution.py:33
  98.8 2.4 %collective-permute-done.20 = bf16[32,3200]{1,0:T(8,128)(2,1)S(1)} collective-permute-done((bf16[32,3200]{1,0:T(8,128)(2,1)S(1)}, bf16[32,3200]{1,0:T(8,128)(2,1)S(1)}, u32[]{:S(2)}, u32[]{:S(2)}) %collective-permute-start.20) | collective-permute-done | bytes 204832 | tf_op jit(solution)/shard_map/ppermute | solution.py:33
  101.3 4.1 %collective-permute-done.19 = bf16[32,3072]{1,0:T(8,128)(2,1)S(1)} collective-permute-done((bf16[32,3072]{1,0:T(8,128)(2,1)S(1)}, bf16[32,3072]{1,0:T(8,128)(2,1)S(1)}, u32[]{:S(2)}, u32[]{:S(2)}) %collective-permute-start.19) | collective-permute-done | bytes 196640 | tf_op jit(solution)/shard_map/ppermute | solution.py:33
  105.5 4.1 %collective-permute-done.22 = bf16[32,3200]{1,0:T(8,128)(2,1)S(1)} collective-permute-done((bf16[32,3200]{1,0:T(8,128)(2,1)S(1)}, bf16[32,3200]{1,0:T(8,128)(2,1)S(1)}, u32[]{:S(2)}, u32[]{:S(2)}) %collective-permute-start.22) | collective-permute-done | bytes 204832 | tf_op jit(solution)/shard_map/ppermute | solution.py:33
  109.9 1.0 maximum_select_fusion
  111.0 0.6 collective-permute-done.23
  111.6 0.2 fusion.43
  111.8 0.6 maximum_divide_fusion
  112.4 1.0 maximum_select_fusion.1
  (62 shorter events, 1.5 us)
Async XLA Ops:
  3.0 9.1 %collective-permute-start = (bf16[64,3200]{1,0:T(8,128)(2,1)}, bf16[64,3200]{1,0:T(8,128)(2,1)S(1)}, u32[]{:S(2)}, u32[]{:S(2)}) collective-permute-start(bf16[64,3200]{1,0:T(8,128)(2,1)} %get-tuple-element.63), channel_id=1, source_target_pairs={{0,8},{1,17},{2,10},{3,19},{4,12},{5,21},{6,14},{7,23},{8,0},{9,25... | collective-permute-start | bytes 1228808 | tf_op jit(solution)/shard_map/ppermute | solution.py:33
  6.0 1.1 copy-start.1
  7.1 5.0 %copy-start.2 = (bf16[64,3200]{1,0:T(8,128)(2,1)S(1)}, bf16[64,3200]{1,0:T(8,128)(2,1)}, u32[]{:S(2)}) copy-start(bf16[64,3200]{1,0:T(8,128)(2,1)} %get-tuple-element.63) | copy-start | bytes 1228804
  7.1 7.2 %copy-start.3 = (bf16[64,3200]{1,0:T(8,128)(2,1)S(1)}, bf16[64,3200]{1,0:T(8,128)(2,1)}, u32[]{:S(2)}) copy-start(bf16[64,3200]{1,0:T(8,128)(2,1)} %get-tuple-element.64) | copy-start | bytes 1228804
  8.2 10.7 %collective-permute-start.2 = (bf16[64,3072]{1,0:T(8,128)(2,1)S(1)}, bf16[64,3072]{1,0:T(8,128)(2,1)S(1)}, u32[]{:S(2)}, u32[]{:S(2)}) collective-permute-start(bf16[64,3072]{1,0:T(8,128)(2,1)S(1)} %get-tuple-element.66), channel_id=1, source_target_pairs={{0,8},{1,17},{2,10},{3,19},{4,12},{5,21},{6,14},{7,23},{8,0},{9,25... | collective-permute-start | bytes 1179656 | tf_op jit(solution)/shard_map/ppermute | solution.py:33
  12.1 2.2 %collective-permute-start.1 = (bf16[64,3200]{1,0:T(8,128)(2,1)S(1)}, bf16[64,3200]{1,0:T(8,128)(2,1)S(1)}, u32[]{:S(2)}, u32[]{:S(2)}) collective-permute-start(bf16[64,3200]{1,0:T(8,128)(2,1)S(1)} %collective-permute-done), channel_id=1, source_target_pairs={{0,1},{1,0},{2,3},{3,2},{4,5},{5,4},{6,7},{7,6},{8,9},{9,8},{10,11... | collective-permute-start | bytes 1228808 | tf_op jit(solution)/shard_map/ppermute | solution.py:33
  12.2 12.4 %collective-permute-start.3 = (bf16[128,3200]{1,0:T(8,128)(2,1)S(1)}, bf16[128,3200]{1,0:T(8,128)(2,1)S(1)}, u32[]{:S(2)}, u32[]{:S(2)}) collective-permute-start(bf16[128,3200]{1,0:T(8,128)(2,1)S(1)} %pad_maximum_fusion.4), channel_id=1, source_target_pairs={{0,16},{1,9},{2,18},{3,11},{4,20},{5,13},{6,22},{7,15},{8,24},{9,1... | collective-permute-start | bytes 2457608 | tf_op jit(solution)/shard_map/ppermute | solution.py:33
  14.3 2.8 %copy-start = (bf16[1,3072,1024]{2,1,0:T(8,128)(2,1)S(1)}, bf16[1,3072,1024]{2,1,0:T(8,128)(2,1)}, u32[]{:S(2)}) copy-start(bf16[1,3072,1024]{2,1,0:T(8,128)(2,1)} %param.11) | copy-start | bytes 18874372
  14.4 4.5 %slice-start = ((s8[6291456]{0:T(1024)(128)(4,1)}), s8[4194304]{0:T(1024)(128)(4,1)S(1)}, s32[]{:S(2)}) async-start(s8[6291456]{0:T(1024)(128)(4,1)} %bitcast.62), calls=%async_computation | async-start | bytes 8388608
  17.1 2.0 %slice-start.1 = ((s8[6291456]{0:T(1024)(128)(4,1)}), s8[2097152]{0:T(1024)(128)(4,1)S(1)}, s32[]{:S(2)}) async-start(s8[6291456]{0:T(1024)(128)(4,1)} %bitcast.62), calls=%async_computation.1 | async-start | bytes 4194304
  21.2 2.0 %collective-permute-start.5 = (bf16[64,3072]{1,0:T(8,128)(2,1)S(1)}, bf16[64,3072]{1,0:T(8,128)(2,1)S(1)}, u32[]{:S(2)}, u32[]{:S(2)}) collective-permute-start(bf16[64,3072]{1,0:T(8,128)(2,1)S(1)} %collective-permute-done.2), channel_id=1, source_target_pairs={{0,1},{1,0},{2,3},{3,2},{4,5},{5,4},{6,7},{7,6},{8,9},{9,8},{10,11... | collective-permute-start | bytes 1179656 | tf_op jit(solution)/shard_map/ppermute | solution.py:33
  21.5 12.6 %collective-permute-start.9 = (bf16[128,3072]{1,0:T(8,128)(2,1)S(1)}, bf16[128,3072]{1,0:T(8,128)(2,1)S(1)}, u32[]{:S(2)}, u32[]{:S(2)}) collective-permute-start(bf16[128,3072]{1,0:T(8,128)(2,1)S(1)} %pad_maximum_fusion.5), channel_id=1, source_target_pairs={{0,16},{1,9},{2,18},{3,11},{4,20},{5,13},{6,22},{7,15},{8,24},{9,1... | collective-permute-start | bytes 2359304 | tf_op jit(solution)/shard_map/ppermute | solution.py:33
  24.6 5.1 %collective-permute-start.4 = (bf16[128,3200]{1,0:T(8,128)(2,1)S(1)}, bf16[128,3200]{1,0:T(8,128)(2,1)S(1)}, u32[]{:S(2)}, u32[]{:S(2)}) collective-permute-start(bf16[128,3200]{1,0:T(8,128)(2,1)S(1)} %collective-permute-done.3), channel_id=1, source_target_pairs={{0,1},{1,0},{2,3},{3,2},{4,5},{5,4},{6,7},{7,6},{8,9},{9,8},{10,11... | collective-permute-start | bytes 2457608 | tf_op jit(solution)/shard_map/ppermute | solution.py:33
  30.1 4.3 %slice-start.2 = ((s8[6291456]{0:T(1024)(128)(4,1)}), s8[4194304]{0:T(1024)(128)(4,1)S(1)}, s32[]{:S(2)}) async-start(s8[6291456]{0:T(1024)(128)(4,1)} %bitcast.73), calls=%async_computation.2 | async-start | bytes 8388608
  31.9 2.5 %slice-start.3 = ((s8[6291456]{0:T(1024)(128)(4,1)}), s8[2097152]{0:T(1024)(128)(4,1)S(1)}, s32[]{:S(2)}) async-start(s8[6291456]{0:T(1024)(128)(4,1)} %bitcast.73), calls=%async_computation.3 | async-start | bytes 4194304
  34.1 7.6 %collective-permute-start.10 = (bf16[128,3072]{1,0:T(8,128)(2,1)S(1)}, bf16[128,3072]{1,0:T(8,128)(2,1)S(1)}, u32[]{:S(2)}, u32[]{:S(2)}) collective-permute-start(bf16[128,3072]{1,0:T(8,128)(2,1)S(1)} %collective-permute-done.9), channel_id=1, source_target_pairs={{0,1},{1,0},{2,3},{3,2},{4,5},{5,4},{6,7},{7,6},{8,9},{9,8},{10,11... | collective-permute-start | bytes 2359304 | tf_op jit(solution)/shard_map/ppermute | solution.py:33
  36.4 2.9 %collective-permute-start.7 = (bf16[128,3072]{1,0:T(8,128)(2,1)S(1)}, bf16[128,3072]{1,0:T(8,128)(2,1)S(1)}, u32[]{:S(2)}, u32[]{:S(2)}) collective-permute-start(bf16[128,3072]{1,0:T(8,128)(2,1)S(1)} %get-tuple-element.78), channel_id=1, source_target_pairs={{0,1},{1,0},{2,3},{3,2},{4,5},{5,4},{6,7},{7,6},{8,9},{9,8},{10,11... | collective-permute-start | bytes 2359304 | tf_op jit(solution)/shard_map/ppermute | solution.py:33
  39.0 12.7 %collective-permute-start.6 = (bf16[128,3072]{1,0:T(8,128)(2,1)S(1)}, bf16[128,3072]{1,0:T(8,128)(2,1)S(1)}, u32[]{:S(2)}, u32[]{:S(2)}) collective-permute-start(bf16[128,3072]{1,0:T(8,128)(2,1)S(1)} %get-tuple-element.81), channel_id=1, source_target_pairs={{0,1},{1,0},{2,3},{3,2},{4,5},{5,4},{6,7},{7,6},{8,9},{9,8},{10,11... | collective-permute-start | bytes 2359304 | tf_op jit(solution)/shard_map/ppermute | solution.py:33
  39.4 12.2 %collective-permute-start.8 = (bf16[128,3072]{1,0:T(8,128)(2,1)S(1)}, bf16[128,3072]{1,0:T(8,128)(2,1)S(1)}, u32[]{:S(2)}, u32[]{:S(2)}) collective-permute-start(bf16[128,3072]{1,0:T(8,128)(2,1)S(1)} %add_convert_fusion.3), channel_id=1, source_target_pairs={{0,16},{1,9},{2,18},{3,11},{4,20},{5,13},{6,22},{7,15},{8,24},{9,1... | collective-permute-start | bytes 2359304 | tf_op jit(solution)/shard_map/ppermute | solution.py:33
  51.2 7.7 %collective-permute-start.12 = (bf16[128,3200]{1,0:T(8,128)(2,1)S(1)}, bf16[128,3200]{1,0:T(8,128)(2,1)S(1)}, u32[]{:S(2)}, u32[]{:S(2)}) collective-permute-start(bf16[128,3200]{1,0:T(8,128)(2,1)S(1)} %get-tuple-element.91), channel_id=1, source_target_pairs={{0,1},{1,0},{2,3},{3,2},{4,5},{5,4},{6,7},{7,6},{8,9},{9,8},{10,11... | collective-permute-start | bytes 2457608 | tf_op jit(solution)/shard_map/ppermute | solution.py:33
  52.0 14.3 %collective-permute-start.11 = (bf16[64,3072]{1,0:T(8,128)(2,1)S(1)}, bf16[64,3072]{1,0:T(8,128)(2,1)S(1)}, u32[]{:S(2)}, u32[]{:S(2)}) collective-permute-start(bf16[64,3072]{1,0:T(8,128)(2,1)S(1)} %slice.99), channel_id=1, source_target_pairs={{0,8},{1,17},{2,10},{3,19},{4,12},{5,21},{6,14},{7,23},{8,0},{9,25... | collective-permute-start | bytes 1179656 | tf_op jit(solution)/shard_map/ppermute | solution.py:33
  58.9 12.7 %collective-permute-start.14 = (bf16[128,3200]{1,0:T(8,128)(2,1)S(1)}, bf16[128,3200]{1,0:T(8,128)(2,1)S(1)}, u32[]{:S(2)}, u32[]{:S(2)}) collective-permute-start(bf16[128,3200]{1,0:T(8,128)(2,1)S(1)} %get-tuple-element.97), channel_id=1, source_target_pairs={{0,1},{1,0},{2,3},{3,2},{4,5},{5,4},{6,7},{7,6},{8,9},{9,8},{10,11... | collective-permute-start | bytes 2457608 | tf_op jit(solution)/shard_map/ppermute | solution.py:33
  59.1 12.4 %collective-permute-start.15 = (bf16[128,3200]{1,0:T(8,128)(2,1)S(1)}, bf16[128,3200]{1,0:T(8,128)(2,1)S(1)}, u32[]{:S(2)}, u32[]{:S(2)}) collective-permute-start(bf16[128,3200]{1,0:T(8,128)(2,1)S(1)} %add_convert_fusion.1), channel_id=1, source_target_pairs={{0,16},{1,9},{2,18},{3,11},{4,20},{5,13},{6,22},{7,15},{8,24},{9,1... | collective-permute-start | bytes 2457608 | tf_op jit(solution)/shard_map/ppermute | solution.py:33
  66.4 15.2 %collective-permute-start.13 = (bf16[32,3072]{1,0:T(8,128)(2,1)S(1)}, bf16[32,3072]{1,0:T(8,128)(2,1)S(1)}, u32[]{:S(2)}, u32[]{:S(2)}) collective-permute-start(bf16[32,3072]{1,0:T(8,128)(2,1)S(1)} %slice.101), channel_id=1, source_target_pairs={{0,2},{1,3},{2,0},{3,1},{4,6},{5,7},{6,4},{7,5},{8,10},{9,11},{10,... | collective-permute-start | bytes 589832 | tf_op jit(solution)/shard_map/ppermute | solution.py:33
  71.9 8.0 %collective-permute-start.16 = (bf16[64,3200]{1,0:T(8,128)(2,1)S(1)}, bf16[64,3200]{1,0:T(8,128)(2,1)S(1)}, u32[]{:S(2)}, u32[]{:S(2)}) collective-permute-start(bf16[64,3200]{1,0:T(8,128)(2,1)S(1)} %slice.103), channel_id=1, source_target_pairs={{0,8},{1,17},{2,10},{3,19},{4,12},{5,21},{6,14},{7,23},{8,0},{9,25... | collective-permute-start | bytes 1228808 | tf_op jit(solution)/shard_map/ppermute | solution.py:33
  80.0 9.7 %collective-permute-start.18 = (bf16[32,3200]{1,0:T(8,128)(2,1)S(1)}, bf16[32,3200]{1,0:T(8,128)(2,1)S(1)}, u32[]{:S(2)}, u32[]{:S(2)}) collective-permute-start(bf16[32,3200]{1,0:T(8,128)(2,1)S(1)} %slice.105), channel_id=1, source_target_pairs={{0,2},{1,3},{2,0},{3,1},{4,6},{5,7},{6,4},{7,5},{8,10},{9,11},{10,... | collective-permute-start | bytes 614408 | tf_op jit(solution)/shard_map/ppermute | solution.py:33
  81.7 15.3 %collective-permute-start.17 = (bf16[32,3072]{1,0:T(8,128)(2,1)S(1)}, bf16[32,3072]{1,0:T(8,128)(2,1)S(1)}, u32[]{:S(2)}, u32[]{:S(2)}) collective-permute-start(bf16[32,3072]{1,0:T(8,128)(2,1)S(1)} %add_convert_fusion.9), channel_id=1, source_target_pairs={{0,4},{1,5},{2,6},{3,7},{4,0},{5,1},{6,2},{7,3},{8,12},{9,13},{10,... | collective-permute-start | bytes 589832 | tf_op jit(solution)/shard_map/ppermute | solution.py:33
  89.8 11.4 %collective-permute-start.20 = (bf16[32,3200]{1,0:T(8,128)(2,1)S(1)}, bf16[32,3200]{1,0:T(8,128)(2,1)S(1)}, u32[]{:S(2)}, u32[]{:S(2)}) collective-permute-start(bf16[32,3200]{1,0:T(8,128)(2,1)S(1)} %add_convert_fusion.7), channel_id=1, source_target_pairs={{0,4},{1,5},{2,6},{3,7},{4,0},{5,1},{6,2},{7,3},{8,12},{9,13},{10,... | collective-permute-start | bytes 614408 | tf_op jit(solution)/shard_map/ppermute | solution.py:33
  96.2 13.7 %copy-start.5 = (s32[128,2]{0,1:T(2,128)S(1)}, s32[128,2]{0,1:T(2,128)}, u32[]{:S(2)}) copy-start(s32[128,2]{0,1:T(2,128)} %param.8) | copy-start | bytes 3076
  97.1 8.3 %collective-permute-start.19 = (bf16[32,3072]{1,0:T(8,128)(2,1)S(1)}, bf16[32,3072]{1,0:T(8,128)(2,1)S(1)}, u32[]{:S(2)}, u32[]{:S(2)}) collective-permute-start(bf16[32,3072]{1,0:T(8,128)(2,1)S(1)} %add_convert_fusion.8), channel_id=1, source_target_pairs={{0,2},{1,3},{2,0},{3,1},{4,6},{5,7},{6,4},{7,5},{8,10},{9,11},{10,... | collective-permute-start | bytes 589832 | tf_op jit(solution)/shard_map/ppermute | solution.py:33
  101.2 8.4 %collective-permute-start.22 = (bf16[32,3200]{1,0:T(8,128)(2,1)S(1)}, bf16[32,3200]{1,0:T(8,128)(2,1)S(1)}, u32[]{:S(2)}, u32[]{:S(2)}) collective-permute-start(bf16[32,3200]{1,0:T(8,128)(2,1)S(1)} %add_convert_fusion.6), channel_id=1, source_target_pairs={{0,2},{1,3},{2,0},{3,1},{4,6},{5,7},{6,4},{7,5},{8,10},{9,11},{10,... | collective-permute-start | bytes 614408 | tf_op jit(solution)/shard_map/ppermute | solution.py:33
  105.5 6.3 %copy-start.4 = (f32[128,2]{0,1:T(2,128)S(1)}, f32[128,2]{0,1:T(2,128)}, u32[]{:S(2)}) copy-start(f32[128,2]{0,1:T(2,128)} %param.9) | copy-start | bytes 3076
  105.5 4.4 %collective-permute-start.21 = (bf16[64,3072]{1,0:T(8,128)(2,1)S(1)}, bf16[64,3072]{1,0:T(8,128)(2,1)S(1)}, u32[]{:S(2)}, u32[]{:S(2)}) collective-permute-start(bf16[64,3072]{1,0:T(8,128)(2,1)S(1)} %maximum_select_fusion.3), channel_id=1, source_target_pairs={{0,1},{1,0},{2,3},{3,2},{4,5},{5,4},{6,7},{7,6},{8,9},{9,8},{10,11... | collective-permute-start | bytes 1179656 | tf_op jit(solution)/shard_map/ppermute | solution.py:33
  109.8 1.8 %collective-permute-start.23 = (bf16[64,3200]{1,0:T(8,128)(2,1)S(1)}, bf16[64,3200]{1,0:T(8,128)(2,1)S(1)}, u32[]{:S(2)}, u32[]{:S(2)}) collective-permute-start(bf16[64,3200]{1,0:T(8,128)(2,1)S(1)} %maximum_select_fusion.2), channel_id=1, source_target_pairs={{0,1},{1,0},{2,3},{3,2},{4,5},{5,4},{6,7},{7,6},{8,9},{9,8},{10,11... | collective-permute-start | bytes 1228808 | tf_op jit(solution)/shard_map/ppermute | solution.py:33

commit v4 on v3

--- a/solution.py
+++ b/solution.py
@@ -217,8 +217,10 @@
         self.mine = add(self.mine, hold(self.came, *after))
         for bit in range(3, log2(self.links.shards)):
             self.mine = add(self.mine, self.links.to_shard(self.mine, bit))
-        self.came = self.links.to_shard(self.mine, 1)
         return self.mine
+
+    def send_half(self, *after):
+        self.came = self.links.to_shard(hold(self.mine, *after), 1)
 
     def join_half(self, *after):
         beside = hold(self.came, *after)
@@ -268,67 +270,44 @@
     return term[:middle], term[middle:]
 
 
-def back_terms(grads_gate, grads_up, pre_ups, gate, up):
-    rows, units, width = grads_gate[0].shape[0], gate.shape[1], gate.shape[0]
-    chunks = len(grads_gate)
+def back_terms(grad_gate, grad_up, pre_up, gate, up):
+    rows, units, width = grad_gate.shape[0], gate.shape[1], gate.shape[0]
     tile = tile_of(width, 512)
     tiles = width // tile
     middle = rows // 2
     nt = (((1,), (1,)), ((), ()))
 
-    def kernel(*refs):
-        grad_refs = refs[: 3 * chunks]
-        gate_ref, up_ref = refs[3 * chunks : 3 * chunks + 2]
-        outs = refs[3 * chunks + 2 : 3 * chunks + 2 + 2 * chunks]
-        gate_all, up_all = refs[-2:]
+    def kernel(gate_grad, up_grad, pre_ref, gate_ref, up_ref, keep_ref, send_ref):
         j = pl.program_id(0)
-
-        @pl.when(j == 0)
-        def _():
-            for k in range(chunks):
-                gate_all[k * rows : (k + 1) * rows, :] = grad_refs[k][...]
-                up_all[k * rows : (k + 1) * rows, :] = grad_refs[chunks + k][...]
-
-        term = lax.dot_general(gate_all[...], gate_ref[...], nt, preferred_element_type=F32)
-        term += lax.dot_general(up_all[...], up_ref[...], nt, preferred_element_type=F32)
+        term = lax.dot_general(gate_grad[...], gate_ref[...], nt, preferred_element_type=F32)
+        term += lax.dot_general(up_grad[...], up_ref[...], nt, preferred_element_type=F32)
         term = term.astype(BF)
         columns = pl.ds(pl.multiple_of(j * tile, LANES), tile)
-        for k in range(2 * chunks):
-            outs[k][:, columns] = term[k * middle : (k + 1) * middle]
+        keep_ref[:, columns] = term[:middle]
+        send_ref[:, columns] = term[middle:]
 
         @pl.when(j == tiles - 1)
         def _():
             lane = lax.broadcasted_iota(jnp.int32, (rows, LANES), 1)
-            for k in range(chunks):
-                prob = jnp.sum(
-                    grad_refs[chunks + k][...].astype(F32)
-                    * grad_refs[2 * chunks + k][...].astype(F32),
-                    axis=1,
-                    keepdims=True,
-                )
-                own = jnp.where(lane == lax.axis_index("expert"), prob, 0.0).astype(BF)
-                outs[2 * k][:, width:] = own[:middle]
-                outs[2 * k + 1][:, width:] = own[middle:]
-
-    operands = [*grads_gate, *grads_up, *pre_ups, gate, up]
-    size = sum(a.size * a.dtype.itemsize for a in operands)
-    size += 2 * chunks * middle * (width + LANES) * 2
+            prob = jnp.sum(
+                up_grad[...].astype(F32) * pre_ref[...].astype(F32), axis=1, keepdims=True
+            )
+            own = jnp.where(lane == lax.axis_index("expert"), prob, 0.0).astype(BF)
+            keep_ref[:, width:] = own[:middle]
+            send_ref[:, width:] = own[middle:]
+
     block = pl.BlockSpec((middle, width + LANES), lambda j: (0, 0))
     full = pl.BlockSpec((rows, units), lambda j: (0, 0))
     row = pl.BlockSpec((tile, units), lambda j: (j, 0))
-    outs = pl.pallas_call(
+    return pl.pallas_call(
         kernel,
         grid=(tiles,),
-        in_specs=[full] * (3 * chunks) + [row] * 2,
-        out_specs=[block] * (2 * chunks),
-        out_shape=[jax.ShapeDtypeStruct((middle, width + LANES), BF)] * (2 * chunks),
-        scratch_shapes=[pltpu.VMEM((chunks * rows, units), BF)] * 2,
+        in_specs=[full] * 3 + [row] * 2,
+        out_specs=[block] * 2,
+        out_shape=[jax.ShapeDtypeStruct((middle, width + LANES), BF)] * 2,
         compiler_params=pltpu.CompilerParams(vmem_limit_bytes=BACK_VMEM << 20),
-        cost_estimate=pl.CostEstimate(
-            flops=0, bytes_accessed=0, transcendentals=0
-        ),
-    )(*operands)
-    return [(outs[2 * k], outs[2 * k + 1]) for k in range(chunks)]
+        cost_estimate=pl.CostEstimate(flops=0, bytes_accessed=0, transcendentals=0),
+    )(grad_gate, grad_up, pre_up, gate, up)
 
 
 def per_device(tokens, assignment, route_weight, cotangent, w_gate, w_up, w_down):
@@ -364,26 +343,27 @@
     o_late = outs.join_second(*out1)
     c2 = c.second(hidden2)
     gate_grad2, up_grad2 = hidden_grads(hold(c2, o_late), down, slope2, silu2, weight2)
-    (back2,) = back_terms([gate_grad2], [up_grad2], [up2], gate, up)
+    back2 = back_terms(gate_grad2, up_grad2, up2, gate, up)
     backs.second(back2)
     o_held = outs.join_first(*back2)
-    (back1,) = back_terms([hold(gate_grad1, o_held)], [up_grad1], [up1], gate, up)
+    back1 = back_terms(hold(gate_grad1, o_held), up_grad1, up1, gate, up)
     backs.first(back1)
     b_late = backs.join_second(*back1)
-
     weight = jnp.concatenate([weight1, weight2], axis=0)
-    scaled = (joined([hidden1, hidden2], b_late).astype(F32) * weight).astype(BF)
-    grad_down = dot(scaled, joined([c1, c2], b_late), 0, 0).astype(BF)
-    o_sum = outs.join_expert(grad_down)
-    b_held = backs.join_first(o_sum)
+    o_sum = outs.join_expert(b_late)
+    scaled = (joined([hidden1, hidden2], o_sum).astype(F32) * weight).astype(BF)
+    grad_down = dot(scaled, joined([c1, c2], o_sum), 0, 0).astype(BF)
+    o_near = outs.join_near(grad_down)
+    b_held = backs.join_first(o_near)
     x_all = joined([x1, x2], b_held)[:, :width]
     grad_gate = dot(x_all, joined([gate_grad1, gate_grad2]), 0, 0).astype(BF)
     b_sum = backs.join_expert(grad_gate)
-    o_near = outs.join_near(b_sum)
-    b_near = backs.join_near(o_near)
+    o_far = outs.join_far(b_sum)
+    b_near = backs.join_near(o_far)
+    outs.send_half(b_near)
     grad_up = dot(hold(x_all, b_near), joined([up_grad1, up_grad2]), 0, 0).astype(BF)
-    o_far = outs.join_far(grad_up)
-    b_far = backs.join_far(o_far)
+    b_far = backs.join_far(grad_up)
+    backs.send_half()
     o_part = outs.join_half(b_far)
     backs.join_half(o_part)
     moe_out = outs.rows(slice(0, width), backs.part)

time: 114 us -> 106 us (0.930)
  waiting for transfers between devices: 27.5 us -> 17 us
  starting transfers between devices: 24.2 us -> 27 us
    ppermute x24, waiting for transfers between devices: 27.5 us -> 17 us  [swap(): return lax.ppermute(value, AXES, pairs)]
    ppermute x24, starting transfers between devices: 24.2 us -> 27 us  [swap(): return lax.ppermute(value, AXES, pairs)]
  transfers between devices with their start and end apart: 24 -> 24, of which waited for: 11 -> 10; matrix products, arithmetic and copies ran while one was open for 37% -> 40% of each run, Pallas kernels for 9% -> 10%
where the time goes in v4:
time: 106 us
  matrix products  37.5 us (35%)
  starting transfers between devices  27 us (25%)
  waiting for transfers between devices  17 us (16%)
  Pallas kernels  12.8 us (12%)
  other arithmetic  5.52 us (5%)
  local copies, waits for them, and re-layouts  4.7 us (4%)
  between operations  1.13 us (1%)
    dot_general x11, matrix products, dot(): lax.dot_general(left, right, (((left_dim,), (right_dim,)), ((), ())), pre...  37.5 us
    ppermute x24, starting transfers between devices, swap(): return lax.ppermute(value, AXES, pairs)  27 us
    ppermute x24, waiting for transfers between devices, swap(): return lax.ppermute(value, AXES, pairs)  17 us
    pallas_call x2, Pallas kernels, back_terms(): pl.pallas_call(kernel, grid=(tiles,), in_specs=[full] * 3 + [row] * 2, ou...  9.41 us
    unnamed x21, local copies, waits for them, and re-layouts  3.92 us
    pallas_call x2, Pallas kernels, halves(): pl.pallas_call(kernel, in_specs=[pl.BlockSpec(memory_space=pltpu.HBM)] *...  3.39 us
  transfers between devices with their start and end apart: 24, of which 10 were waited for; matrix products, arithmetic and copies ran while one was open for 40% of the time, Pallas kernels for 10%

profile of v4, /device:TPU:0, one launch (start us, length us, event | category | flops | bytes accessed | tf_op | source)
XLA Modules:
  0.0 105.7 jit_solution(5547282999281058577)
XLA Ops:
  0.6 2.3 %shard_map.118 = (bf16[64,3200]{1,0:T(8,128)(2,1)}, bf16[64,3200]{1,0:T(8,128)(2,1)}) custom-call(bf16[128,3072]{1,0:T(8,128)(2,1)} %refs_0_.1, s32[2,128]{1,0:T(2,128)} %bitcast.67, f32[2,128]{1,0:T(2,128)} %bitcast.66), custom_call_target="tpu_custom_call" | custom-call | tf_op jit(solution)/shard_map/pallas_call | solution.py:132
  3.0 3.0 %collective-permute-start = (bf16[64,3200]{1,0:T(8,128)(2,1)}, bf16[64,3200]{1,0:T(8,128)(2,1)S(1)}, u32[]{:S(2)}, u32[]{:S(2)}) collective-permute-start(bf16[64,3200]{1,0:T(8,128)(2,1)} %get-tuple-element.64), channel_id=1, source_target_pairs={{0,8},{1,17},{2,10},{3,19},{4,12},{5,21},{6,14},{7,23},{8,0},{9,25... | collective-permute-start | bytes 1228808 | tf_op jit(solution)/shard_map/ppermute | solution.py:33
  6.0 1.1 %copy-done.1 = bf16[128,3072]{1,0:T(8,128)(2,1)S(1)} copy-done((bf16[128,3072]{1,0:T(8,128)(2,1)S(1)}, bf16[128,3072]{1,0:T(8,128)(2,1)}, u32[]{:S(2)}) %copy-start.1) | copy-done | bytes 786456
  7.1 1.1 shard_map.119
  8.3 3.8 %collective-permute-done = bf16[64,3200]{1,0:T(8,128)(2,1)S(1)} collective-permute-done((bf16[64,3200]{1,0:T(8,128)(2,1)}, bf16[64,3200]{1,0:T(8,128)(2,1)S(1)}, u32[]{:S(2)}, u32[]{:S(2)}) %collective-permute-start) | collective-permute-done | bytes 409632 | tf_op jit(solution)/shard_map/ppermute | solution.py:33
  12.2 2.1 %collective-permute-start.3 = (bf16[128,3200]{1,0:T(8,128)(2,1)S(1)}, bf16[128,3200]{1,0:T(8,128)(2,1)S(1)}, u32[]{:S(2)}, u32[]{:S(2)}) collective-permute-start(bf16[128,3200]{1,0:T(8,128)(2,1)S(1)} %pad_maximum_fusion.4), channel_id=1, source_target_pairs={{0,16},{1,9},{2,18},{3,11},{4,20},{5,13},{6,22},{7,15},{8,24},{9,1... | collective-permute-start | bytes 2457608 | tf_op jit(solution)/shard_map/ppermute | solution.py:33
  14.3 0.1 pad_maximum_fusion.1
  14.4 0.2 slice.92
  14.6 2.5 %copy-done = bf16[1,3072,1024]{2,1,0:T(8,128)(2,1)S(1)} copy-done((bf16[1,3072,1024]{2,1,0:T(8,128)(2,1)S(1)}, bf16[1,3072,1024]{2,1,0:T(8,128)(2,1)}, u32[]{:S(2)}) %copy-start) | copy-done | bytes 6291480
  17.1 1.8 %fusion.54 = f32[256,1024]{1,0:T(8,128)S(1)} fusion(bf16[1,3072,1024]{2,1,0:T(8,128)(2,1)S(1)} %copy-done, bf16[256,3200]{1,0:T(8,128)(2,1)S(1)} %pad_maximum_fusion.1), kind=kOutput, calls=%fused_computation.91 | convolution fusion | flops 1610612736 | bytes 8912896 | tf_op jit(solution)/shard_map/dot_general | solution.py:245
  18.9 0.2 slice-done.1
  19.1 2.0 %multiply_convert_fusion.8 = (bf16[256,1024]{1,0:T(8,128)(2,1)S(1)}, bf16[256,1024]{1,0:T(8,128)(2,1)S(1)}, bf16[256,1024]{1,0:T(8,128)(2,1)S(1)}, bf16[256,1024]{1,0:T(8,128)(2,1)S(1)}) fusion(f32[256,1024]{1,0:T(8,128)S(1)} %fusion.54, bf16[256,3072]{1,0:T(8,128)(2,1)S(1)} %slice.92, bf16[1,3072,1024]{2,1,0:T(8,128)(2,1)S(1)} %bitcast.63), kind=kOutput, calls=%fused_computation.47 | convolution fusion | flops 1614282752 | bytes 11010048 | tf_op jit(solution)/shard_map/dot_general | solution.py:245
  21.2 0.3 collective-permute-start.5
  21.5 1.6 %collective-permute-start.9 = (bf16[128,3072]{1,0:T(8,128)(2,1)S(1)}, bf16[128,3072]{1,0:T(8,128)(2,1)S(1)}, u32[]{:S(2)}, u32[]{:S(2)}) collective-permute-start(bf16[128,3072]{1,0:T(8,128)(2,1)S(1)} %pad_maximum_fusion.5), channel_id=1, source_target_pairs={{0,16},{1,9},{2,18},{3,11},{4,20},{5,13},{6,22},{7,15},{8,24},{9,1... | collective-permute-start | bytes 2359304 | tf_op jit(solution)/shard_map/ppermute | solution.py:33
  23.1 0.1 select_reduce_fusion.1
  23.2 1.4 %collective-permute-done.3 = bf16[128,3200]{1,0:T(8,128)(2,1)S(1)} collective-permute-done((bf16[128,3200]{1,0:T(8,128)(2,1)S(1)}, bf16[128,3200]{1,0:T(8,128)(2,1)S(1)}, u32[]{:S(2)}, u32[]{:S(2)}) %collective-permute-start.3) | collective-permute-done | bytes 819232 | tf_op jit(solution)/shard_map/ppermute | solution.py:33
  24.6 0.3 collective-permute-start.4
  24.9 4.7 %multiply_convert_fusion.6 = (bf16[256,1024]{1,0:T(8,128)(2,1)S(1)}, bf16[256,1024]{1,0:T(8,128)(2,1)S(1)}) fusion(bf16[256,1024]{1,0:T(8,128)(2,1)S(1)} %get-tuple-element.73, bf16[256,1024]{1,0:T(8,128)(2,1)S(1)} %get-tuple-element.72, f32[256]{0:T(256)S(1)} %select_reduce_fusion.1, bf16[1,1024,3072]{2,1,0:T(8,128)(2,1)} %param.13, ...), kind=kOutput, calls=%fused_computation.45 | convolution fusion | flops 1618739200 | bytes 9962496 | tf_op jit(solution)/shard_map/dot_general | solution.py:245
  29.6 0.1 pad_maximum_fusion.3
  29.8 0.1 pad_maximum_fusion.2
  29.9 0.2 slice.71
  30.1 1.8 %fusion.52 = f32[256,1024]{1,0:T(8,128)S(1)} fusion(bf16[1,3072,1024]{2,1,0:T(8,128)(2,1)S(1)} %copy-done, bf16[256,3200]{1,0:T(8,128)(2,1)S(1)} %pad_maximum_fusion.2), kind=kOutput, calls=%fused_computation.89 | convolution fusion | flops 1610612736 | bytes 8912896 | tf_op jit(solution)/shard_map/dot_general | solution.py:245
  31.9 2.1 %multiply_convert_fusion.4 = (bf16[256,1024]{1,0:T(8,128)(2,1)S(1)}, bf16[256,1024]{1,0:T(8,128)(2,1)S(1)}, bf16[256,1024]{1,0:T(8,128)(2,1)S(1)}, bf16[256,1024]{1,0:T(8,128)(2,1)S(1)}) fusion(f32[256,1024]{1,0:T(8,128)S(1)} %fusion.52, bf16[256,3072]{1,0:T(8,128)(2,1)S(1)} %slice.71, bf16[1,3072,1024]{2,1,0:T(8,128)(2,1)S(1)} %bitcast.63), kind=kOutput, calls=%fused_computation.41 | convolution fusion | flops 1614282752 | bytes 11010048 | tf_op jit(solution)/shard_map/dot_general | solution.py:245
  34.0 0.1 select_reduce_fusion
  34.1 0.3 collective-permute-start.10
  34.4 1.9 %fusion.17 = bf16[256,3072]{1,0:T(8,128)(2,1)S(1)} fusion(bf16[256,1024]{1,0:T(8,128)(2,1)S(1)} %get-tuple-element.102, bf16[1,1024,3072]{2,1,0:T(8,128)(2,1)S(1)} %bitcast.74, f32[256]{0:T(256)S(1)} %select_reduce_fusion), kind=kOutput, calls=%fused_computation.14 | convolution fusion | flops 1612185600 | bytes 8389632 | tf_op jit(solution)/shard_map/dot_general | solution.py:245
  36.2 0.1 fusion.59
  36.4 0.4 collective-permute-start.7
  36.7 2.1 %fusion.14 = bf16[256,3072]{1,0:T(8,128)(2,1)S(1)} fusion(bf16[256,1024]{1,0:T(8,128)(2,1)S(1)} %get-tuple-element.101, bf16[1,1024,3072]{2,1,0:T(8,128)(2,1)S(1)} %bitcast.74, f32[256]{0:T(256)S(1)} %select_reduce_fusion.1), kind=kOutput, calls=%fused_computation.13 | convolution fusion | flops 1612185600 | bytes 8389632 | tf_op jit(solution)/shard_map/dot_general | solution.py:245
  38.8 0.1 fusion.58
  39.0 0.3 collective-permute-start.6
  39.2 0.2 add_convert_fusion.3
  39.4 2.2 %collective-permute-start.8 = (bf16[128,3072]{1,0:T(8,128)(2,1)S(1)}, bf16[128,3072]{1,0:T(8,128)(2,1)S(1)}, u32[]{:S(2)}, u32[]{:S(2)}) collective-permute-start(bf16[128,3072]{1,0:T(8,128)(2,1)S(1)} %add_convert_fusion.3), channel_id=1, source_target_pairs={{0,16},{1,9},{2,18},{3,11},{4,20},{5,13},{6,22},{7,15},{8,24},{9,1... | collective-permute-start | bytes 2359304 | tf_op jit(solution)/shard_map/ppermute | solution.py:33
  41.7 4.7 %multiply_convert_fusion.2 = (bf16[256,1024]{1,0:T(8,128)(2,1)S(1)}, bf16[256,1024]{1,0:T(8,128)(2,1)S(1)}) fusion(bf16[256,1024]{1,0:T(8,128)(2,1)S(1)} %get-tuple-element.87, bf16[256,1024]{1,0:T(8,128)(2,1)S(1)} %get-tuple-element.86, f32[256]{0:T(256)S(1)} %select_reduce_fusion, bf16[256,3072]{1,0:T(8,128)(2,1)S(1)} %constant_dynamic-update-slice_fusion, ...), kind=kOutput, calls=%fused_computation.39 | convolution fusion | flops 1612447744 | bytes 9962496 | tf_op jit(solution)/shard_map/dot_general | solution.py:245
  46.5 4.7 %shard_map.120 = (bf16[128,3200]{1,0:T(8,128)(2,1)S(1)}, bf16[128,3200]{1,0:T(8,128)(2,1)S(1)}) custom-call(bf16[256,1024]{1,0:T(8,128)(2,1)S(1)} %get-tuple-element.110.gate_grad, bf16[256,1024]{1,0:T(8,128)(2,1)S(1)} %get-tuple-element.117.up_grad, bf16[256,1024]{1,0:T(8,128)(2,1)S(1)} %get-tuple-element.90.pre_ref, bf16[3072,1024]{1,0:T(8,128)(2,1)S(1)} %bitcast.60, ...), custom_call_target="tpu_custom_call" | custom-call | tf_op jit(solution)/shard_map/pallas_call | solution.py:302
  51.2 0.2 collective-permute-start.12
  51.5 0.2 collective-permute-done.8
  51.7 0.4 add_convert_fusion.2
  52.1 2.1 %collective-permute-start.11 = (bf16[64,3072]{1,0:T(8,128)(2,1)S(1)}, bf16[64,3072]{1,0:T(8,128)(2,1)S(1)}, u32[]{:S(2)}, u32[]{:S(2)}) collective-permute-start(bf16[64,3072]{1,0:T(8,128)(2,1)S(1)} %slice.99), channel_id=1, source_target_pairs={{0,8},{1,17},{2,10},{3,19},{4,12},{5,21},{6,14},{7,23},{8,0},{9,25... | collective-permute-start | bytes 1179656 | tf_op jit(solution)/shard_map/ppermute | solution.py:33
  54.1 4.7 %shard_map.121 = (bf16[128,3200]{1,0:T(8,128)(2,1)S(1)}, bf16[128,3200]{1,0:T(8,128)(2,1)S(1)}) custom-call(bf16[256,1024]{1,0:T(8,128)(2,1)S(1)} %get-tuple-element.109.gate_grad, bf16[256,1024]{1,0:T(8,128)(2,1)S(1)} %get-tuple-element.116.up_grad, bf16[256,1024]{1,0:T(8,128)(2,1)S(1)} %get-tuple-element.96.pre_ref, bf16[3072,1024]{1,0:T(8,128)(2,1)S(1)} %bitcast.61, ...), custom_call_target="tpu_custom_call" | custom-call | tf_op jit(solution)/shard_map/pallas_call | solution.py:302
  58.9 0.2 add_convert_fusion.1
  59.2 1.6 %collective-permute-start.16 = (bf16[128,3200]{1,0:T(8,128)(2,1)S(1)}, bf16[128,3200]{1,0:T(8,128)(2,1)S(1)}, u32[]{:S(2)}, u32[]{:S(2)}) collective-permute-start(bf16[128,3200]{1,0:T(8,128)(2,1)S(1)} %add_convert_fusion.1), channel_id=1, source_target_pairs={{0,16},{1,9},{2,18},{3,11},{4,20},{5,13},{6,22},{7,15},{8,24},{9,1... | collective-permute-start | bytes 2457608 | tf_op jit(solution)/shard_map/ppermute | solution.py:33
  60.9 1.6 %collective-permute-start.13 = (bf16[32,3072]{1,0:T(8,128)(2,1)S(1)}, bf16[32,3072]{1,0:T(8,128)(2,1)S(1)}, u32[]{:S(2)}, u32[]{:S(2)}) collective-permute-start(bf16[32,3072]{1,0:T(8,128)(2,1)S(1)} %slice.101), channel_id=1, source_target_pairs={{0,2},{1,3},{2,0},{3,1},{4,6},{5,7},{6,4},{7,5},{8,10},{9,11},{10,... | collective-permute-start | bytes 589832 | tf_op jit(solution)/shard_map/ppermute | solution.py:33
  62.5 5.6 %convolution_convert_fusion.2 = bf16[1024,3072]{1,0:T(8,128)(2,1)} fusion(bf16[256,3072]{1,0:T(8,128)(2,1)S(1)} %constant_dynamic-update-slice_fusion, bf16[256,3072]{1,0:T(8,128)(2,1)S(1)} %pad_maximum_fusion.3, bf16[256,1024]{1,0:T(8,128)(2,1)S(1)} %get-tuple-element.102, bf16[256,1024]{1,0:T(8,128)(2,1)S(1)} %get-tuple-element.101, f32[512]{0:T(512)S(1)} %bitcast.72), kind=kOutput, calls=%fused_computation.10 | convolution fusion | flops 3233808384 | bytes 10487808 | tf_op jit(solution)/shard_map/dot_general | solution.py:245
  68.1 2.7 %collective-permute-start.14 = (bf16[32,3072]{1,0:T(8,128)(2,1)S(1)}, bf16[32,3072]{1,0:T(8,128)(2,1)S(1)}, u32[]{:S(2)}, u32[]{:S(2)}) collective-permute-start(bf16[32,3072]{1,0:T(8,128)(2,1)S(1)} %add_convert_fusion.9), channel_id=1, source_target_pairs={{0,4},{1,5},{2,6},{3,7},{4,0},{5,1},{6,2},{7,3},{8,12},{9,13},{10,... | collective-permute-start | bytes 589832 | tf_op jit(solution)/shard_map/ppermute | solution.py:33
  70.8 0.8 collective-permute-done.16
  71.6 0.3 add_convert_fusion
  71.9 0.9 collective-permute-start.17
  72.8 0.4 pad_maximum_fusion
  73.2 5.5 %convolution_convert_fusion.1 = bf16[3072,1024]{1,0:T(8,128)(2,1)} fusion(bf16[512,3072]{1,0:T(8,128)(2,1)S(1)} %pad_maximum_fusion, bf16[256,1024]{1,0:T(8,128)(2,1)S(1)} %get-tuple-element.110.gate_grad, bf16[256,1024]{1,0:T(8,128)(2,1)S(1)} %get-tuple-element.109.gate_grad), kind=kOutput, calls=%fused_computation.9 | convolution fusion | flops 3226468352 | bytes 10485760 | tf_op jit(solution)/shard_map/dot_general | solution.py:245
  78.7 1.2 %collective-permute-done.17 = bf16[64,3200]{1,0:T(8,128)(2,1)S(1)} collective-permute-done((bf16[64,3200]{1,0:T(8,128)(2,1)S(1)}, bf16[64,3200]{1,0:T(8,128)(2,1)S(1)}, u32[]{:S(2)}, u32[]{:S(2)}) %collective-permute-start.17) | collective-permute-done | bytes 409632 | tf_op jit(solution)/shard_map/ppermute | solution.py:33
  80.1 1.6 %collective-permute-start.18 = (bf16[32,3200]{1,0:T(8,128)(2,1)S(1)}, bf16[32,3200]{1,0:T(8,128)(2,1)S(1)}, u32[]{:S(2)}, u32[]{:S(2)}) collective-permute-start(bf16[32,3200]{1,0:T(8,128)(2,1)S(1)} %slice.105), channel_id=1, source_target_pairs={{0,2},{1,3},{2,0},{3,1},{4,6},{5,7},{6,4},{7,5},{8,10},{9,11},{10,... | collective-permute-start | bytes 614408 | tf_op jit(solution)/shard_map/ppermute | solution.py:33
  81.7 4.2 %collective-permute-done.18 = bf16[32,3200]{1,0:T(8,128)(2,1)S(1)} collective-permute-done((bf16[32,3200]{1,0:T(8,128)(2,1)S(1)}, bf16[32,3200]{1,0:T(8,128)(2,1)S(1)}, u32[]{:S(2)}, u32[]{:S(2)}) %collective-permute-start.18) | collective-permute-done | bytes 204832 | tf_op jit(solution)/shard_map/ppermute | solution.py:33
  86.0 2.7 %collective-permute-start.20 = (bf16[32,3200]{1,0:T(8,128)(2,1)S(1)}, bf16[32,3200]{1,0:T(8,128)(2,1)S(1)}, u32[]{:S(2)}, u32[]{:S(2)}) collective-permute-start(bf16[32,3200]{1,0:T(8,128)(2,1)S(1)} %add_convert_fusion.7), channel_id=1, source_target_pairs={{0,4},{1,5},{2,6},{3,7},{4,0},{5,1},{6,2},{7,3},{8,12},{9,13},{10,... | collective-permute-start | bytes 614408 | tf_op jit(solution)/shard_map/ppermute | solution.py:33
  88.6 1.6 %collective-permute-start.19 = (bf16[32,3072]{1,0:T(8,128)(2,1)S(1)}, bf16[32,3072]{1,0:T(8,128)(2,1)S(1)}, u32[]{:S(2)}, u32[]{:S(2)}) collective-permute-start(bf16[32,3072]{1,0:T(8,128)(2,1)S(1)} %add_convert_fusion.8), channel_id=1, source_target_pairs={{0,2},{1,3},{2,0},{3,1},{4,6},{5,7},{6,4},{7,5},{8,10},{9,11},{10,... | collective-permute-start | bytes 589832 | tf_op jit(solution)/shard_map/ppermute | solution.py:33
  90.2 5.5 %convolution_convert_fusion = bf16[3072,1024]{1,0:T(8,128)(2,1)} fusion(bf16[512,3072]{1,0:T(8,128)(2,1)S(1)} %pad_maximum_fusion, bf16[256,1024]{1,0:T(8,128)(2,1)S(1)} %get-tuple-element.117.up_grad, bf16[256,1024]{1,0:T(8,128)(2,1)S(1)} %get-tuple-element.116.up_grad), kind=kOutput, calls=%fused_computation.8 | convolution fusion | flops 3226468352 | bytes 10485760 | tf_op jit(solution)/shard_map/dot_general | solution.py:245
  95.7 0.4 collective-permute-done.20
  96.2 1.3 %collective-permute-start.22 = (bf16[32,3200]{1,0:T(8,128)(2,1)S(1)}, bf16[32,3200]{1,0:T(8,128)(2,1)S(1)}, u32[]{:S(2)}, u32[]{:S(2)}) collective-permute-start(bf16[32,3200]{1,0:T(8,128)(2,1)S(1)} %add_convert_fusion.6), channel_id=1, source_target_pairs={{0,2},{1,3},{2,0},{3,1},{4,6},{5,7},{6,4},{7,5},{8,10},{9,11},{10,... | collective-permute-start | bytes 614408 | tf_op jit(solution)/shard_map/ppermute | solution.py:33
  97.7 4.3 %collective-permute-done.22 = bf16[32,3200]{1,0:T(8,128)(2,1)S(1)} collective-permute-done((bf16[32,3200]{1,0:T(8,128)(2,1)S(1)}, bf16[32,3200]{1,0:T(8,128)(2,1)S(1)}, u32[]{:S(2)}, u32[]{:S(2)}) %collective-permute-start.22) | collective-permute-done | bytes 204832 | tf_op jit(solution)/shard_map/ppermute | solution.py:33
  102.2 1.0 maximum_select_fusion
  103.3 0.6 collective-permute-done.23
  103.9 0.2 fusion.43
  104.1 0.6 maximum_divide_fusion
  104.7 1.0 maximum_select_fusion.1
  (62 shorter events, 1.3 us)
Async XLA Ops:
  3.0 9.1 %collective-permute-start = (bf16[64,3200]{1,0:T(8,128)(2,1)}, bf16[64,3200]{1,0:T(8,128)(2,1)S(1)}, u32[]{:S(2)}, u32[]{:S(2)}) collective-permute-start(bf16[64,3200]{1,0:T(8,128)(2,1)} %get-tuple-element.64), channel_id=1, source_target_pairs={{0,8},{1,17},{2,10},{3,19},{4,12},{5,21},{6,14},{7,23},{8,0},{9,25... | collective-permute-start | bytes 1228808 | tf_op jit(solution)/shard_map/ppermute | solution.py:33
  6.0 1.1 %copy-start.1 = (bf16[128,3072]{1,0:T(8,128)(2,1)S(1)}, bf16[128,3072]{1,0:T(8,128)(2,1)}, u32[]{:S(2)}) copy-start(bf16[128,3072]{1,0:T(8,128)(2,1)} %refs_0_.2) | copy-start | bytes 2359300
  7.1 5.0 %copy-start.2 = (bf16[64,3200]{1,0:T(8,128)(2,1)S(1)}, bf16[64,3200]{1,0:T(8,128)(2,1)}, u32[]{:S(2)}) copy-start(bf16[64,3200]{1,0:T(8,128)(2,1)} %get-tuple-element.64) | copy-start | bytes 1228804
  7.1 7.2 %copy-start.3 = (bf16[64,3200]{1,0:T(8,128)(2,1)S(1)}, bf16[64,3200]{1,0:T(8,128)(2,1)}, u32[]{:S(2)}) copy-start(bf16[64,3200]{1,0:T(8,128)(2,1)} %get-tuple-element.65) | copy-start | bytes 1228804
  8.2 10.7 %collective-permute-start.2 = (bf16[64,3072]{1,0:T(8,128)(2,1)S(1)}, bf16[64,3072]{1,0:T(8,128)(2,1)S(1)}, u32[]{:S(2)}, u32[]{:S(2)}) collective-permute-start(bf16[64,3072]{1,0:T(8,128)(2,1)S(1)} %get-tuple-element.67), channel_id=1, source_target_pairs={{0,8},{1,17},{2,10},{3,19},{4,12},{5,21},{6,14},{7,23},{8,0},{9,25... | collective-permute-start | bytes 1179656 | tf_op jit(solution)/shard_map/ppermute | solution.py:33
  12.1 2.2 %collective-permute-start.1 = (bf16[64,3200]{1,0:T(8,128)(2,1)S(1)}, bf16[64,3200]{1,0:T(8,128)(2,1)S(1)}, u32[]{:S(2)}, u32[]{:S(2)}) collective-permute-start(bf16[64,3200]{1,0:T(8,128)(2,1)S(1)} %collective-permute-done), channel_id=1, source_target_pairs={{0,1},{1,0},{2,3},{3,2},{4,5},{5,4},{6,7},{7,6},{8,9},{9,8},{10,11... | collective-permute-start | bytes 1228808 | tf_op jit(solution)/shard_map/ppermute | solution.py:33
  12.2 12.4 %collective-permute-start.3 = (bf16[128,3200]{1,0:T(8,128)(2,1)S(1)}, bf16[128,3200]{1,0:T(8,128)(2,1)S(1)}, u32[]{:S(2)}, u32[]{:S(2)}) collective-permute-start(bf16[128,3200]{1,0:T(8,128)(2,1)S(1)} %pad_maximum_fusion.4), channel_id=1, source_target_pairs={{0,16},{1,9},{2,18},{3,11},{4,20},{5,13},{6,22},{7,15},{8,24},{9,1... | collective-permute-start | bytes 2457608 | tf_op jit(solution)/shard_map/ppermute | solution.py:33
  14.3 2.8 %copy-start = (bf16[1,3072,1024]{2,1,0:T(8,128)(2,1)S(1)}, bf16[1,3072,1024]{2,1,0:T(8,128)(2,1)}, u32[]{:S(2)}) copy-start(bf16[1,3072,1024]{2,1,0:T(8,128)(2,1)} %param.11) | copy-start | bytes 18874372
  14.4 4.5 %slice-start = ((s8[6291456]{0:T(1024)(128)(4,1)}), s8[4194304]{0:T(1024)(128)(4,1)S(1)}, s32[]{:S(2)}) async-start(s8[6291456]{0:T(1024)(128)(4,1)} %bitcast.62), calls=%async_computation | async-start | bytes 8388608
  17.1 2.0 %slice-start.1 = ((s8[6291456]{0:T(1024)(128)(4,1)}), s8[2097152]{0:T(1024)(128)(4,1)S(1)}, s32[]{:S(2)}) async-start(s8[6291456]{0:T(1024)(128)(4,1)} %bitcast.62), calls=%async_computation.1 | async-start | bytes 4194304
  21.2 2.1 %collective-permute-start.5 = (bf16[64,3072]{1,0:T(8,128)(2,1)S(1)}, bf16[64,3072]{1,0:T(8,128)(2,1)S(1)}, u32[]{:S(2)}, u32[]{:S(2)}) collective-permute-start(bf16[64,3072]{1,0:T(8,128)(2,1)S(1)} %collective-permute-done.2), channel_id=1, source_target_pairs={{0,1},{1,0},{2,3},{3,2},{4,5},{5,4},{6,7},{7,6},{8,9},{9,8},{10,11... | collective-permute-start | bytes 1179656 | tf_op jit(solution)/shard_map/ppermute | solution.py:33
  21.5 12.6 %collective-permute-start.9 = (bf16[128,3072]{1,0:T(8,128)(2,1)S(1)}, bf16[128,3072]{1,0:T(8,128)(2,1)S(1)}, u32[]{:S(2)}, u32[]{:S(2)}) collective-permute-start(bf16[128,3072]{1,0:T(8,128)(2,1)S(1)} %pad_maximum_fusion.5), channel_id=1, source_target_pairs={{0,16},{1,9},{2,18},{3,11},{4,20},{5,13},{6,22},{7,15},{8,24},{9,1... | collective-permute-start | bytes 2359304 | tf_op jit(solution)/shard_map/ppermute | solution.py:33
  24.6 5.1 %collective-permute-start.4 = (bf16[128,3200]{1,0:T(8,128)(2,1)S(1)}, bf16[128,3200]{1,0:T(8,128)(2,1)S(1)}, u32[]{:S(2)}, u32[]{:S(2)}) collective-permute-start(bf16[128,3200]{1,0:T(8,128)(2,1)S(1)} %collective-permute-done.3), channel_id=1, source_target_pairs={{0,1},{1,0},{2,3},{3,2},{4,5},{5,4},{6,7},{7,6},{8,9},{9,8},{10,11... | collective-permute-start | bytes 2457608 | tf_op jit(solution)/shard_map/ppermute | solution.py:33
  30.1 4.3 %slice-start.2 = ((s8[6291456]{0:T(1024)(128)(4,1)}), s8[4194304]{0:T(1024)(128)(4,1)S(1)}, s32[]{:S(2)}) async-start(s8[6291456]{0:T(1024)(128)(4,1)} %bitcast.73), calls=%async_computation.2 | async-start | bytes 8388608
  31.9 2.5 %slice-start.3 = ((s8[6291456]{0:T(1024)(128)(4,1)}), s8[2097152]{0:T(1024)(128)(4,1)S(1)}, s32[]{:S(2)}) async-start(s8[6291456]{0:T(1024)(128)(4,1)} %bitcast.73), calls=%async_computation.3 | async-start | bytes 4194304
  34.1 7.6 %collective-permute-start.10 = (bf16[128,3072]{1,0:T(8,128)(2,1)S(1)}, bf16[128,3072]{1,0:T(8,128)(2,1)S(1)}, u32[]{:S(2)}, u32[]{:S(2)}) collective-permute-start(bf16[128,3072]{1,0:T(8,128)(2,1)S(1)} %collective-permute-done.9), channel_id=1, source_target_pairs={{0,1},{1,0},{2,3},{3,2},{4,5},{5,4},{6,7},{7,6},{8,9},{9,8},{10,11... | collective-permute-start | bytes 2359304 | tf_op jit(solution)/shard_map/ppermute | solution.py:33
  36.4 2.9 %collective-permute-start.7 = (bf16[128,3072]{1,0:T(8,128)(2,1)S(1)}, bf16[128,3072]{1,0:T(8,128)(2,1)S(1)}, u32[]{:S(2)}, u32[]{:S(2)}) collective-permute-start(bf16[128,3072]{1,0:T(8,128)(2,1)S(1)} %get-tuple-element.79), channel_id=1, source_target_pairs={{0,1},{1,0},{2,3},{3,2},{4,5},{5,4},{6,7},{7,6},{8,9},{9,8},{10,11... | collective-permute-start | bytes 2359304 | tf_op jit(solution)/shard_map/ppermute | solution.py:33
  39.0 12.7 %collective-permute-start.6 = (bf16[128,3072]{1,0:T(8,128)(2,1)S(1)}, bf16[128,3072]{1,0:T(8,128)(2,1)S(1)}, u32[]{:S(2)}, u32[]{:S(2)}) collective-permute-start(bf16[128,3072]{1,0:T(8,128)(2,1)S(1)} %get-tuple-element.82), channel_id=1, source_target_pairs={{0,1},{1,0},{2,3},{3,2},{4,5},{5,4},{6,7},{7,6},{8,9},{9,8},{10,11... | collective-permute-start | bytes 2359304 | tf_op jit(solution)/shard_map/ppermute | solution.py:33
  39.4 12.2 %collective-permute-start.8 = (bf16[128,3072]{1,0:T(8,128)(2,1)S(1)}, bf16[128,3072]{1,0:T(8,128)(2,1)S(1)}, u32[]{:S(2)}, u32[]{:S(2)}) collective-permute-start(bf16[128,3072]{1,0:T(8,128)(2,1)S(1)} %add_convert_fusion.3), channel_id=1, source_target_pairs={{0,16},{1,9},{2,18},{3,11},{4,20},{5,13},{6,22},{7,15},{8,24},{9,1... | collective-permute-start | bytes 2359304 | tf_op jit(solution)/shard_map/ppermute | solution.py:33
  51.2 7.7 %collective-permute-start.12 = (bf16[128,3200]{1,0:T(8,128)(2,1)S(1)}, bf16[128,3200]{1,0:T(8,128)(2,1)S(1)}, u32[]{:S(2)}, u32[]{:S(2)}) collective-permute-start(bf16[128,3200]{1,0:T(8,128)(2,1)S(1)} %get-tuple-element.92), channel_id=1, source_target_pairs={{0,1},{1,0},{2,3},{3,2},{4,5},{5,4},{6,7},{7,6},{8,9},{9,8},{10,11... | collective-permute-start | bytes 2457608 | tf_op jit(solution)/shard_map/ppermute | solution.py:33
  52.1 8.7 %collective-permute-start.11 = (bf16[64,3072]{1,0:T(8,128)(2,1)S(1)}, bf16[64,3072]{1,0:T(8,128)(2,1)S(1)}, u32[]{:S(2)}, u32[]{:S(2)}) collective-permute-start(bf16[64,3072]{1,0:T(8,128)(2,1)S(1)} %slice.99), channel_id=1, source_target_pairs={{0,8},{1,17},{2,10},{3,19},{4,12},{5,21},{6,14},{7,23},{8,0},{9,25... | collective-permute-start | bytes 1179656 | tf_op jit(solution)/shard_map/ppermute | solution.py:33
  58.8 12.8 %collective-permute-start.15 = (bf16[128,3200]{1,0:T(8,128)(2,1)S(1)}, bf16[128,3200]{1,0:T(8,128)(2,1)S(1)}, u32[]{:S(2)}, u32[]{:S(2)}) collective-permute-start(bf16[128,3200]{1,0:T(8,128)(2,1)S(1)} %get-tuple-element.98), channel_id=1, source_target_pairs={{0,1},{1,0},{2,3},{3,2},{4,5},{5,4},{6,7},{7,6},{8,9},{9,8},{10,11... | collective-permute-start | bytes 2457608 | tf_op jit(solution)/shard_map/ppermute | solution.py:33
  59.2 12.4 %collective-permute-start.16 = (bf16[128,3200]{1,0:T(8,128)(2,1)S(1)}, bf16[128,3200]{1,0:T(8,128)(2,1)S(1)}, u32[]{:S(2)}, u32[]{:S(2)}) collective-permute-start(bf16[128,3200]{1,0:T(8,128)(2,1)S(1)} %add_convert_fusion.1), channel_id=1, source_target_pairs={{0,16},{1,9},{2,18},{3,11},{4,20},{5,13},{6,22},{7,15},{8,24},{9,1... | collective-permute-start | bytes 2457608 | tf_op jit(solution)/shard_map/ppermute | solution.py:33
  60.9 7.2 %collective-permute-start.13 = (bf16[32,3072]{1,0:T(8,128)(2,1)S(1)}, bf16[32,3072]{1,0:T(8,128)(2,1)S(1)}, u32[]{:S(2)}, u32[]{:S(2)}) collective-permute-start(bf16[32,3072]{1,0:T(8,128)(2,1)S(1)} %slice.101), channel_id=1, source_target_pairs={{0,2},{1,3},{2,0},{3,1},{4,6},{5,7},{6,4},{7,5},{8,10},{9,11},{10,... | collective-permute-start | bytes 589832 | tf_op jit(solution)/shard_map/ppermute | solution.py:33
  68.1 13.6 %collective-permute-start.14 = (bf16[32,3072]{1,0:T(8,128)(2,1)S(1)}, bf16[32,3072]{1,0:T(8,128)(2,1)S(1)}, u32[]{:S(2)}, u32[]{:S(2)}) collective-permute-start(bf16[32,3072]{1,0:T(8,128)(2,1)S(1)} %add_convert_fusion.9), channel_id=1, source_target_pairs={{0,4},{1,5},{2,6},{3,7},{4,0},{5,1},{6,2},{7,3},{8,12},{9,13},{10,... | collective-permute-start | bytes 589832 | tf_op jit(solution)/shard_map/ppermute | solution.py:33
  71.9 8.0 %collective-permute-start.17 = (bf16[64,3200]{1,0:T(8,128)(2,1)S(1)}, bf16[64,3200]{1,0:T(8,128)(2,1)S(1)}, u32[]{:S(2)}, u32[]{:S(2)}) collective-permute-start(bf16[64,3200]{1,0:T(8,128)(2,1)S(1)} %slice.103), channel_id=1, source_target_pairs={{0,8},{1,17},{2,10},{3,19},{4,12},{5,21},{6,14},{7,23},{8,0},{9,25... | collective-permute-start | bytes 1228808 | tf_op jit(solution)/shard_map/ppermute | solution.py:33
  80.1 5.9 %collective-permute-start.18 = (bf16[32,3200]{1,0:T(8,128)(2,1)S(1)}, bf16[32,3200]{1,0:T(8,128)(2,1)S(1)}, u32[]{:S(2)}, u32[]{:S(2)}) collective-permute-start(bf16[32,3200]{1,0:T(8,128)(2,1)S(1)} %slice.105), channel_id=1, source_target_pairs={{0,2},{1,3},{2,0},{3,1},{4,6},{5,7},{6,4},{7,5},{8,10},{9,11},{10,... | collective-permute-start | bytes 614408 | tf_op jit(solution)/shard_map/ppermute | solution.py:33
  86.0 10.1 %collective-permute-start.20 = (bf16[32,3200]{1,0:T(8,128)(2,1)S(1)}, bf16[32,3200]{1,0:T(8,128)(2,1)S(1)}, u32[]{:S(2)}, u32[]{:S(2)}) collective-permute-start(bf16[32,3200]{1,0:T(8,128)(2,1)S(1)} %add_convert_fusion.7), channel_id=1, source_target_pairs={{0,4},{1,5},{2,6},{3,7},{4,0},{5,1},{6,2},{7,3},{8,12},{9,13},{10,... | collective-permute-start | bytes 614408 | tf_op jit(solution)/shard_map/ppermute | solution.py:33
  88.6 7.6 %collective-permute-start.19 = (bf16[32,3072]{1,0:T(8,128)(2,1)S(1)}, bf16[32,3072]{1,0:T(8,128)(2,1)S(1)}, u32[]{:S(2)}, u32[]{:S(2)}) collective-permute-start(bf16[32,3072]{1,0:T(8,128)(2,1)S(1)} %add_convert_fusion.8), channel_id=1, source_target_pairs={{0,2},{1,3},{2,0},{3,1},{4,6},{5,7},{6,4},{7,5},{8,10},{9,11},{10,... | collective-permute-start | bytes 589832 | tf_op jit(solution)/shard_map/ppermute | solution.py:33
  95.7 6.5 %copy-start.5 = (s32[128,2]{0,1:T(2,128)S(1)}, s32[128,2]{0,1:T(2,128)}, u32[]{:S(2)}) copy-start(s32[128,2]{0,1:T(2,128)} %param.8) | copy-start | bytes 3076
  96.2 5.8 %collective-permute-start.22 = (bf16[32,3200]{1,0:T(8,128)(2,1)S(1)}, bf16[32,3200]{1,0:T(8,128)(2,1)S(1)}, u32[]{:S(2)}, u32[]{:S(2)}) collective-permute-start(bf16[32,3200]{1,0:T(8,128)(2,1)S(1)} %add_convert_fusion.6), channel_id=1, source_target_pairs={{0,2},{1,3},{2,0},{3,1},{4,6},{5,7},{6,4},{7,5},{8,10},{9,11},{10,... | collective-permute-start | bytes 614408 | tf_op jit(solution)/shard_map/ppermute | solution.py:33
  97.6 6.5 %copy-start.4 = (f32[128,2]{0,1:T(2,128)S(1)}, f32[128,2]{0,1:T(2,128)}, u32[]{:S(2)}) copy-start(f32[128,2]{0,1:T(2,128)} %param.9) | copy-start | bytes 3076
  97.6 4.6 %collective-permute-start.21 = (bf16[64,3072]{1,0:T(8,128)(2,1)S(1)}, bf16[64,3072]{1,0:T(8,128)(2,1)S(1)}, u32[]{:S(2)}, u32[]{:S(2)}) collective-permute-start(bf16[64,3072]{1,0:T(8,128)(2,1)S(1)} %maximum_select_fusion.3), channel_id=1, source_target_pairs={{0,1},{1,0},{2,3},{3,2},{4,5},{5,4},{6,7},{7,6},{8,9},{9,8},{10,11... | collective-permute-start | bytes 1179656 | tf_op jit(solution)/shard_map/ppermute | solution.py:33
  102.0 1.8 %collective-permute-start.23 = (bf16[64,3200]{1,0:T(8,128)(2,1)S(1)}, bf16[64,3200]{1,0:T(8,128)(2,1)S(1)}, u32[]{:S(2)}, u32[]{:S(2)}) collective-permute-start(bf16[64,3200]{1,0:T(8,128)(2,1)S(1)} %maximum_select_fusion.2), channel_id=1, source_target_pairs={{0,1},{1,0},{2,3},{3,2},{4,5},{5,4},{6,7},{7,6},{8,9},{9,8},{10,11... | collective-permute-start | bytes 1228808 | tf_op jit(solution)/shard_map/ppermute | solution.py:33

commit v5 on v4

--- a/solution.py
+++ b/solution.py
@@ -234,11 +234,9 @@
 
     def rows(self, columns, *after):
         part, other = self.part[:, columns], hold(self.came, *after)[:, columns]
-        return jnp.where(
-            self.links.core == 0,
-            jnp.concatenate([part, other], axis=0),
-            jnp.concatenate([other, part], axis=0),
-        )
+        both = lax.optimization_barrier(jnp.concatenate([part, part], axis=0))
+        start = (1 - self.links.core) * part.shape[0]
+        return lax.dynamic_update_slice_in_dim(both, other, start, 0)
 
 
 def dot(left, right, left_dim, right_dim):
@@ -272,7 +270,7 @@
 
 def back_terms(grad_gate, grad_up, pre_up, gate, up):
     rows, units, width = grad_gate.shape[0], gate.shape[1], gate.shape[0]
-    tile = tile_of(width, 512)
+    tile = tile_of(width, 768)
     tiles = width // tile
     middle = rows // 2
     nt = (((1,), (1,)), ((), ()))
@@ -305,7 +303,7 @@
         in_specs=[full] * 3 + [row] * 2,
         out_specs=[block] * 2,
         out_shape=[jax.ShapeDtypeStruct((middle, width + LANES), BF)] * 2,
-        compiler_params=pltpu.CompilerParams(vmem_limit_bytes=BACK_VMEM << 20),
+        compiler_params=pltpu.CompilerParams(vmem_limit_bytes=24 << 20),
         cost_estimate=pl.CostEstimate(flops=0, bytes_accessed=0, transcendentals=0),
     )(grad_gate, grad_up, pre_up, gate, up)
 

time: 106 us -> 105 us (level)
  other arithmetic: 5.52 us -> 3.6 us
    select_n x2 -> x0, other arithmetic: 2.08 us -> none  [rows(): jnp.where(self.links.core == 0, jnp.concatenate([part, other], axis=0), j...]
    unnamed x21 -> x25, local copies, waits for them, and re-layouts: 3.92 us -> 3.99 us
  transfers between devices with their start and end apart: 24 -> 24, of which waited for: 10 -> 10; matrix products, arithmetic and copies ran while one was open for 40% -> 40% of each run, Pallas kernels for 10% -> 9%
where the time goes in v5:
time: 105 us; the launch traced here: 104 us
  matrix products  37.7 us (36%)
  starting transfers between devices  27.1 us (26%)
  waiting for transfers between devices  18 us (17%)
  Pallas kernels  12.1 us (12%)
  local copies, waits for them, and re-layouts  4.81 us (5%)
  other arithmetic  3.6 us (3%)
  between operations  1.18 us (1%)
    dot_general x11, matrix products, dot(): lax.dot_general(left, right, (((left_dim,), (right_dim,)), ((), ())), pre...  37.7 us
    ppermute x24, starting transfers between devices, swap(): return lax.ppermute(value, AXES, pairs)  27.1 us
    ppermute x24, waiting for transfers between devices, swap(): return lax.ppermute(value, AXES, pairs)  18 us
    pallas_call x2, Pallas kernels, back_terms(): pl.pallas_call(kernel, grid=(tiles,), in_specs=[full] * 3 + [row] * 2, ou...  8.66 us
    unnamed x25, local copies, waits for them, and re-layouts  3.99 us
    pallas_call x2, Pallas kernels, halves(): pl.pallas_call(kernel, in_specs=[pl.BlockSpec(memory_space=pltpu.HBM)] *...  3.4 us
  transfers between devices with their start and end apart: 24, of which 10 were waited for; matrix products, arithmetic and copies ran while one was open for 40% of the time, Pallas kernels for 9%

profile of v5, /device:TPU:0, one launch (start us, length us, event | category | flops | bytes accessed | tf_op | source)
XLA Modules:
  0.0 104.4 jit_solution(5459318497662368886)
XLA Ops:
  0.6 2.3 %shard_map.118 = (bf16[64,3200]{1,0:T(8,128)(2,1)}, bf16[64,3200]{1,0:T(8,128)(2,1)}) custom-call(bf16[128,3072]{1,0:T(8,128)(2,1)} %refs_0_.1, s32[2,128]{1,0:T(2,128)} %bitcast.67, f32[2,128]{1,0:T(2,128)} %bitcast.66), custom_call_target="tpu_custom_call" | custom-call | tf_op jit(solution)/shard_map/pallas_call | solution.py:132
  3.0 3.0 %collective-permute-start = (bf16[64,3200]{1,0:T(8,128)(2,1)}, bf16[64,3200]{1,0:T(8,128)(2,1)S(1)}, u32[]{:S(2)}, u32[]{:S(2)}) collective-permute-start(bf16[64,3200]{1,0:T(8,128)(2,1)} %get-tuple-element.64), channel_id=1, source_target_pairs={{0,8},{1,17},{2,10},{3,19},{4,12},{5,21},{6,14},{7,23},{8,0},{9,25... | collective-permute-start | bytes 1228808 | tf_op jit(solution)/shard_map/ppermute | solution.py:33
  6.0 1.1 %copy-done.1 = bf16[128,3072]{1,0:T(8,128)(2,1)S(1)} copy-done((bf16[128,3072]{1,0:T(8,128)(2,1)S(1)}, bf16[128,3072]{1,0:T(8,128)(2,1)}, u32[]{:S(2)}) %copy-start.1) | copy-done | bytes 786456
  7.1 1.1 %shard_map.119 = (bf16[64,3072]{1,0:T(8,128)(2,1)S(1)}, bf16[64,3072]{1,0:T(8,128)(2,1)S(1)}) custom-call(bf16[128,3072]{1,0:T(8,128)(2,1)S(1)} %copy-done.1), custom_call_target="tpu_custom_call" | custom-call | flops 60000002048 | tf_op jit(solution)/shard_map/pallas_call | solution.py:132
  8.3 3.8 %collective-permute-done = bf16[64,3200]{1,0:T(8,128)(2,1)S(1)} collective-permute-done((bf16[64,3200]{1,0:T(8,128)(2,1)}, bf16[64,3200]{1,0:T(8,128)(2,1)S(1)}, u32[]{:S(2)}, u32[]{:S(2)}) %collective-permute-start) | collective-permute-done | bytes 409632 | tf_op jit(solution)/shard_map/ppermute | solution.py:33
  12.2 2.1 %collective-permute-start.3 = (bf16[128,3200]{1,0:T(8,128)(2,1)S(1)}, bf16[128,3200]{1,0:T(8,128)(2,1)S(1)}, u32[]{:S(2)}, u32[]{:S(2)}) collective-permute-start(bf16[128,3200]{1,0:T(8,128)(2,1)S(1)} %pad_maximum_fusion.4), channel_id=1, source_target_pairs={{0,16},{1,9},{2,18},{3,11},{4,20},{5,13},{6,22},{7,15},{8,24},{9,1... | collective-permute-start | bytes 2457608 | tf_op jit(solution)/shard_map/ppermute | solution.py:33
  14.3 0.1 pad_maximum_fusion.1
  14.4 0.2 slice.92
  14.6 2.5 %copy-done = bf16[1,3072,1024]{2,1,0:T(8,128)(2,1)S(1)} copy-done((bf16[1,3072,1024]{2,1,0:T(8,128)(2,1)S(1)}, bf16[1,3072,1024]{2,1,0:T(8,128)(2,1)}, u32[]{:S(2)}) %copy-start) | copy-done | bytes 6291480
  17.1 1.8 %fusion.54 = f32[256,1024]{1,0:T(8,128)S(1)} fusion(bf16[1,3072,1024]{2,1,0:T(8,128)(2,1)S(1)} %copy-done, bf16[256,3200]{1,0:T(8,128)(2,1)S(1)} %pad_maximum_fusion.1), kind=kOutput, calls=%fused_computation.94 | convolution fusion | flops 1610612736 | bytes 8912896 | tf_op jit(solution)/shard_map/dot_general | solution.py:243
  18.9 0.2 slice-done.1
  19.1 2.1 %multiply_convert_fusion.8 = (bf16[256,1024]{1,0:T(8,128)(2,1)S(1)}, bf16[256,1024]{1,0:T(8,128)(2,1)S(1)}, bf16[256,1024]{1,0:T(8,128)(2,1)S(1)}, bf16[256,1024]{1,0:T(8,128)(2,1)S(1)}) fusion(f32[256,1024]{1,0:T(8,128)S(1)} %fusion.54, bf16[256,3072]{1,0:T(8,128)(2,1)S(1)} %slice.92, bf16[1,3072,1024]{2,1,0:T(8,128)(2,1)S(1)} %bitcast.63), kind=kOutput, calls=%fused_computation.47 | convolution fusion | flops 1614282752 | bytes 11010048 | tf_op jit(solution)/shard_map/dot_general | solution.py:243
  21.2 0.3 collective-permute-start.5
  21.6 1.6 %collective-permute-start.9 = (bf16[128,3072]{1,0:T(8,128)(2,1)S(1)}, bf16[128,3072]{1,0:T(8,128)(2,1)S(1)}, u32[]{:S(2)}, u32[]{:S(2)}) collective-permute-start(bf16[128,3072]{1,0:T(8,128)(2,1)S(1)} %pad_maximum_fusion.5), channel_id=1, source_target_pairs={{0,16},{1,9},{2,18},{3,11},{4,20},{5,13},{6,22},{7,15},{8,24},{9,1... | collective-permute-start | bytes 2359304 | tf_op jit(solution)/shard_map/ppermute | solution.py:33
  23.2 0.1 select_reduce_fusion.1
  23.3 1.3 %collective-permute-done.3 = bf16[128,3200]{1,0:T(8,128)(2,1)S(1)} collective-permute-done((bf16[128,3200]{1,0:T(8,128)(2,1)S(1)}, bf16[128,3200]{1,0:T(8,128)(2,1)S(1)}, u32[]{:S(2)}, u32[]{:S(2)}) %collective-permute-start.3) | collective-permute-done | bytes 819232 | tf_op jit(solution)/shard_map/ppermute | solution.py:33
  24.6 0.3 collective-permute-start.4
  24.9 4.8 %multiply_convert_fusion.6 = (bf16[256,1024]{1,0:T(8,128)(2,1)S(1)}, bf16[256,1024]{1,0:T(8,128)(2,1)S(1)}) fusion(bf16[256,1024]{1,0:T(8,128)(2,1)S(1)} %get-tuple-element.73, bf16[256,1024]{1,0:T(8,128)(2,1)S(1)} %get-tuple-element.72, f32[256]{0:T(256)S(1)} %select_reduce_fusion.1, bf16[1,1024,3072]{2,1,0:T(8,128)(2,1)} %param.13, ...), kind=kOutput, calls=%fused_computation.45 | convolution fusion | flops 1618739200 | bytes 9962496 | tf_op jit(solution)/shard_map/dot_general | solution.py:243
  29.7 0.1 pad_maximum_fusion.3
  29.8 0.1 pad_maximum_fusion.2
  29.9 0.2 slice.71
  30.1 1.8 %fusion.52 = f32[256,1024]{1,0:T(8,128)S(1)} fusion(bf16[1,3072,1024]{2,1,0:T(8,128)(2,1)S(1)} %copy-done, bf16[256,3200]{1,0:T(8,128)(2,1)S(1)} %pad_maximum_fusion.2), kind=kOutput, calls=%fused_computation.92 | convolution fusion | flops 1610612736 | bytes 8912896 | tf_op jit(solution)/shard_map/dot_general | solution.py:243
  31.9 2.1 %multiply_convert_fusion.4 = (bf16[256,1024]{1,0:T(8,128)(2,1)S(1)}, bf16[256,1024]{1,0:T(8,128)(2,1)S(1)}, bf16[256,1024]{1,0:T(8,128)(2,1)S(1)}, bf16[256,1024]{1,0:T(8,128)(2,1)S(1)}) fusion(f32[256,1024]{1,0:T(8,128)S(1)} %fusion.52, bf16[256,3072]{1,0:T(8,128)(2,1)S(1)} %slice.71, bf16[1,3072,1024]{2,1,0:T(8,128)(2,1)S(1)} %bitcast.63), kind=kOutput, calls=%fused_computation.41 | convolution fusion | flops 1614282752 | bytes 11010048 | tf_op jit(solution)/shard_map/dot_general | solution.py:243
  34.1 0.1 select_reduce_fusion
  34.2 0.3 collective-permute-start.10
  34.5 1.9 %fusion.17 = bf16[256,3072]{1,0:T(8,128)(2,1)S(1)} fusion(bf16[256,1024]{1,0:T(8,128)(2,1)S(1)} %get-tuple-element.102, bf16[1,1024,3072]{2,1,0:T(8,128)(2,1)S(1)} %bitcast.74, f32[256]{0:T(256)S(1)} %select_reduce_fusion), kind=kOutput, calls=%fused_computation.14 | convolution fusion | flops 1612185600 | bytes 8389632 | tf_op jit(solution)/shard_map/dot_general | solution.py:243
  36.3 0.1 fusion.59
  36.5 0.4 collective-permute-start.7
  36.8 2.0 %fusion.14 = bf16[256,3072]{1,0:T(8,128)(2,1)S(1)} fusion(bf16[256,1024]{1,0:T(8,128)(2,1)S(1)} %get-tuple-element.101, bf16[1,1024,3072]{2,1,0:T(8,128)(2,1)S(1)} %bitcast.74, f32[256]{0:T(256)S(1)} %select_reduce_fusion.1), kind=kOutput, calls=%fused_computation.13 | convolution fusion | flops 1612185600 | bytes 8389632 | tf_op jit(solution)/shard_map/dot_general | solution.py:243
  38.9 0.1 fusion.58
  39.1 0.3 collective-permute-start.6
  39.3 0.2 add_convert_fusion.3
  39.5 2.2 %collective-permute-start.8 = (bf16[128,3072]{1,0:T(8,128)(2,1)S(1)}, bf16[128,3072]{1,0:T(8,128)(2,1)S(1)}, u32[]{:S(2)}, u32[]{:S(2)}) collective-permute-start(bf16[128,3072]{1,0:T(8,128)(2,1)S(1)} %add_convert_fusion.3), channel_id=1, source_target_pairs={{0,16},{1,9},{2,18},{3,11},{4,20},{5,13},{6,22},{7,15},{8,24},{9,1... | collective-permute-start | bytes 2359304 | tf_op jit(solution)/shard_map/ppermute | solution.py:33
  41.8 4.7 %multiply_convert_fusion.2 = (bf16[256,1024]{1,0:T(8,128)(2,1)S(1)}, bf16[256,1024]{1,0:T(8,128)(2,1)S(1)}) fusion(bf16[256,1024]{1,0:T(8,128)(2,1)S(1)} %get-tuple-element.87, bf16[256,1024]{1,0:T(8,128)(2,1)S(1)} %get-tuple-element.86, f32[256]{0:T(256)S(1)} %select_reduce_fusion, bf16[256,3072]{1,0:T(8,128)(2,1)S(1)} %constant_dynamic-update-slice_fusion, ...), kind=kOutput, calls=%fused_computation.39 | convolution fusion | flops 1612447744 | bytes 9962496 | tf_op jit(solution)/shard_map/dot_general | solution.py:243
  46.6 4.3 %shard_map.120 = (bf16[128,3200]{1,0:T(8,128)(2,1)S(1)}, bf16[128,3200]{1,0:T(8,128)(2,1)S(1)}) custom-call(bf16[256,1024]{1,0:T(8,128)(2,1)S(1)} %get-tuple-element.110.gate_grad, bf16[256,1024]{1,0:T(8,128)(2,1)S(1)} %get-tuple-element.117.up_grad, bf16[256,1024]{1,0:T(8,128)(2,1)S(1)} %get-tuple-element.90.pre_ref, bf16[3072,1024]{1,0:T(8,128)(2,1)S(1)} %bitcast.60, ...), custom_call_target="tpu_custom_call" | custom-call | tf_op jit(solution)/shard_map/pallas_call | solution.py:300
  50.9 0.2 collective-permute-start.12
  51.2 0.6 collective-permute-done.8
  51.8 0.4 add_convert_fusion.2
  52.2 2.1 %collective-permute-start.11 = (bf16[64,3072]{1,0:T(8,128)(2,1)S(1)}, bf16[64,3072]{1,0:T(8,128)(2,1)S(1)}, u32[]{:S(2)}, u32[]{:S(2)}) collective-permute-start(bf16[64,3072]{1,0:T(8,128)(2,1)S(1)} %slice.99), channel_id=1, source_target_pairs={{0,8},{1,17},{2,10},{3,19},{4,12},{5,21},{6,14},{7,23},{8,0},{9,25... | collective-permute-start | bytes 1179656 | tf_op jit(solution)/shard_map/ppermute | solution.py:33
  54.2 4.3 %shard_map.121 = (bf16[128,3200]{1,0:T(8,128)(2,1)S(1)}, bf16[128,3200]{1,0:T(8,128)(2,1)S(1)}) custom-call(bf16[256,1024]{1,0:T(8,128)(2,1)S(1)} %get-tuple-element.109.gate_grad, bf16[256,1024]{1,0:T(8,128)(2,1)S(1)} %get-tuple-element.116.up_grad, bf16[256,1024]{1,0:T(8,128)(2,1)S(1)} %get-tuple-element.96.pre_ref, bf16[3072,1024]{1,0:T(8,128)(2,1)S(1)} %bitcast.61, ...), custom_call_target="tpu_custom_call" | custom-call | tf_op jit(solution)/shard_map/pallas_call | solution.py:300
  58.6 0.2 add_convert_fusion.1
  58.8 1.6 %collective-permute-start.16 = (bf16[128,3200]{1,0:T(8,128)(2,1)S(1)}, bf16[128,3200]{1,0:T(8,128)(2,1)S(1)}, u32[]{:S(2)}, u32[]{:S(2)}) collective-permute-start(bf16[128,3200]{1,0:T(8,128)(2,1)S(1)} %add_convert_fusion.1), channel_id=1, source_target_pairs={{0,16},{1,9},{2,18},{3,11},{4,20},{5,13},{6,22},{7,15},{8,24},{9,1... | collective-permute-start | bytes 2457608 | tf_op jit(solution)/shard_map/ppermute | solution.py:33
  60.4 0.1 add_convert_fusion.5
  60.5 1.7 %collective-permute-start.13 = (bf16[32,3072]{1,0:T(8,128)(2,1)S(1)}, bf16[32,3072]{1,0:T(8,128)(2,1)S(1)}, u32[]{:S(2)}, u32[]{:S(2)}) collective-permute-start(bf16[32,3072]{1,0:T(8,128)(2,1)S(1)} %slice.101), channel_id=1, source_target_pairs={{0,2},{1,3},{2,0},{3,1},{4,6},{5,7},{6,4},{7,5},{8,10},{9,11},{10,... | collective-permute-start | bytes 589832 | tf_op jit(solution)/shard_map/ppermute | solution.py:33
  62.3 5.6 %convolution_convert_fusion.2 = bf16[1024,3072]{1,0:T(8,128)(2,1)} fusion(bf16[256,3072]{1,0:T(8,128)(2,1)S(1)} %constant_dynamic-update-slice_fusion, bf16[256,3072]{1,0:T(8,128)(2,1)S(1)} %pad_maximum_fusion.3, bf16[256,1024]{1,0:T(8,128)(2,1)S(1)} %get-tuple-element.102, bf16[256,1024]{1,0:T(8,128)(2,1)S(1)} %get-tuple-element.101, f32[512]{0:T(512)S(1)} %bitcast.72), kind=kOutput, calls=%fused_computation.10 | convolution fusion | flops 3233808384 | bytes 10487808 | tf_op jit(solution)/shard_map/dot_general | solution.py:243
  67.9 2.7 %collective-permute-start.14 = (bf16[32,3072]{1,0:T(8,128)(2,1)S(1)}, bf16[32,3072]{1,0:T(8,128)(2,1)S(1)}, u32[]{:S(2)}, u32[]{:S(2)}) collective-permute-start(bf16[32,3072]{1,0:T(8,128)(2,1)S(1)} %add_convert_fusion.9), channel_id=1, source_target_pairs={{0,4},{1,5},{2,6},{3,7},{4,0},{5,1},{6,2},{7,3},{8,12},{9,13},{10,... | collective-permute-start | bytes 589832 | tf_op jit(solution)/shard_map/ppermute | solution.py:33
  70.5 0.7 collective-permute-done.16
  71.2 0.3 add_convert_fusion
  71.6 0.9 collective-permute-start.17
  72.5 0.4 pad_maximum_fusion
  72.9 5.5 %convolution_convert_fusion.1 = bf16[3072,1024]{1,0:T(8,128)(2,1)} fusion(bf16[512,3072]{1,0:T(8,128)(2,1)S(1)} %pad_maximum_fusion, bf16[256,1024]{1,0:T(8,128)(2,1)S(1)} %get-tuple-element.110.gate_grad, bf16[256,1024]{1,0:T(8,128)(2,1)S(1)} %get-tuple-element.109.gate_grad), kind=kOutput, calls=%fused_computation.9 | convolution fusion | flops 3226468352 | bytes 10485760 | tf_op jit(solution)/shard_map/dot_general | solution.py:243
  78.4 1.2 %collective-permute-done.17 = bf16[64,3200]{1,0:T(8,128)(2,1)S(1)} collective-permute-done((bf16[64,3200]{1,0:T(8,128)(2,1)S(1)}, bf16[64,3200]{1,0:T(8,128)(2,1)S(1)}, u32[]{:S(2)}, u32[]{:S(2)}) %collective-permute-start.17) | collective-permute-done | bytes 409632 | tf_op jit(solution)/shard_map/ppermute | solution.py:33
  79.6 0.1 add_convert_fusion.4
  79.7 1.6 %collective-permute-start.18 = (bf16[32,3200]{1,0:T(8,128)(2,1)S(1)}, bf16[32,3200]{1,0:T(8,128)(2,1)S(1)}, u32[]{:S(2)}, u32[]{:S(2)}) collective-permute-start(bf16[32,3200]{1,0:T(8,128)(2,1)S(1)} %slice.105), channel_id=1, source_target_pairs={{0,2},{1,3},{2,0},{3,1},{4,6},{5,7},{6,4},{7,5},{8,10},{9,11},{10,... | collective-permute-start | bytes 614408 | tf_op jit(solution)/shard_map/ppermute | solution.py:33
  81.4 4.2 %collective-permute-done.18 = bf16[32,3200]{1,0:T(8,128)(2,1)S(1)} collective-permute-done((bf16[32,3200]{1,0:T(8,128)(2,1)S(1)}, bf16[32,3200]{1,0:T(8,128)(2,1)S(1)}, u32[]{:S(2)}, u32[]{:S(2)}) %collective-permute-start.18) | collective-permute-done | bytes 204832 | tf_op jit(solution)/shard_map/ppermute | solution.py:33
  85.6 2.7 %collective-permute-start.20 = (bf16[32,3200]{1,0:T(8,128)(2,1)S(1)}, bf16[32,3200]{1,0:T(8,128)(2,1)S(1)}, u32[]{:S(2)}, u32[]{:S(2)}) collective-permute-start(bf16[32,3200]{1,0:T(8,128)(2,1)S(1)} %add_convert_fusion.7), channel_id=1, source_target_pairs={{0,4},{1,5},{2,6},{3,7},{4,0},{5,1},{6,2},{7,3},{8,12},{9,13},{10,... | collective-permute-start | bytes 614408 | tf_op jit(solution)/shard_map/ppermute | solution.py:33
  88.3 1.6 %collective-permute-start.19 = (bf16[32,3072]{1,0:T(8,128)(2,1)S(1)}, bf16[32,3072]{1,0:T(8,128)(2,1)S(1)}, u32[]{:S(2)}, u32[]{:S(2)}) collective-permute-start(bf16[32,3072]{1,0:T(8,128)(2,1)S(1)} %add_convert_fusion.8), channel_id=1, source_target_pairs={{0,2},{1,3},{2,0},{3,1},{4,6},{5,7},{6,4},{7,5},{8,10},{9,11},{10,... | collective-permute-start | bytes 589832 | tf_op jit(solution)/shard_map/ppermute | solution.py:33
  89.9 5.5 %convolution_convert_fusion = bf16[3072,1024]{1,0:T(8,128)(2,1)} fusion(bf16[512,3072]{1,0:T(8,128)(2,1)S(1)} %pad_maximum_fusion, bf16[256,1024]{1,0:T(8,128)(2,1)S(1)} %get-tuple-element.117.up_grad, bf16[256,1024]{1,0:T(8,128)(2,1)S(1)} %get-tuple-element.116.up_grad), kind=kOutput, calls=%fused_computation.8 | convolution fusion | flops 3226468352 | bytes 10485760 | tf_op jit(solution)/shard_map/dot_general | solution.py:243
  95.3 0.4 collective-permute-done.20
  95.9 1.4 %collective-permute-start.22 = (bf16[32,3200]{1,0:T(8,128)(2,1)S(1)}, bf16[32,3200]{1,0:T(8,128)(2,1)S(1)}, u32[]{:S(2)}, u32[]{:S(2)}) collective-permute-start(bf16[32,3200]{1,0:T(8,128)(2,1)S(1)} %add_convert_fusion.6), channel_id=1, source_target_pairs={{0,2},{1,3},{2,0},{3,1},{4,6},{5,7},{6,4},{7,5},{8,10},{9,11},{10,... | collective-permute-start | bytes 614408 | tf_op jit(solution)/shard_map/ppermute | solution.py:33
  97.5 4.2 %collective-permute-done.22 = bf16[32,3200]{1,0:T(8,128)(2,1)S(1)} collective-permute-done((bf16[32,3200]{1,0:T(8,128)(2,1)S(1)}, bf16[32,3200]{1,0:T(8,128)(2,1)S(1)}, u32[]{:S(2)}, u32[]{:S(2)}) %collective-permute-start.22) | collective-permute-done | bytes 204832 | tf_op jit(solution)/shard_map/ppermute | solution.py:33
  102.0 1.5 %collective-permute-done.23 = bf16[64,3200]{1,0:T(8,128)(2,1)S(1)} collective-permute-done((bf16[64,3200]{1,0:T(8,128)(2,1)S(1)}, bf16[64,3200]{1,0:T(8,128)(2,1)S(1)}, u32[]{:S(2)}, u32[]{:S(2)}) %collective-permute-start.23) | collective-permute-done | bytes 409632 | tf_op jit(solution)/shard_map/ppermute | solution.py:33
  103.6 0.2 fusion.43
  103.8 0.6 maximum_divide_fusion
  (68 shorter events, 1.4 us)
Async XLA Ops:
  3.0 9.1 %collective-permute-start = (bf16[64,3200]{1,0:T(8,128)(2,1)}, bf16[64,3200]{1,0:T(8,128)(2,1)S(1)}, u32[]{:S(2)}, u32[]{:S(2)}) collective-permute-start(bf16[64,3200]{1,0:T(8,128)(2,1)} %get-tuple-element.64), channel_id=1, source_target_pairs={{0,8},{1,17},{2,10},{3,19},{4,12},{5,21},{6,14},{7,23},{8,0},{9,25... | collective-permute-start | bytes 1228808 | tf_op jit(solution)/shard_map/ppermute | solution.py:33
  6.0 1.1 %copy-start.1 = (bf16[128,3072]{1,0:T(8,128)(2,1)S(1)}, bf16[128,3072]{1,0:T(8,128)(2,1)}, u32[]{:S(2)}) copy-start(bf16[128,3072]{1,0:T(8,128)(2,1)} %refs_0_.2) | copy-start | bytes 2359300
  7.1 1.2 %copy-start.7 = (s32[128,2]{0,1:T(2,128)S(1)}, s32[128,2]{0,1:T(2,128)}, u32[]{:S(2)}) copy-start(s32[128,2]{0,1:T(2,128)} %param.8) | copy-start | bytes 3076
  7.1 5.0 %copy-start.2 = (bf16[64,3200]{1,0:T(8,128)(2,1)S(1)}, bf16[64,3200]{1,0:T(8,128)(2,1)}, u32[]{:S(2)}) copy-start(bf16[64,3200]{1,0:T(8,128)(2,1)} %get-tuple-element.64) | copy-start | bytes 1228804
  7.1 7.2 %copy-start.5 = (bf16[64,3200]{1,0:T(8,128)(2,1)S(1)}, bf16[64,3200]{1,0:T(8,128)(2,1)}, u32[]{:S(2)}) copy-start(bf16[64,3200]{1,0:T(8,128)(2,1)} %get-tuple-element.65) | copy-start | bytes 1228804
  8.2 10.7 %collective-permute-start.2 = (bf16[64,3072]{1,0:T(8,128)(2,1)S(1)}, bf16[64,3072]{1,0:T(8,128)(2,1)S(1)}, u32[]{:S(2)}, u32[]{:S(2)}) collective-permute-start(bf16[64,3072]{1,0:T(8,128)(2,1)S(1)} %get-tuple-element.67), channel_id=1, source_target_pairs={{0,8},{1,17},{2,10},{3,19},{4,12},{5,21},{6,14},{7,23},{8,0},{9,25... | collective-permute-start | bytes 1179656 | tf_op jit(solution)/shard_map/ppermute | solution.py:33
  12.1 2.2 %collective-permute-start.1 = (bf16[64,3200]{1,0:T(8,128)(2,1)S(1)}, bf16[64,3200]{1,0:T(8,128)(2,1)S(1)}, u32[]{:S(2)}, u32[]{:S(2)}) collective-permute-start(bf16[64,3200]{1,0:T(8,128)(2,1)S(1)} %collective-permute-done), channel_id=1, source_target_pairs={{0,1},{1,0},{2,3},{3,2},{4,5},{5,4},{6,7},{7,6},{8,9},{9,8},{10,11... | collective-permute-start | bytes 1228808 | tf_op jit(solution)/shard_map/ppermute | solution.py:33
  12.2 12.4 %collective-permute-start.3 = (bf16[128,3200]{1,0:T(8,128)(2,1)S(1)}, bf16[128,3200]{1,0:T(8,128)(2,1)S(1)}, u32[]{:S(2)}, u32[]{:S(2)}) collective-permute-start(bf16[128,3200]{1,0:T(8,128)(2,1)S(1)} %pad_maximum_fusion.4), channel_id=1, source_target_pairs={{0,16},{1,9},{2,18},{3,11},{4,20},{5,13},{6,22},{7,15},{8,24},{9,1... | collective-permute-start | bytes 2457608 | tf_op jit(solution)/shard_map/ppermute | solution.py:33
  14.3 2.8 %copy-start = (bf16[1,3072,1024]{2,1,0:T(8,128)(2,1)S(1)}, bf16[1,3072,1024]{2,1,0:T(8,128)(2,1)}, u32[]{:S(2)}) copy-start(bf16[1,3072,1024]{2,1,0:T(8,128)(2,1)} %param.11) | copy-start | bytes 18874372
  14.4 4.5 %slice-start = ((s8[6291456]{0:T(1024)(128)(4,1)}), s8[4194304]{0:T(1024)(128)(4,1)S(1)}, s32[]{:S(2)}) async-start(s8[6291456]{0:T(1024)(128)(4,1)} %bitcast.62), calls=%async_computation | async-start | bytes 8388608
  17.1 2.0 %slice-start.1 = ((s8[6291456]{0:T(1024)(128)(4,1)}), s8[2097152]{0:T(1024)(128)(4,1)S(1)}, s32[]{:S(2)}) async-start(s8[6291456]{0:T(1024)(128)(4,1)} %bitcast.62), calls=%async_computation.1 | async-start | bytes 4194304
  21.2 2.0 %collective-permute-start.5 = (bf16[64,3072]{1,0:T(8,128)(2,1)S(1)}, bf16[64,3072]{1,0:T(8,128)(2,1)S(1)}, u32[]{:S(2)}, u32[]{:S(2)}) collective-permute-start(bf16[64,3072]{1,0:T(8,128)(2,1)S(1)} %collective-permute-done.2), channel_id=1, source_target_pairs={{0,1},{1,0},{2,3},{3,2},{4,5},{5,4},{6,7},{7,6},{8,9},{9,8},{10,11... | collective-permute-start | bytes 1179656 | tf_op jit(solution)/shard_map/ppermute | solution.py:33
  21.6 12.6 %collective-permute-start.9 = (bf16[128,3072]{1,0:T(8,128)(2,1)S(1)}, bf16[128,3072]{1,0:T(8,128)(2,1)S(1)}, u32[]{:S(2)}, u32[]{:S(2)}) collective-permute-start(bf16[128,3072]{1,0:T(8,128)(2,1)S(1)} %pad_maximum_fusion.5), channel_id=1, source_target_pairs={{0,16},{1,9},{2,18},{3,11},{4,20},{5,13},{6,22},{7,15},{8,24},{9,1... | collective-permute-start | bytes 2359304 | tf_op jit(solution)/shard_map/ppermute | solution.py:33
  24.6 5.2 %collective-permute-start.4 = (bf16[128,3200]{1,0:T(8,128)(2,1)S(1)}, bf16[128,3200]{1,0:T(8,128)(2,1)S(1)}, u32[]{:S(2)}, u32[]{:S(2)}) collective-permute-start(bf16[128,3200]{1,0:T(8,128)(2,1)S(1)} %collective-permute-done.3), channel_id=1, source_target_pairs={{0,1},{1,0},{2,3},{3,2},{4,5},{5,4},{6,7},{7,6},{8,9},{9,8},{10,11... | collective-permute-start | bytes 2457608 | tf_op jit(solution)/shard_map/ppermute | solution.py:33
  30.1 4.4 %slice-start.2 = ((s8[6291456]{0:T(1024)(128)(4,1)}), s8[4194304]{0:T(1024)(128)(4,1)S(1)}, s32[]{:S(2)}) async-start(s8[6291456]{0:T(1024)(128)(4,1)} %bitcast.73), calls=%async_computation.2 | async-start | bytes 8388608
  31.9 2.5 %slice-start.3 = ((s8[6291456]{0:T(1024)(128)(4,1)}), s8[2097152]{0:T(1024)(128)(4,1)S(1)}, s32[]{:S(2)}) async-start(s8[6291456]{0:T(1024)(128)(4,1)} %bitcast.73), calls=%async_computation.3 | async-start | bytes 4194304
  34.2 7.6 %collective-permute-start.10 = (bf16[128,3072]{1,0:T(8,128)(2,1)S(1)}, bf16[128,3072]{1,0:T(8,128)(2,1)S(1)}, u32[]{:S(2)}, u32[]{:S(2)}) collective-permute-start(bf16[128,3072]{1,0:T(8,128)(2,1)S(1)} %collective-permute-done.9), channel_id=1, source_target_pairs={{0,1},{1,0},{2,3},{3,2},{4,5},{5,4},{6,7},{7,6},{8,9},{9,8},{10,11... | collective-permute-start | bytes 2359304 | tf_op jit(solution)/shard_map/ppermute | solution.py:33
  36.5 2.9 %collective-permute-start.7 = (bf16[128,3072]{1,0:T(8,128)(2,1)S(1)}, bf16[128,3072]{1,0:T(8,128)(2,1)S(1)}, u32[]{:S(2)}, u32[]{:S(2)}) collective-permute-start(bf16[128,3072]{1,0:T(8,128)(2,1)S(1)} %get-tuple-element.79), channel_id=1, source_target_pairs={{0,1},{1,0},{2,3},{3,2},{4,5},{5,4},{6,7},{7,6},{8,9},{9,8},{10,11... | collective-permute-start | bytes 2359304 | tf_op jit(solution)/shard_map/ppermute | solution.py:33
  39.1 12.7 %collective-permute-start.6 = (bf16[128,3072]{1,0:T(8,128)(2,1)S(1)}, bf16[128,3072]{1,0:T(8,128)(2,1)S(1)}, u32[]{:S(2)}, u32[]{:S(2)}) collective-permute-start(bf16[128,3072]{1,0:T(8,128)(2,1)S(1)} %get-tuple-element.82), channel_id=1, source_target_pairs={{0,1},{1,0},{2,3},{3,2},{4,5},{5,4},{6,7},{7,6},{8,9},{9,8},{10,11... | collective-permute-start | bytes 2359304 | tf_op jit(solution)/shard_map/ppermute | solution.py:33
  39.5 12.2 %collective-permute-start.8 = (bf16[128,3072]{1,0:T(8,128)(2,1)S(1)}, bf16[128,3072]{1,0:T(8,128)(2,1)S(1)}, u32[]{:S(2)}, u32[]{:S(2)}) collective-permute-start(bf16[128,3072]{1,0:T(8,128)(2,1)S(1)} %add_convert_fusion.3), channel_id=1, source_target_pairs={{0,16},{1,9},{2,18},{3,11},{4,20},{5,13},{6,22},{7,15},{8,24},{9,1... | collective-permute-start | bytes 2359304 | tf_op jit(solution)/shard_map/ppermute | solution.py:33
  50.9 7.7 %collective-permute-start.12 = (bf16[128,3200]{1,0:T(8,128)(2,1)S(1)}, bf16[128,3200]{1,0:T(8,128)(2,1)S(1)}, u32[]{:S(2)}, u32[]{:S(2)}) collective-permute-start(bf16[128,3200]{1,0:T(8,128)(2,1)S(1)} %get-tuple-element.92), channel_id=1, source_target_pairs={{0,1},{1,0},{2,3},{3,2},{4,5},{5,4},{6,7},{7,6},{8,9},{9,8},{10,11... | collective-permute-start | bytes 2457608 | tf_op jit(solution)/shard_map/ppermute | solution.py:33
  52.2 8.3 %collective-permute-start.11 = (bf16[64,3072]{1,0:T(8,128)(2,1)S(1)}, bf16[64,3072]{1,0:T(8,128)(2,1)S(1)}, u32[]{:S(2)}, u32[]{:S(2)}) collective-permute-start(bf16[64,3072]{1,0:T(8,128)(2,1)S(1)} %slice.99), channel_id=1, source_target_pairs={{0,8},{1,17},{2,10},{3,19},{4,12},{5,21},{6,14},{7,23},{8,0},{9,25... | collective-permute-start | bytes 1179656 | tf_op jit(solution)/shard_map/ppermute | solution.py:33
  58.5 12.7 %collective-permute-start.15 = (bf16[128,3200]{1,0:T(8,128)(2,1)S(1)}, bf16[128,3200]{1,0:T(8,128)(2,1)S(1)}, u32[]{:S(2)}, u32[]{:S(2)}) collective-permute-start(bf16[128,3200]{1,0:T(8,128)(2,1)S(1)} %get-tuple-element.98), channel_id=1, source_target_pairs={{0,1},{1,0},{2,3},{3,2},{4,5},{5,4},{6,7},{7,6},{8,9},{9,8},{10,11... | collective-permute-start | bytes 2457608 | tf_op jit(solution)/shard_map/ppermute | solution.py:33
  58.8 12.4 %collective-permute-start.16 = (bf16[128,3200]{1,0:T(8,128)(2,1)S(1)}, bf16[128,3200]{1,0:T(8,128)(2,1)S(1)}, u32[]{:S(2)}, u32[]{:S(2)}) collective-permute-start(bf16[128,3200]{1,0:T(8,128)(2,1)S(1)} %add_convert_fusion.1), channel_id=1, source_target_pairs={{0,16},{1,9},{2,18},{3,11},{4,20},{5,13},{6,22},{7,15},{8,24},{9,1... | collective-permute-start | bytes 2457608 | tf_op jit(solution)/shard_map/ppermute | solution.py:33
  60.5 7.3 %collective-permute-start.13 = (bf16[32,3072]{1,0:T(8,128)(2,1)S(1)}, bf16[32,3072]{1,0:T(8,128)(2,1)S(1)}, u32[]{:S(2)}, u32[]{:S(2)}) collective-permute-start(bf16[32,3072]{1,0:T(8,128)(2,1)S(1)} %slice.101), channel_id=1, source_target_pairs={{0,2},{1,3},{2,0},{3,1},{4,6},{5,7},{6,4},{7,5},{8,10},{9,11},{10,... | collective-permute-start | bytes 589832 | tf_op jit(solution)/shard_map/ppermute | solution.py:33
  67.9 13.5 %collective-permute-start.14 = (bf16[32,3072]{1,0:T(8,128)(2,1)S(1)}, bf16[32,3072]{1,0:T(8,128)(2,1)S(1)}, u32[]{:S(2)}, u32[]{:S(2)}) collective-permute-start(bf16[32,3072]{1,0:T(8,128)(2,1)S(1)} %add_convert_fusion.9), channel_id=1, source_target_pairs={{0,4},{1,5},{2,6},{3,7},{4,0},{5,1},{6,2},{7,3},{8,12},{9,13},{10,... | collective-permute-start | bytes 589832 | tf_op jit(solution)/shard_map/ppermute | solution.py:33
  71.6 8.0 %collective-permute-start.17 = (bf16[64,3200]{1,0:T(8,128)(2,1)S(1)}, bf16[64,3200]{1,0:T(8,128)(2,1)S(1)}, u32[]{:S(2)}, u32[]{:S(2)}) collective-permute-start(bf16[64,3200]{1,0:T(8,128)(2,1)S(1)} %slice.103), channel_id=1, source_target_pairs={{0,8},{1,17},{2,10},{3,19},{4,12},{5,21},{6,14},{7,23},{8,0},{9,25... | collective-permute-start | bytes 1228808 | tf_op jit(solution)/shard_map/ppermute | solution.py:33
  79.7 5.9 %collective-permute-start.18 = (bf16[32,3200]{1,0:T(8,128)(2,1)S(1)}, bf16[32,3200]{1,0:T(8,128)(2,1)S(1)}, u32[]{:S(2)}, u32[]{:S(2)}) collective-permute-start(bf16[32,3200]{1,0:T(8,128)(2,1)S(1)} %slice.105), channel_id=1, source_target_pairs={{0,2},{1,3},{2,0},{3,1},{4,6},{5,7},{6,4},{7,5},{8,10},{9,11},{10,... | collective-permute-start | bytes 614408 | tf_op jit(solution)/shard_map/ppermute | solution.py:33
  85.6 10.1 %collective-permute-start.20 = (bf16[32,3200]{1,0:T(8,128)(2,1)S(1)}, bf16[32,3200]{1,0:T(8,128)(2,1)S(1)}, u32[]{:S(2)}, u32[]{:S(2)}) collective-permute-start(bf16[32,3200]{1,0:T(8,128)(2,1)S(1)} %add_convert_fusion.7), channel_id=1, source_target_pairs={{0,4},{1,5},{2,6},{3,7},{4,0},{5,1},{6,2},{7,3},{8,12},{9,13},{10,... | collective-permute-start | bytes 614408 | tf_op jit(solution)/shard_map/ppermute | solution.py:33
  88.3 7.6 %collective-permute-start.19 = (bf16[32,3072]{1,0:T(8,128)(2,1)S(1)}, bf16[32,3072]{1,0:T(8,128)(2,1)S(1)}, u32[]{:S(2)}, u32[]{:S(2)}) collective-permute-start(bf16[32,3072]{1,0:T(8,128)(2,1)S(1)} %add_convert_fusion.8), channel_id=1, source_target_pairs={{0,2},{1,3},{2,0},{3,1},{4,6},{5,7},{6,4},{7,5},{8,10},{9,11},{10,... | collective-permute-start | bytes 589832 | tf_op jit(solution)/shard_map/ppermute | solution.py:33
  95.9 5.8 %collective-permute-start.22 = (bf16[32,3200]{1,0:T(8,128)(2,1)S(1)}, bf16[32,3200]{1,0:T(8,128)(2,1)S(1)}, u32[]{:S(2)}, u32[]{:S(2)}) collective-permute-start(bf16[32,3200]{1,0:T(8,128)(2,1)S(1)} %add_convert_fusion.6), channel_id=1, source_target_pairs={{0,2},{1,3},{2,0},{3,1},{4,6},{5,7},{6,4},{7,5},{8,10},{9,11},{10,... | collective-permute-start | bytes 614408 | tf_op jit(solution)/shard_map/ppermute | solution.py:33
  97.3 4.6 %collective-permute-start.21 = (bf16[64,3072]{1,0:T(8,128)(2,1)S(1)}, bf16[64,3072]{1,0:T(8,128)(2,1)S(1)}, u32[]{:S(2)}, u32[]{:S(2)}) collective-permute-start(bf16[64,3072]{1,0:T(8,128)(2,1)S(1)} %maximum_select_fusion.1), channel_id=1, source_target_pairs={{0,1},{1,0},{2,3},{3,2},{4,5},{5,4},{6,7},{7,6},{8,9},{9,8},{10,11... | collective-permute-start | bytes 1179656 | tf_op jit(solution)/shard_map/ppermute | solution.py:33
  97.4 6.3 %copy-start.6 = (f32[128,2]{0,1:T(2,128)S(1)}, f32[128,2]{0,1:T(2,128)}, u32[]{:S(2)}) copy-start(f32[128,2]{0,1:T(2,128)} %param.9) | copy-start | bytes 3076
  101.7 1.8 %collective-permute-start.23 = (bf16[64,3200]{1,0:T(8,128)(2,1)S(1)}, bf16[64,3200]{1,0:T(8,128)(2,1)S(1)}, u32[]{:S(2)}, u32[]{:S(2)}) collective-permute-start(bf16[64,3200]{1,0:T(8,128)(2,1)S(1)} %maximum_select_fusion), channel_id=1, source_target_pairs={{0,1},{1,0},{2,3},{3,2},{4,5},{5,4},{6,7},{7,6},{8,9},{9,8},{10,11... | collective-permute-start | bytes 1228808 | tf_op jit(solution)/shard_map/ppermute | solution.py:33
  102.0 2.4 %copy-start.3 = (bf16[128,3072]{1,0:T(8,128)(2,1)}, bf16[128,3072]{1,0:T(8,128)(2,1)S(1)}, u32[]{:S(2)}) copy-start(bf16[128,3072]{1,0:T(8,128)(2,1)S(1)} %constant_dynamic-update-slice_fusion.2) | copy-start | bytes 2359300
  103.6 0.9 copy-start.4

commit v6 on v5

--- a/solution.py
+++ b/solution.py
@@ -139,7 +139,7 @@
             pltpu.VMEM((max(top, 1), count), F32),
             pltpu.SemaphoreType.DMA((6,)),
         ],
-        compiler_params=pltpu.CompilerParams(vmem_limit_bytes=(16 if weight else 63) << 20),
+        compiler_params=pltpu.CompilerParams(vmem_limit_bytes=(16 if weight else 60) << 20),
         cost_estimate=pl.CostEstimate(flops=weight, bytes_accessed=0, transcendentals=0),
     )(*operands)
 

time: 105 us -> 105 us (level)
  no operation moved by 1% of the time
where the time goes in v6:
time: 105 us; the launch traced here: 104 us
  matrix products  37.7 us (36%)
  starting transfers between devices  27.1 us (26%)
  waiting for transfers between devices  18 us (17%)
  Pallas kernels  12.1 us (12%)
  local copies, waits for them, and re-layouts  4.81 us (5%)
  other arithmetic  3.6 us (3%)
  between operations  1.18 us (1%)
    dot_general x11, matrix products, dot(): lax.dot_general(left, right, (((left_dim,), (right_dim,)), ((), ())), pre...  37.7 us
    ppermute x24, starting transfers between devices, swap(): return lax.ppermute(value, AXES, pairs)  27.1 us
    ppermute x24, waiting for transfers between devices, swap(): return lax.ppermute(value, AXES, pairs)  18 us
    pallas_call x2, Pallas kernels, back_terms(): pl.pallas_call(kernel, grid=(tiles,), in_specs=[full] * 3 + [row] * 2, ou...  8.66 us
    unnamed x25, local copies, waits for them, and re-layouts  3.99 us
    pallas_call x2, Pallas kernels, halves(): pl.pallas_call(kernel, in_specs=[pl.BlockSpec(memory_space=pltpu.HBM)] *...  3.4 us
  transfers between devices with their start and end apart: 24, of which 10 were waited for; matrix products, arithmetic and copies ran while one was open for 40% of the time, Pallas kernels for 9%

profile of v6, /device:TPU:0, one launch (start us, length us, event | category | flops | bytes accessed | tf_op | source)
XLA Modules:
  0.0 104.4 jit_solution(5459318497662368886)
XLA Ops:
  0.6 2.3 %shard_map.118 = (bf16[64,3200]{1,0:T(8,128)(2,1)}, bf16[64,3200]{1,0:T(8,128)(2,1)}) custom-call(bf16[128,3072]{1,0:T(8,128)(2,1)} %refs_0_.1, s32[2,128]{1,0:T(2,128)} %bitcast.67, f32[2,128]{1,0:T(2,128)} %bitcast.66), custom_call_target="tpu_custom_call" | custom-call | tf_op jit(solution)/shard_map/pallas_call | solution.py:132
  3.0 3.0 %collective-permute-start = (bf16[64,3200]{1,0:T(8,128)(2,1)}, bf16[64,3200]{1,0:T(8,128)(2,1)S(1)}, u32[]{:S(2)}, u32[]{:S(2)}) collective-permute-start(bf16[64,3200]{1,0:T(8,128)(2,1)} %get-tuple-element.64), channel_id=1, source_target_pairs={{0,8},{1,17},{2,10},{3,19},{4,12},{5,21},{6,14},{7,23},{8,0},{9,25... | collective-permute-start | bytes 1228808 | tf_op jit(solution)/shard_map/ppermute | solution.py:33
  6.0 1.1 %copy-done.1 = bf16[128,3072]{1,0:T(8,128)(2,1)S(1)} copy-done((bf16[128,3072]{1,0:T(8,128)(2,1)S(1)}, bf16[128,3072]{1,0:T(8,128)(2,1)}, u32[]{:S(2)}) %copy-start.1) | copy-done | bytes 786456
  7.1 1.1 %shard_map.119 = (bf16[64,3072]{1,0:T(8,128)(2,1)S(1)}, bf16[64,3072]{1,0:T(8,128)(2,1)S(1)}) custom-call(bf16[128,3072]{1,0:T(8,128)(2,1)S(1)} %copy-done.1), custom_call_target="tpu_custom_call" | custom-call | flops 60000002048 | tf_op jit(solution)/shard_map/pallas_call | solution.py:132
  8.3 3.8 %collective-permute-done = bf16[64,3200]{1,0:T(8,128)(2,1)S(1)} collective-permute-done((bf16[64,3200]{1,0:T(8,128)(2,1)}, bf16[64,3200]{1,0:T(8,128)(2,1)S(1)}, u32[]{:S(2)}, u32[]{:S(2)}) %collective-permute-start) | collective-permute-done | bytes 409632 | tf_op jit(solution)/shard_map/ppermute | solution.py:33
  12.2 2.1 %collective-permute-start.3 = (bf16[128,3200]{1,0:T(8,128)(2,1)S(1)}, bf16[128,3200]{1,0:T(8,128)(2,1)S(1)}, u32[]{:S(2)}, u32[]{:S(2)}) collective-permute-start(bf16[128,3200]{1,0:T(8,128)(2,1)S(1)} %pad_maximum_fusion.4), channel_id=1, source_target_pairs={{0,16},{1,9},{2,18},{3,11},{4,20},{5,13},{6,22},{7,15},{8,24},{9,1... | collective-permute-start | bytes 2457608 | tf_op jit(solution)/shard_map/ppermute | solution.py:33
  14.3 0.1 pad_maximum_fusion.1
  14.4 0.2 slice.92
  14.6 2.5 %copy-done = bf16[1,3072,1024]{2,1,0:T(8,128)(2,1)S(1)} copy-done((bf16[1,3072,1024]{2,1,0:T(8,128)(2,1)S(1)}, bf16[1,3072,1024]{2,1,0:T(8,128)(2,1)}, u32[]{:S(2)}) %copy-start) | copy-done | bytes 6291480
  17.1 1.8 %fusion.54 = f32[256,1024]{1,0:T(8,128)S(1)} fusion(bf16[1,3072,1024]{2,1,0:T(8,128)(2,1)S(1)} %copy-done, bf16[256,3200]{1,0:T(8,128)(2,1)S(1)} %pad_maximum_fusion.1), kind=kOutput, calls=%fused_computation.94 | convolution fusion | flops 1610612736 | bytes 8912896 | tf_op jit(solution)/shard_map/dot_general | solution.py:243
  18.9 0.2 slice-done.1
  19.1 2.1 %multiply_convert_fusion.8 = (bf16[256,1024]{1,0:T(8,128)(2,1)S(1)}, bf16[256,1024]{1,0:T(8,128)(2,1)S(1)}, bf16[256,1024]{1,0:T(8,128)(2,1)S(1)}, bf16[256,1024]{1,0:T(8,128)(2,1)S(1)}) fusion(f32[256,1024]{1,0:T(8,128)S(1)} %fusion.54, bf16[256,3072]{1,0:T(8,128)(2,1)S(1)} %slice.92, bf16[1,3072,1024]{2,1,0:T(8,128)(2,1)S(1)} %bitcast.63), kind=kOutput, calls=%fused_computation.47 | convolution fusion | flops 1614282752 | bytes 11010048 | tf_op jit(solution)/shard_map/dot_general | solution.py:243
  21.2 0.3 collective-permute-start.5
  21.6 1.6 %collective-permute-start.9 = (bf16[128,3072]{1,0:T(8,128)(2,1)S(1)}, bf16[128,3072]{1,0:T(8,128)(2,1)S(1)}, u32[]{:S(2)}, u32[]{:S(2)}) collective-permute-start(bf16[128,3072]{1,0:T(8,128)(2,1)S(1)} %pad_maximum_fusion.5), channel_id=1, source_target_pairs={{0,16},{1,9},{2,18},{3,11},{4,20},{5,13},{6,22},{7,15},{8,24},{9,1... | collective-permute-start | bytes 2359304 | tf_op jit(solution)/shard_map/ppermute | solution.py:33
  23.2 0.1 select_reduce_fusion.1
  23.3 1.3 %collective-permute-done.3 = bf16[128,3200]{1,0:T(8,128)(2,1)S(1)} collective-permute-done((bf16[128,3200]{1,0:T(8,128)(2,1)S(1)}, bf16[128,3200]{1,0:T(8,128)(2,1)S(1)}, u32[]{:S(2)}, u32[]{:S(2)}) %collective-permute-start.3) | collective-permute-done | bytes 819232 | tf_op jit(solution)/shard_map/ppermute | solution.py:33
  24.6 0.3 collective-permute-start.4
  24.9 4.8 %multiply_convert_fusion.6 = (bf16[256,1024]{1,0:T(8,128)(2,1)S(1)}, bf16[256,1024]{1,0:T(8,128)(2,1)S(1)}) fusion(bf16[256,1024]{1,0:T(8,128)(2,1)S(1)} %get-tuple-element.73, bf16[256,1024]{1,0:T(8,128)(2,1)S(1)} %get-tuple-element.72, f32[256]{0:T(256)S(1)} %select_reduce_fusion.1, bf16[1,1024,3072]{2,1,0:T(8,128)(2,1)} %param.13, ...), kind=kOutput, calls=%fused_computation.45 | convolution fusion | flops 1618739200 | bytes 9962496 | tf_op jit(solution)/shard_map/dot_general | solution.py:243
  29.7 0.1 pad_maximum_fusion.3
  29.8 0.1 pad_maximum_fusion.2
  29.9 0.2 slice.71
  30.1 1.8 %fusion.52 = f32[256,1024]{1,0:T(8,128)S(1)} fusion(bf16[1,3072,1024]{2,1,0:T(8,128)(2,1)S(1)} %copy-done, bf16[256,3200]{1,0:T(8,128)(2,1)S(1)} %pad_maximum_fusion.2), kind=kOutput, calls=%fused_computation.92 | convolution fusion | flops 1610612736 | bytes 8912896 | tf_op jit(solution)/shard_map/dot_general | solution.py:243
  31.9 2.1 %multiply_convert_fusion.4 = (bf16[256,1024]{1,0:T(8,128)(2,1)S(1)}, bf16[256,1024]{1,0:T(8,128)(2,1)S(1)}, bf16[256,1024]{1,0:T(8,128)(2,1)S(1)}, bf16[256,1024]{1,0:T(8,128)(2,1)S(1)}) fusion(f32[256,1024]{1,0:T(8,128)S(1)} %fusion.52, bf16[256,3072]{1,0:T(8,128)(2,1)S(1)} %slice.71, bf16[1,3072,1024]{2,1,0:T(8,128)(2,1)S(1)} %bitcast.63), kind=kOutput, calls=%fused_computation.41 | convolution fusion | flops 1614282752 | bytes 11010048 | tf_op jit(solution)/shard_map/dot_general | solution.py:243
  34.1 0.1 select_reduce_fusion
  34.2 0.3 collective-permute-start.10
  34.5 1.9 %fusion.17 = bf16[256,3072]{1,0:T(8,128)(2,1)S(1)} fusion(bf16[256,1024]{1,0:T(8,128)(2,1)S(1)} %get-tuple-element.102, bf16[1,1024,3072]{2,1,0:T(8,128)(2,1)S(1)} %bitcast.74, f32[256]{0:T(256)S(1)} %select_reduce_fusion), kind=kOutput, calls=%fused_computation.14 | convolution fusion | flops 1612185600 | bytes 8389632 | tf_op jit(solution)/shard_map/dot_general | solution.py:243
  36.3 0.1 fusion.59
  36.5 0.4 collective-permute-start.7
  36.8 2.0 %fusion.14 = bf16[256,3072]{1,0:T(8,128)(2,1)S(1)} fusion(bf16[256,1024]{1,0:T(8,128)(2,1)S(1)} %get-tuple-element.101, bf16[1,1024,3072]{2,1,0:T(8,128)(2,1)S(1)} %bitcast.74, f32[256]{0:T(256)S(1)} %select_reduce_fusion.1), kind=kOutput, calls=%fused_computation.13 | convolution fusion | flops 1612185600 | bytes 8389632 | tf_op jit(solution)/shard_map/dot_general | solution.py:243
  38.9 0.1 fusion.58
  39.1 0.3 collective-permute-start.6
  39.3 0.2 add_convert_fusion.3
  39.5 2.2 %collective-permute-start.8 = (bf16[128,3072]{1,0:T(8,128)(2,1)S(1)}, bf16[128,3072]{1,0:T(8,128)(2,1)S(1)}, u32[]{:S(2)}, u32[]{:S(2)}) collective-permute-start(bf16[128,3072]{1,0:T(8,128)(2,1)S(1)} %add_convert_fusion.3), channel_id=1, source_target_pairs={{0,16},{1,9},{2,18},{3,11},{4,20},{5,13},{6,22},{7,15},{8,24},{9,1... | collective-permute-start | bytes 2359304 | tf_op jit(solution)/shard_map/ppermute | solution.py:33
  41.8 4.7 %multiply_convert_fusion.2 = (bf16[256,1024]{1,0:T(8,128)(2,1)S(1)}, bf16[256,1024]{1,0:T(8,128)(2,1)S(1)}) fusion(bf16[256,1024]{1,0:T(8,128)(2,1)S(1)} %get-tuple-element.87, bf16[256,1024]{1,0:T(8,128)(2,1)S(1)} %get-tuple-element.86, f32[256]{0:T(256)S(1)} %select_reduce_fusion, bf16[256,3072]{1,0:T(8,128)(2,1)S(1)} %constant_dynamic-update-slice_fusion, ...), kind=kOutput, calls=%fused_computation.39 | convolution fusion | flops 1612447744 | bytes 9962496 | tf_op jit(solution)/shard_map/dot_general | solution.py:243
  46.6 4.3 %shard_map.120 = (bf16[128,3200]{1,0:T(8,128)(2,1)S(1)}, bf16[128,3200]{1,0:T(8,128)(2,1)S(1)}) custom-call(bf16[256,1024]{1,0:T(8,128)(2,1)S(1)} %get-tuple-element.110.gate_grad, bf16[256,1024]{1,0:T(8,128)(2,1)S(1)} %get-tuple-element.117.up_grad, bf16[256,1024]{1,0:T(8,128)(2,1)S(1)} %get-tuple-element.90.pre_ref, bf16[3072,1024]{1,0:T(8,128)(2,1)S(1)} %bitcast.60, ...), custom_call_target="tpu_custom_call" | custom-call | tf_op jit(solution)/shard_map/pallas_call | solution.py:300
  50.9 0.2 collective-permute-start.12
  51.2 0.6 collective-permute-done.8
  51.8 0.4 add_convert_fusion.2
  52.2 2.1 %collective-permute-start.11 = (bf16[64,3072]{1,0:T(8,128)(2,1)S(1)}, bf16[64,3072]{1,0:T(8,128)(2,1)S(1)}, u32[]{:S(2)}, u32[]{:S(2)}) collective-permute-start(bf16[64,3072]{1,0:T(8,128)(2,1)S(1)} %slice.99), channel_id=1, source_target_pairs={{0,8},{1,17},{2,10},{3,19},{4,12},{5,21},{6,14},{7,23},{8,0},{9,25... | collective-permute-start | bytes 1179656 | tf_op jit(solution)/shard_map/ppermute | solution.py:33
  54.2 4.3 %shard_map.121 = (bf16[128,3200]{1,0:T(8,128)(2,1)S(1)}, bf16[128,3200]{1,0:T(8,128)(2,1)S(1)}) custom-call(bf16[256,1024]{1,0:T(8,128)(2,1)S(1)} %get-tuple-element.109.gate_grad, bf16[256,1024]{1,0:T(8,128)(2,1)S(1)} %get-tuple-element.116.up_grad, bf16[256,1024]{1,0:T(8,128)(2,1)S(1)} %get-tuple-element.96.pre_ref, bf16[3072,1024]{1,0:T(8,128)(2,1)S(1)} %bitcast.61, ...), custom_call_target="tpu_custom_call" | custom-call | tf_op jit(solution)/shard_map/pallas_call | solution.py:300
  58.6 0.2 add_convert_fusion.1
  58.8 1.6 %collective-permute-start.16 = (bf16[128,3200]{1,0:T(8,128)(2,1)S(1)}, bf16[128,3200]{1,0:T(8,128)(2,1)S(1)}, u32[]{:S(2)}, u32[]{:S(2)}) collective-permute-start(bf16[128,3200]{1,0:T(8,128)(2,1)S(1)} %add_convert_fusion.1), channel_id=1, source_target_pairs={{0,16},{1,9},{2,18},{3,11},{4,20},{5,13},{6,22},{7,15},{8,24},{9,1... | collective-permute-start | bytes 2457608 | tf_op jit(solution)/shard_map/ppermute | solution.py:33
  60.4 0.1 add_convert_fusion.5
  60.5 1.7 %collective-permute-start.13 = (bf16[32,3072]{1,0:T(8,128)(2,1)S(1)}, bf16[32,3072]{1,0:T(8,128)(2,1)S(1)}, u32[]{:S(2)}, u32[]{:S(2)}) collective-permute-start(bf16[32,3072]{1,0:T(8,128)(2,1)S(1)} %slice.101), channel_id=1, source_target_pairs={{0,2},{1,3},{2,0},{3,1},{4,6},{5,7},{6,4},{7,5},{8,10},{9,11},{10,... | collective-permute-start | bytes 589832 | tf_op jit(solution)/shard_map/ppermute | solution.py:33
  62.3 5.6 %convolution_convert_fusion.2 = bf16[1024,3072]{1,0:T(8,128)(2,1)} fusion(bf16[256,3072]{1,0:T(8,128)(2,1)S(1)} %constant_dynamic-update-slice_fusion, bf16[256,3072]{1,0:T(8,128)(2,1)S(1)} %pad_maximum_fusion.3, bf16[256,1024]{1,0:T(8,128)(2,1)S(1)} %get-tuple-element.102, bf16[256,1024]{1,0:T(8,128)(2,1)S(1)} %get-tuple-element.101, f32[512]{0:T(512)S(1)} %bitcast.72), kind=kOutput, calls=%fused_computation.10 | convolution fusion | flops 3233808384 | bytes 10487808 | tf_op jit(solution)/shard_map/dot_general | solution.py:243
  67.9 2.7 %collective-permute-start.14 = (bf16[32,3072]{1,0:T(8,128)(2,1)S(1)}, bf16[32,3072]{1,0:T(8,128)(2,1)S(1)}, u32[]{:S(2)}, u32[]{:S(2)}) collective-permute-start(bf16[32,3072]{1,0:T(8,128)(2,1)S(1)} %add_convert_fusion.9), channel_id=1, source_target_pairs={{0,4},{1,5},{2,6},{3,7},{4,0},{5,1},{6,2},{7,3},{8,12},{9,13},{10,... | collective-permute-start | bytes 589832 | tf_op jit(solution)/shard_map/ppermute | solution.py:33
  70.5 0.7 collective-permute-done.16
  71.2 0.3 add_convert_fusion
  71.6 0.9 collective-permute-start.17
  72.5 0.4 pad_maximum_fusion
  72.9 5.5 %convolution_convert_fusion.1 = bf16[3072,1024]{1,0:T(8,128)(2,1)} fusion(bf16[512,3072]{1,0:T(8,128)(2,1)S(1)} %pad_maximum_fusion, bf16[256,1024]{1,0:T(8,128)(2,1)S(1)} %get-tuple-element.110.gate_grad, bf16[256,1024]{1,0:T(8,128)(2,1)S(1)} %get-tuple-element.109.gate_grad), kind=kOutput, calls=%fused_computation.9 | convolution fusion | flops 3226468352 | bytes 10485760 | tf_op jit(solution)/shard_map/dot_general | solution.py:243
  78.4 1.2 %collective-permute-done.17 = bf16[64,3200]{1,0:T(8,128)(2,1)S(1)} collective-permute-done((bf16[64,3200]{1,0:T(8,128)(2,1)S(1)}, bf16[64,3200]{1,0:T(8,128)(2,1)S(1)}, u32[]{:S(2)}, u32[]{:S(2)}) %collective-permute-start.17) | collective-permute-done | bytes 409632 | tf_op jit(solution)/shard_map/ppermute | solution.py:33
  79.6 0.1 add_convert_fusion.4
  79.7 1.6 %collective-permute-start.18 = (bf16[32,3200]{1,0:T(8,128)(2,1)S(1)}, bf16[32,3200]{1,0:T(8,128)(2,1)S(1)}, u32[]{:S(2)}, u32[]{:S(2)}) collective-permute-start(bf16[32,3200]{1,0:T(8,128)(2,1)S(1)} %slice.105), channel_id=1, source_target_pairs={{0,2},{1,3},{2,0},{3,1},{4,6},{5,7},{6,4},{7,5},{8,10},{9,11},{10,... | collective-permute-start | bytes 614408 | tf_op jit(solution)/shard_map/ppermute | solution.py:33
  81.4 4.2 %collective-permute-done.18 = bf16[32,3200]{1,0:T(8,128)(2,1)S(1)} collective-permute-done((bf16[32,3200]{1,0:T(8,128)(2,1)S(1)}, bf16[32,3200]{1,0:T(8,128)(2,1)S(1)}, u32[]{:S(2)}, u32[]{:S(2)}) %collective-permute-start.18) | collective-permute-done | bytes 204832 | tf_op jit(solution)/shard_map/ppermute | solution.py:33
  85.6 2.7 %collective-permute-start.20 = (bf16[32,3200]{1,0:T(8,128)(2,1)S(1)}, bf16[32,3200]{1,0:T(8,128)(2,1)S(1)}, u32[]{:S(2)}, u32[]{:S(2)}) collective-permute-start(bf16[32,3200]{1,0:T(8,128)(2,1)S(1)} %add_convert_fusion.7), channel_id=1, source_target_pairs={{0,4},{1,5},{2,6},{3,7},{4,0},{5,1},{6,2},{7,3},{8,12},{9,13},{10,... | collective-permute-start | bytes 614408 | tf_op jit(solution)/shard_map/ppermute | solution.py:33
  88.3 1.6 %collective-permute-start.19 = (bf16[32,3072]{1,0:T(8,128)(2,1)S(1)}, bf16[32,3072]{1,0:T(8,128)(2,1)S(1)}, u32[]{:S(2)}, u32[]{:S(2)}) collective-permute-start(bf16[32,3072]{1,0:T(8,128)(2,1)S(1)} %add_convert_fusion.8), channel_id=1, source_target_pairs={{0,2},{1,3},{2,0},{3,1},{4,6},{5,7},{6,4},{7,5},{8,10},{9,11},{10,... | collective-permute-start | bytes 589832 | tf_op jit(solution)/shard_map/ppermute | solution.py:33
  89.9 5.5 %convolution_convert_fusion = bf16[3072,1024]{1,0:T(8,128)(2,1)} fusion(bf16[512,3072]{1,0:T(8,128)(2,1)S(1)} %pad_maximum_fusion, bf16[256,1024]{1,0:T(8,128)(2,1)S(1)} %get-tuple-element.117.up_grad, bf16[256,1024]{1,0:T(8,128)(2,1)S(1)} %get-tuple-element.116.up_grad), kind=kOutput, calls=%fused_computation.8 | convolution fusion | flops 3226468352 | bytes 10485760 | tf_op jit(solution)/shard_map/dot_general | solution.py:243
  95.3 0.4 collective-permute-done.20
  95.9 1.4 %collective-permute-start.22 = (bf16[32,3200]{1,0:T(8,128)(2,1)S(1)}, bf16[32,3200]{1,0:T(8,128)(2,1)S(1)}, u32[]{:S(2)}, u32[]{:S(2)}) collective-permute-start(bf16[32,3200]{1,0:T(8,128)(2,1)S(1)} %add_convert_fusion.6), channel_id=1, source_target_pairs={{0,2},{1,3},{2,0},{3,1},{4,6},{5,7},{6,4},{7,5},{8,10},{9,11},{10,... | collective-permute-start | bytes 614408 | tf_op jit(solution)/shard_map/ppermute | solution.py:33
  97.5 4.2 %collective-permute-done.22 = bf16[32,3200]{1,0:T(8,128)(2,1)S(1)} collective-permute-done((bf16[32,3200]{1,0:T(8,128)(2,1)S(1)}, bf16[32,3200]{1,0:T(8,128)(2,1)S(1)}, u32[]{:S(2)}, u32[]{:S(2)}) %collective-permute-start.22) | collective-permute-done | bytes 204832 | tf_op jit(solution)/shard_map/ppermute | solution.py:33
  102.0 1.5 %collective-permute-done.23 = bf16[64,3200]{1,0:T(8,128)(2,1)S(1)} collective-permute-done((bf16[64,3200]{1,0:T(8,128)(2,1)S(1)}, bf16[64,3200]{1,0:T(8,128)(2,1)S(1)}, u32[]{:S(2)}, u32[]{:S(2)}) %collective-permute-start.23) | collective-permute-done | bytes 409632 | tf_op jit(solution)/shard_map/ppermute | solution.py:33
  103.6 0.2 fusion.43
  103.8 0.6 maximum_divide_fusion
  (68 shorter events, 1.4 us)
Async XLA Ops:
  3.0 9.1 %collective-permute-start = (bf16[64,3200]{1,0:T(8,128)(2,1)}, bf16[64,3200]{1,0:T(8,128)(2,1)S(1)}, u32[]{:S(2)}, u32[]{:S(2)}) collective-permute-start(bf16[64,3200]{1,0:T(8,128)(2,1)} %get-tuple-element.64), channel_id=1, source_target_pairs={{0,8},{1,17},{2,10},{3,19},{4,12},{5,21},{6,14},{7,23},{8,0},{9,25... | collective-permute-start | bytes 1228808 | tf_op jit(solution)/shard_map/ppermute | solution.py:33
  6.0 1.1 %copy-start.1 = (bf16[128,3072]{1,0:T(8,128)(2,1)S(1)}, bf16[128,3072]{1,0:T(8,128)(2,1)}, u32[]{:S(2)}) copy-start(bf16[128,3072]{1,0:T(8,128)(2,1)} %refs_0_.2) | copy-start | bytes 2359300
  7.1 1.2 %copy-start.7 = (s32[128,2]{0,1:T(2,128)S(1)}, s32[128,2]{0,1:T(2,128)}, u32[]{:S(2)}) copy-start(s32[128,2]{0,1:T(2,128)} %param.8) | copy-start | bytes 3076
  7.1 5.0 %copy-start.2 = (bf16[64,3200]{1,0:T(8,128)(2,1)S(1)}, bf16[64,3200]{1,0:T(8,128)(2,1)}, u32[]{:S(2)}) copy-start(bf16[64,3200]{1,0:T(8,128)(2,1)} %get-tuple-element.64) | copy-start | bytes 1228804
  7.1 7.2 %copy-start.5 = (bf16[64,3200]{1,0:T(8,128)(2,1)S(1)}, bf16[64,3200]{1,0:T(8,128)(2,1)}, u32[]{:S(2)}) copy-start(bf16[64,3200]{1,0:T(8,128)(2,1)} %get-tuple-element.65) | copy-start | bytes 1228804
  8.2 10.7 %collective-permute-start.2 = (bf16[64,3072]{1,0:T(8,128)(2,1)S(1)}, bf16[64,3072]{1,0:T(8,128)(2,1)S(1)}, u32[]{:S(2)}, u32[]{:S(2)}) collective-permute-start(bf16[64,3072]{1,0:T(8,128)(2,1)S(1)} %get-tuple-element.67), channel_id=1, source_target_pairs={{0,8},{1,17},{2,10},{3,19},{4,12},{5,21},{6,14},{7,23},{8,0},{9,25... | collective-permute-start | bytes 1179656 | tf_op jit(solution)/shard_map/ppermute | solution.py:33
  12.1 2.2 %collective-permute-start.1 = (bf16[64,3200]{1,0:T(8,128)(2,1)S(1)}, bf16[64,3200]{1,0:T(8,128)(2,1)S(1)}, u32[]{:S(2)}, u32[]{:S(2)}) collective-permute-start(bf16[64,3200]{1,0:T(8,128)(2,1)S(1)} %collective-permute-done), channel_id=1, source_target_pairs={{0,1},{1,0},{2,3},{3,2},{4,5},{5,4},{6,7},{7,6},{8,9},{9,8},{10,11... | collective-permute-start | bytes 1228808 | tf_op jit(solution)/shard_map/ppermute | solution.py:33
  12.2 12.4 %collective-permute-start.3 = (bf16[128,3200]{1,0:T(8,128)(2,1)S(1)}, bf16[128,3200]{1,0:T(8,128)(2,1)S(1)}, u32[]{:S(2)}, u32[]{:S(2)}) collective-permute-start(bf16[128,3200]{1,0:T(8,128)(2,1)S(1)} %pad_maximum_fusion.4), channel_id=1, source_target_pairs={{0,16},{1,9},{2,18},{3,11},{4,20},{5,13},{6,22},{7,15},{8,24},{9,1... | collective-permute-start | bytes 2457608 | tf_op jit(solution)/shard_map/ppermute | solution.py:33
  14.3 2.8 %copy-start = (bf16[1,3072,1024]{2,1,0:T(8,128)(2,1)S(1)}, bf16[1,3072,1024]{2,1,0:T(8,128)(2,1)}, u32[]{:S(2)}) copy-start(bf16[1,3072,1024]{2,1,0:T(8,128)(2,1)} %param.11) | copy-start | bytes 18874372
  14.4 4.5 %slice-start = ((s8[6291456]{0:T(1024)(128)(4,1)}), s8[4194304]{0:T(1024)(128)(4,1)S(1)}, s32[]{:S(2)}) async-start(s8[6291456]{0:T(1024)(128)(4,1)} %bitcast.62), calls=%async_computation | async-start | bytes 8388608
  17.1 2.0 %slice-start.1 = ((s8[6291456]{0:T(1024)(128)(4,1)}), s8[2097152]{0:T(1024)(128)(4,1)S(1)}, s32[]{:S(2)}) async-start(s8[6291456]{0:T(1024)(128)(4,1)} %bitcast.62), calls=%async_computation.1 | async-start | bytes 4194304
  21.2 2.0 %collective-permute-start.5 = (bf16[64,3072]{1,0:T(8,128)(2,1)S(1)}, bf16[64,3072]{1,0:T(8,128)(2,1)S(1)}, u32[]{:S(2)}, u32[]{:S(2)}) collective-permute-start(bf16[64,3072]{1,0:T(8,128)(2,1)S(1)} %collective-permute-done.2), channel_id=1, source_target_pairs={{0,1},{1,0},{2,3},{3,2},{4,5},{5,4},{6,7},{7,6},{8,9},{9,8},{10,11... | collective-permute-start | bytes 1179656 | tf_op jit(solution)/shard_map/ppermute | solution.py:33
  21.6 12.6 %collective-permute-start.9 = (bf16[128,3072]{1,0:T(8,128)(2,1)S(1)}, bf16[128,3072]{1,0:T(8,128)(2,1)S(1)}, u32[]{:S(2)}, u32[]{:S(2)}) collective-permute-start(bf16[128,3072]{1,0:T(8,128)(2,1)S(1)} %pad_maximum_fusion.5), channel_id=1, source_target_pairs={{0,16},{1,9},{2,18},{3,11},{4,20},{5,13},{6,22},{7,15},{8,24},{9,1... | collective-permute-start | bytes 2359304 | tf_op jit(solution)/shard_map/ppermute | solution.py:33
  24.6 5.2 %collective-permute-start.4 = (bf16[128,3200]{1,0:T(8,128)(2,1)S(1)}, bf16[128,3200]{1,0:T(8,128)(2,1)S(1)}, u32[]{:S(2)}, u32[]{:S(2)}) collective-permute-start(bf16[128,3200]{1,0:T(8,128)(2,1)S(1)} %collective-permute-done.3), channel_id=1, source_target_pairs={{0,1},{1,0},{2,3},{3,2},{4,5},{5,4},{6,7},{7,6},{8,9},{9,8},{10,11... | collective-permute-start | bytes 2457608 | tf_op jit(solution)/shard_map/ppermute | solution.py:33
  30.1 4.4 %slice-start.2 = ((s8[6291456]{0:T(1024)(128)(4,1)}), s8[4194304]{0:T(1024)(128)(4,1)S(1)}, s32[]{:S(2)}) async-start(s8[6291456]{0:T(1024)(128)(4,1)} %bitcast.73), calls=%async_computation.2 | async-start | bytes 8388608
  31.9 2.5 %slice-start.3 = ((s8[6291456]{0:T(1024)(128)(4,1)}), s8[2097152]{0:T(1024)(128)(4,1)S(1)}, s32[]{:S(2)}) async-start(s8[6291456]{0:T(1024)(128)(4,1)} %bitcast.73), calls=%async_computation.3 | async-start | bytes 4194304
  34.2 7.6 %collective-permute-start.10 = (bf16[128,3072]{1,0:T(8,128)(2,1)S(1)}, bf16[128,3072]{1,0:T(8,128)(2,1)S(1)}, u32[]{:S(2)}, u32[]{:S(2)}) collective-permute-start(bf16[128,3072]{1,0:T(8,128)(2,1)S(1)} %collective-permute-done.9), channel_id=1, source_target_pairs={{0,1},{1,0},{2,3},{3,2},{4,5},{5,4},{6,7},{7,6},{8,9},{9,8},{10,11... | collective-permute-start | bytes 2359304 | tf_op jit(solution)/shard_map/ppermute | solution.py:33
  36.5 2.9 %collective-permute-start.7 = (bf16[128,3072]{1,0:T(8,128)(2,1)S(1)}, bf16[128,3072]{1,0:T(8,128)(2,1)S(1)}, u32[]{:S(2)}, u32[]{:S(2)}) collective-permute-start(bf16[128,3072]{1,0:T(8,128)(2,1)S(1)} %get-tuple-element.79), channel_id=1, source_target_pairs={{0,1},{1,0},{2,3},{3,2},{4,5},{5,4},{6,7},{7,6},{8,9},{9,8},{10,11... | collective-permute-start | bytes 2359304 | tf_op jit(solution)/shard_map/ppermute | solution.py:33
  39.1 12.7 %collective-permute-start.6 = (bf16[128,3072]{1,0:T(8,128)(2,1)S(1)}, bf16[128,3072]{1,0:T(8,128)(2,1)S(1)}, u32[]{:S(2)}, u32[]{:S(2)}) collective-permute-start(bf16[128,3072]{1,0:T(8,128)(2,1)S(1)} %get-tuple-element.82), channel_id=1, source_target_pairs={{0,1},{1,0},{2,3},{3,2},{4,5},{5,4},{6,7},{7,6},{8,9},{9,8},{10,11... | collective-permute-start | bytes 2359304 | tf_op jit(solution)/shard_map/ppermute | solution.py:33
  39.5 12.2 %collective-permute-start.8 = (bf16[128,3072]{1,0:T(8,128)(2,1)S(1)}, bf16[128,3072]{1,0:T(8,128)(2,1)S(1)}, u32[]{:S(2)}, u32[]{:S(2)}) collective-permute-start(bf16[128,3072]{1,0:T(8,128)(2,1)S(1)} %add_convert_fusion.3), channel_id=1, source_target_pairs={{0,16},{1,9},{2,18},{3,11},{4,20},{5,13},{6,22},{7,15},{8,24},{9,1... | collective-permute-start | bytes 2359304 | tf_op jit(solution)/shard_map/ppermute | solution.py:33
  50.9 7.7 %collective-permute-start.12 = (bf16[128,3200]{1,0:T(8,128)(2,1)S(1)}, bf16[128,3200]{1,0:T(8,128)(2,1)S(1)}, u32[]{:S(2)}, u32[]{:S(2)}) collective-permute-start(bf16[128,3200]{1,0:T(8,128)(2,1)S(1)} %get-tuple-element.92), channel_id=1, source_target_pairs={{0,1},{1,0},{2,3},{3,2},{4,5},{5,4},{6,7},{7,6},{8,9},{9,8},{10,11... | collective-permute-start | bytes 2457608 | tf_op jit(solution)/shard_map/ppermute | solution.py:33
  52.2 8.3 %collective-permute-start.11 = (bf16[64,3072]{1,0:T(8,128)(2,1)S(1)}, bf16[64,3072]{1,0:T(8,128)(2,1)S(1)}, u32[]{:S(2)}, u32[]{:S(2)}) collective-permute-start(bf16[64,3072]{1,0:T(8,128)(2,1)S(1)} %slice.99), channel_id=1, source_target_pairs={{0,8},{1,17},{2,10},{3,19},{4,12},{5,21},{6,14},{7,23},{8,0},{9,25... | collective-permute-start | bytes 1179656 | tf_op jit(solution)/shard_map/ppermute | solution.py:33
  58.5 12.7 %collective-permute-start.15 = (bf16[128,3200]{1,0:T(8,128)(2,1)S(1)}, bf16[128,3200]{1,0:T(8,128)(2,1)S(1)}, u32[]{:S(2)}, u32[]{:S(2)}) collective-permute-start(bf16[128,3200]{1,0:T(8,128)(2,1)S(1)} %get-tuple-element.98), channel_id=1, source_target_pairs={{0,1},{1,0},{2,3},{3,2},{4,5},{5,4},{6,7},{7,6},{8,9},{9,8},{10,11... | collective-permute-start | bytes 2457608 | tf_op jit(solution)/shard_map/ppermute | solution.py:33
  58.8 12.4 %collective-permute-start.16 = (bf16[128,3200]{1,0:T(8,128)(2,1)S(1)}, bf16[128,3200]{1,0:T(8,128)(2,1)S(1)}, u32[]{:S(2)}, u32[]{:S(2)}) collective-permute-start(bf16[128,3200]{1,0:T(8,128)(2,1)S(1)} %add_convert_fusion.1), channel_id=1, source_target_pairs={{0,16},{1,9},{2,18},{3,11},{4,20},{5,13},{6,22},{7,15},{8,24},{9,1... | collective-permute-start | bytes 2457608 | tf_op jit(solution)/shard_map/ppermute | solution.py:33
  60.5 7.3 %collective-permute-start.13 = (bf16[32,3072]{1,0:T(8,128)(2,1)S(1)}, bf16[32,3072]{1,0:T(8,128)(2,1)S(1)}, u32[]{:S(2)}, u32[]{:S(2)}) collective-permute-start(bf16[32,3072]{1,0:T(8,128)(2,1)S(1)} %slice.101), channel_id=1, source_target_pairs={{0,2},{1,3},{2,0},{3,1},{4,6},{5,7},{6,4},{7,5},{8,10},{9,11},{10,... | collective-permute-start | bytes 589832 | tf_op jit(solution)/shard_map/ppermute | solution.py:33
  67.9 13.5 %collective-permute-start.14 = (bf16[32,3072]{1,0:T(8,128)(2,1)S(1)}, bf16[32,3072]{1,0:T(8,128)(2,1)S(1)}, u32[]{:S(2)}, u32[]{:S(2)}) collective-permute-start(bf16[32,3072]{1,0:T(8,128)(2,1)S(1)} %add_convert_fusion.9), channel_id=1, source_target_pairs={{0,4},{1,5},{2,6},{3,7},{4,0},{5,1},{6,2},{7,3},{8,12},{9,13},{10,... | collective-permute-start | bytes 589832 | tf_op jit(solution)/shard_map/ppermute | solution.py:33
  71.6 8.0 %collective-permute-start.17 = (bf16[64,3200]{1,0:T(8,128)(2,1)S(1)}, bf16[64,3200]{1,0:T(8,128)(2,1)S(1)}, u32[]{:S(2)}, u32[]{:S(2)}) collective-permute-start(bf16[64,3200]{1,0:T(8,128)(2,1)S(1)} %slice.103), channel_id=1, source_target_pairs={{0,8},{1,17},{2,10},{3,19},{4,12},{5,21},{6,14},{7,23},{8,0},{9,25... | collective-permute-start | bytes 1228808 | tf_op jit(solution)/shard_map/ppermute | solution.py:33
  79.7 5.9 %collective-permute-start.18 = (bf16[32,3200]{1,0:T(8,128)(2,1)S(1)}, bf16[32,3200]{1,0:T(8,128)(2,1)S(1)}, u32[]{:S(2)}, u32[]{:S(2)}) collective-permute-start(bf16[32,3200]{1,0:T(8,128)(2,1)S(1)} %slice.105), channel_id=1, source_target_pairs={{0,2},{1,3},{2,0},{3,1},{4,6},{5,7},{6,4},{7,5},{8,10},{9,11},{10,... | collective-permute-start | bytes 614408 | tf_op jit(solution)/shard_map/ppermute | solution.py:33
  85.6 10.1 %collective-permute-start.20 = (bf16[32,3200]{1,0:T(8,128)(2,1)S(1)}, bf16[32,3200]{1,0:T(8,128)(2,1)S(1)}, u32[]{:S(2)}, u32[]{:S(2)}) collective-permute-start(bf16[32,3200]{1,0:T(8,128)(2,1)S(1)} %add_convert_fusion.7), channel_id=1, source_target_pairs={{0,4},{1,5},{2,6},{3,7},{4,0},{5,1},{6,2},{7,3},{8,12},{9,13},{10,... | collective-permute-start | bytes 614408 | tf_op jit(solution)/shard_map/ppermute | solution.py:33
  88.3 7.6 %collective-permute-start.19 = (bf16[32,3072]{1,0:T(8,128)(2,1)S(1)}, bf16[32,3072]{1,0:T(8,128)(2,1)S(1)}, u32[]{:S(2)}, u32[]{:S(2)}) collective-permute-start(bf16[32,3072]{1,0:T(8,128)(2,1)S(1)} %add_convert_fusion.8), channel_id=1, source_target_pairs={{0,2},{1,3},{2,0},{3,1},{4,6},{5,7},{6,4},{7,5},{8,10},{9,11},{10,... | collective-permute-start | bytes 589832 | tf_op jit(solution)/shard_map/ppermute | solution.py:33
  95.9 5.8 %collective-permute-start.22 = (bf16[32,3200]{1,0:T(8,128)(2,1)S(1)}, bf16[32,3200]{1,0:T(8,128)(2,1)S(1)}, u32[]{:S(2)}, u32[]{:S(2)}) collective-permute-start(bf16[32,3200]{1,0:T(8,128)(2,1)S(1)} %add_convert_fusion.6), channel_id=1, source_target_pairs={{0,2},{1,3},{2,0},{3,1},{4,6},{5,7},{6,4},{7,5},{8,10},{9,11},{10,... | collective-permute-start | bytes 614408 | tf_op jit(solution)/shard_map/ppermute | solution.py:33
  97.3 4.6 %collective-permute-start.21 = (bf16[64,3072]{1,0:T(8,128)(2,1)S(1)}, bf16[64,3072]{1,0:T(8,128)(2,1)S(1)}, u32[]{:S(2)}, u32[]{:S(2)}) collective-permute-start(bf16[64,3072]{1,0:T(8,128)(2,1)S(1)} %maximum_select_fusion.1), channel_id=1, source_target_pairs={{0,1},{1,0},{2,3},{3,2},{4,5},{5,4},{6,7},{7,6},{8,9},{9,8},{10,11... | collective-permute-start | bytes 1179656 | tf_op jit(solution)/shard_map/ppermute | solution.py:33
  97.4 6.3 %copy-start.6 = (f32[128,2]{0,1:T(2,128)S(1)}, f32[128,2]{0,1:T(2,128)}, u32[]{:S(2)}) copy-start(f32[128,2]{0,1:T(2,128)} %param.9) | copy-start | bytes 3076
  101.7 1.8 %collective-permute-start.23 = (bf16[64,3200]{1,0:T(8,128)(2,1)S(1)}, bf16[64,3200]{1,0:T(8,128)(2,1)S(1)}, u32[]{:S(2)}, u32[]{:S(2)}) collective-permute-start(bf16[64,3200]{1,0:T(8,128)(2,1)S(1)} %maximum_select_fusion), channel_id=1, source_target_pairs={{0,1},{1,0},{2,3},{3,2},{4,5},{5,4},{6,7},{7,6},{8,9},{9,8},{10,11... | collective-permute-start | bytes 1228808 | tf_op jit(solution)/shard_map/ppermute | solution.py:33
  102.0 2.4 %copy-start.3 = (bf16[128,3072]{1,0:T(8,128)(2,1)}, bf16[128,3072]{1,0:T(8,128)(2,1)S(1)}, u32[]{:S(2)}) copy-start(bf16[128,3072]{1,0:T(8,128)(2,1)S(1)} %constant_dynamic-update-slice_fusion.2) | copy-start | bytes 2359300
  103.6 0.9 copy-start.4
